TPU v7x, 128 devices: a whole 4x4x4 slice. The times are simulated.
128 devices in a mesh: dp: 4 (over x), fsdp: 16 (over z, y_hi, core), seq: 2 (over y_lo).
Axes of the slice: x: 4, y: 4 (y_hi: 2, y_lo: 2; y = y_hi * 2 + y_lo), z: 4, core: 2. Of those that a mesh axis runs over, the one named last changes fastest.
Arguments:
- tokens: bfloat16 [32768, 1152], P(('dp', 'fsdp', 'seq')), may hold values from -6 to 6
- w_query: bfloat16 [1152, 1024], P('fsdp'), may hold values from -0.1875 to 0.1875
- w_key: bfloat16 [1152, 256], P('fsdp'), may hold values from -0.1875 to 0.1875
- w_value: bfloat16 [1152, 256], P('fsdp'), may hold values from -0.1875 to 0.1875
- w_out: bfloat16 [1024, 1152], P('fsdp'), may hold values from -0.1875 to 0.1875
- w_gate: bfloat16 [1152, 6912], P('fsdp'), may hold values from -0.1875 to 0.1875
- w_up: bfloat16 [1152, 6912], P('fsdp'), may hold values from -0.1875 to 0.1875
- w_down: bfloat16 [6912, 1152], P('fsdp'), may hold values from -0.078125 to 0.078125
- pre_attn_gain: bfloat16 [1152], P('fsdp'), may hold values from -0.29882812 to 0.29882812
- post_attn_gain: bfloat16 [1152], P('fsdp'), may hold values from -0.29882812 to 0.29882812
- pre_mlp_gain: bfloat16 [1152], P('fsdp'), may hold values from -0.29882812 to 0.29882812
- post_mlp_gain: bfloat16 [1152], P('fsdp'), may hold values from -0.29882812 to 0.29882812
- query_gain: bfloat16 [256], P('fsdp'), may hold values from 0 to 0.59765625
- key_gain: bfloat16 [256], P('fsdp'), may hold values from 0 to 0.59765625
- cotangent: bfloat16 [32768, 1152], P(('dp', 'fsdp', 'seq')), may hold values from -6 to 6
Outputs:
- layer_out: bfloat16 [32768, 1152], P(('dp', 'fsdp', 'seq'))
- grad_tokens: bfloat16 [32768, 1152], P(('dp', 'fsdp', 'seq'))
- grad_w_query: float32 [1152, 1024], P('fsdp')
- grad_w_key: float32 [1152, 256], P('fsdp')
- grad_w_value: float32 [1152, 256], P('fsdp')
- grad_w_out: float32 [1024, 1152], P('fsdp')
- grad_w_gate: float32 [1152, 6912], P('fsdp')
- grad_w_up: float32 [1152, 6912], P('fsdp')
- grad_w_down: float32 [6912, 1152], P('fsdp')
- grad_pre_attn_gain: float32 [1152], P('fsdp')
- grad_post_attn_gain: float32 [1152], P('fsdp')
- grad_pre_mlp_gain: float32 [1152], P('fsdp')
- grad_post_mlp_gain: float32 [1152], P('fsdp')
- grad_query_gain: float32 [256], P('fsdp')
- grad_key_gain: float32 [256], P('fsdp')
All inputs are finite; a program needn't handle non-finite values.
Results may differ from a plain program's by a relative error of at most 0.025.
Values may be sent and summed in bfloat16 or wider, within the bound.
A program may use at most 256 MiB of HBM per device.

v0:
```python
import math

import jax
import jax.numpy as jnp
from jax import lax
from jax.sharding import PartitionSpec as P


def rms_norm(values, scale_gain):
    factor = lax.rsqrt(jnp.mean(values * values, axis=-1, keepdims=True) + 1e-06)
    return values * factor * (1.0 + scale_gain)


def rotate(values, positions):
    half_dim = values.shape[-1] // 2
    frequency = jnp.exp(
        jnp.arange(half_dim, dtype=jnp.float32) * (-2.0 * math.log(1000000.0) / values.shape[-1])
    )
    angles = positions[:, None] * frequency[None, :]
    cosine = jnp.cos(angles)[:, None, :]
    sine_part = jnp.sin(angles)[:, None, :]
    first_half = values[..., :half_dim]
    second_half = values[..., half_dim:]
    return jnp.concatenate(
        [
            first_half * cosine - second_half * sine_part,
            second_half * cosine + first_half * sine_part,
        ],
        axis=-1,
    )


def contract_rows(left_side, right_side):
    return lax.dot_general(
        left_side, right_side, (((0,), (0,)), ((), ())), preferred_element_type=jnp.float32
    )


def contract_cols(left_side, right_side):
    return lax.dot_general(
        left_side, right_side, (((1,), (1,)), ((), ())), preferred_element_type=jnp.float32
    )


def body(
    tokens,
    w_query,
    w_key,
    w_value,
    w_out,
    w_gate,
    w_up,
    w_down,
    pre_attn_gain,
    post_attn_gain,
    pre_mlp_gain,
    post_mlp_gain,
    query_gain,
    key_gain,
    cotangent,
):
    local_rows = tokens.shape[0]
    model_width = tokens.shape[1]
    head_dim = w_key.shape[1]
    head_count = w_query.shape[1] // head_dim
    hidden_units = w_gate.shape[1]
    out_width = head_count * head_dim
    shard_count = lax.axis_size("fsdp")
    gathered = (
        lax.all_gather(w_query, "fsdp", axis=0, tiled=True),
        lax.all_gather(w_key, "fsdp", axis=0, tiled=True),
        lax.all_gather(w_value, "fsdp", axis=0, tiled=True),
        lax.all_gather(w_out, "fsdp", axis=0, tiled=True),
        lax.all_gather(pre_attn_gain, "fsdp", axis=0, tiled=True),
        lax.all_gather(post_attn_gain, "fsdp", axis=0, tiled=True),
        lax.all_gather(pre_mlp_gain, "fsdp", axis=0, tiled=True),
        lax.all_gather(post_mlp_gain, "fsdp", axis=0, tiled=True),
        lax.all_gather(query_gain, "fsdp", axis=0, tiled=True),
        lax.all_gather(key_gain, "fsdp", axis=0, tiled=True),
    )
    full_query, full_key, full_value, full_out = (
        gathered[0],
        gathered[1],
        gathered[2],
        gathered[3],
    )
    gain_set = tuple((member.astype(jnp.float32) for member in gathered[4:]))
    attn_gain_in, attn_gain_out, mlp_gain_in, mlp_gain_out, query_scale, key_scale = gain_set
    seq_start = lax.axis_index("seq") * local_rows
    query_places = seq_start + jnp.arange(local_rows, dtype=jnp.int32)
    positions = query_places.astype(jnp.float32)
    inputs = tokens.astype(jnp.float32)
    normed_f, attn_in_pull = jax.vjp(rms_norm, inputs, attn_gain_in)
    normed = normed_f.astype(jnp.bfloat16)
    query_pre = jnp.dot(normed, full_query, preferred_element_type=jnp.float32).reshape(
        local_rows, head_count, head_dim
    )
    key_pre = jnp.dot(normed, full_key, preferred_element_type=jnp.float32).reshape(
        local_rows, 1, head_dim
    )
    value_local = jnp.dot(normed, full_value, preferred_element_type=jnp.float32).astype(
        jnp.bfloat16
    )

    def shape_heads(query_in, key_in, query_gain_f, key_gain_f):
        query_out = rotate(rms_norm(query_in, query_gain_f), positions) * head_dim ** (-0.5)
        key_out = rotate(rms_norm(key_in, key_gain_f), positions)
        return (query_out, key_out)

    (query_f, key_f), heads_pull = jax.vjp(shape_heads, query_pre, key_pre, query_scale, key_scale)
    queries = query_f.astype(jnp.bfloat16)
    key_local = key_f[:, 0, :].astype(jnp.bfloat16)
    key_rows, value_rows = (
        lax.all_gather(key_local, "seq", axis=0, tiled=True),
        lax.all_gather(value_local, "seq", axis=0, tiled=True),
    )
    seq_length = key_rows.shape[0]
    allowed = jnp.arange(seq_length, dtype=jnp.int32)[None, :] <= query_places[:, None]

    def masked_scores():
        raw_scores = jnp.einsum(
            "ihd,jd->hij", queries, key_rows, preferred_element_type=jnp.float32
        )
        return jnp.where(allowed[None, :, :], raw_scores, -1e30)

    scores = masked_scores()
    row_peak = jnp.max(scores, axis=-1, keepdims=True)
    exp_terms = jnp.exp(scores - row_peak)
    row_total = jnp.sum(exp_terms, axis=-1, keepdims=True)
    log_total = row_peak + jnp.log(row_total)
    probs_bf = (exp_terms / row_total).astype(jnp.bfloat16)
    context = jnp.einsum("hij,jd->ihd", probs_bf, value_rows, preferred_element_type=jnp.float32)
    context = context.astype(jnp.bfloat16).reshape(local_rows, out_width)
    attended = jnp.dot(context, full_out, preferred_element_type=jnp.float32)
    post_attn, attn_out_pull = jax.vjp(rms_norm, attended, attn_gain_out)
    middle = inputs + post_attn
    mlp_in_f, mlp_in_pull = jax.vjp(rms_norm, middle, mlp_gain_in)
    mlp_in = mlp_in_f.astype(jnp.bfloat16)
    pieces = (
        lax.all_gather(w_gate, "fsdp", axis=0, tiled=True),
        lax.all_gather(w_up, "fsdp", axis=0, tiled=True),
    )
    columns = mlp_in
    gate_pre = jnp.dot(columns, pieces[0], preferred_element_type=jnp.float32)
    up_pre = jnp.dot(columns, pieces[1], preferred_element_type=jnp.float32)

    def gated(gate_in, up_in):
        return jax.nn.gelu(gate_in, approximate=True) * up_in

    hidden_f, gated_pull = jax.vjp(gated, gate_pre, up_pre)
    hidden = hidden_f.astype(jnp.bfloat16)
    columns = hidden
    mixed = jnp.dot(
        columns,
        lax.all_gather(w_down, "fsdp", axis=0, tiled=True),
        preferred_element_type=jnp.float32,
    )
    post_mlp, mlp_out_pull = jax.vjp(rms_norm, mixed, mlp_gain_out)
    layer_out = (middle + post_mlp).astype(jnp.bfloat16)
    cot_seed = cotangent.astype(jnp.float32)
    mixed_grad_f, grad_gain_d = mlp_out_pull(cot_seed)
    mixed_grad = mixed_grad_f.astype(jnp.bfloat16)
    hidden_grad = contract_cols(mixed_grad, lax.all_gather(w_down, "fsdp", axis=0, tiled=True))
    gate_grad_f, up_grad_f = gated_pull(hidden_grad)
    gate_grad = gate_grad_f.astype(jnp.bfloat16)
    up_grad = up_grad_f.astype(jnp.bfloat16)
    pieces = (
        lax.all_gather(w_gate, "fsdp", axis=0, tiled=True),
        lax.all_gather(w_up, "fsdp", axis=0, tiled=True),
    )
    update = contract_cols(gate_grad, pieces[0]) + contract_cols(up_grad, pieces[1])
    middle_part, grad_gain_c = mlp_in_pull(update)
    middle_grad = cot_seed + middle_part
    attended_grad_f, grad_gain_b = attn_out_pull(middle_grad)
    attended_grad = attended_grad_f.astype(jnp.bfloat16)
    context_grad = (
        contract_cols(attended_grad, full_out)
        .astype(jnp.bfloat16)
        .reshape(local_rows, head_count, head_dim)
    )
    scores_again = masked_scores()
    prob_rows = jnp.exp(scores_again - log_total)
    prob_grad = jnp.einsum(
        "ihd,jd->hij", context_grad, value_rows, preferred_element_type=jnp.float32
    )
    row_dot = jnp.sum(prob_rows * prob_grad, axis=-1, keepdims=True)
    score_grad = (prob_rows * (prob_grad - row_dot)).astype(jnp.bfloat16)
    query_grad = jnp.einsum(
        "hij,jd->ihd", score_grad, key_rows, preferred_element_type=jnp.float32
    ).astype(jnp.bfloat16)
    key_part = jnp.einsum("hij,ihd->jd", score_grad, queries, preferred_element_type=jnp.float32)
    value_part = jnp.einsum(
        "hij,ihd->jd",
        prob_rows.astype(jnp.bfloat16),
        context_grad,
        preferred_element_type=jnp.float32,
    )
    key_sum, value_sum = (
        lax.psum_scatter(
            key_part.astype(jnp.bfloat16), "seq", scatter_dimension=0, tiled=True
        ).astype(jnp.float32),
        lax.psum_scatter(
            value_part.astype(jnp.bfloat16), "seq", scatter_dimension=0, tiled=True
        ).astype(jnp.float32),
    )
    key_grad = key_sum.astype(jnp.bfloat16)
    value_grad = value_sum.astype(jnp.bfloat16)
    query_pre_grad, key_pre_grad, grad_query_scale, grad_key_scale = heads_pull(
        (query_grad.astype(jnp.float32), key_grad.astype(jnp.float32)[:, None, :])
    )
    query_pre_bf = query_pre_grad.astype(jnp.bfloat16).reshape(local_rows, out_width)
    key_pre_bf = key_pre_grad.reshape(local_rows, head_dim).astype(jnp.bfloat16)
    normed_grad = (
        contract_cols(query_pre_bf, full_query)
        + contract_cols(key_pre_bf, full_key)
        + contract_cols(value_grad, full_value)
    )
    input_part, grad_gain_a = attn_in_pull(normed_grad)
    grad_tokens = (middle_grad + input_part).astype(jnp.bfloat16)
    gain_totals = lax.psum(
        (grad_gain_a, grad_gain_b, grad_gain_c, grad_gain_d, grad_query_scale, grad_key_scale),
        ("dp", "fsdp", "seq"),
    )
    shard_index = lax.axis_index("fsdp")
    gain_shards = tuple(
        (
            lax.dynamic_slice_in_dim(
                member,
                shard_index * (member.shape[0] // shard_count),
                member.shape[0] // shard_count,
            )
            for member in gain_totals
        )
    )
    attn_side = jnp.concatenate([query_pre_bf, key_pre_bf, value_grad], axis=1)
    mlp_side = jnp.concatenate([gate_grad, up_grad], axis=1)
    ctx_width = out_width // shard_count
    unit_width = hidden_units // shard_count
    in_piece = lax.psum_scatter(
        jnp.concatenate(
            [contract_rows(normed, attn_side), contract_rows(mlp_in, mlp_side)], axis=1
        ).astype(jnp.bfloat16),
        "fsdp",
        scatter_dimension=0,
        tiled=True,
    )
    amount = (ctx_width + unit_width) * lax.axis_size("fsdp")
    per_block = ctx_width + unit_width
    block_num = amount // per_block
    top_part = contract_rows(context, attended_grad).reshape(block_num, ctx_width, model_width)
    bottom_part = contract_rows(hidden, mixed_grad).reshape(block_num, unit_width, model_width)
    out_piece = lax.psum_scatter(
        jnp.concatenate([top_part, bottom_part], axis=1)
        .reshape(block_num * per_block, model_width)
        .astype(jnp.bfloat16),
        "fsdp",
        scatter_dimension=0,
        tiled=True,
    )
    in_sum, out_sum = (
        lax.psum(in_piece, ("dp", "seq")).astype(jnp.float32),
        lax.psum(out_piece, ("dp", "seq")).astype(jnp.float32),
    )
    out_blocks = out_sum.reshape(-1, ctx_width + unit_width, model_width)
    grad_w_out = out_blocks[:, :ctx_width, :].reshape(-1, model_width)
    grad_w_down = out_blocks[:, ctx_width:, :].reshape(-1, model_width)
    grad_w_query = in_sum[:, :out_width]
    grad_w_key = in_sum[:, out_width : out_width + head_dim]
    grad_w_value = in_sum[:, out_width + head_dim : out_width + 2 * head_dim]
    grad_w_gate = in_sum[:, out_width + 2 * head_dim : out_width + 2 * head_dim + hidden_units]
    grad_w_up = in_sum[:, out_width + 2 * head_dim + hidden_units :]
    return (
        layer_out,
        grad_tokens,
        grad_w_query,
        grad_w_key,
        grad_w_value,
        grad_w_out,
        grad_w_gate,
        grad_w_up,
        grad_w_down,
        gain_shards[0],
        gain_shards[1],
        gain_shards[2],
        gain_shards[3],
        gain_shards[4],
        gain_shards[5],
    )


def solution(mesh):
    placed = (
        P(("dp", "fsdp", "seq"), None),
        P("fsdp", None),
        P("fsdp", None),
        P("fsdp", None),
        P("fsdp", None),
        P("fsdp", None),
        P("fsdp", None),
        P("fsdp", None),
        P("fsdp"),
        P("fsdp"),
        P("fsdp"),
        P("fsdp"),
        P("fsdp"),
        P("fsdp"),
        P(("dp", "fsdp", "seq"), None),
    )
    return jax.shard_map(
        body,
        mesh=mesh,
        in_specs=placed,
        out_specs=(
            P(("dp", "fsdp", "seq"), None),
            P(("dp", "fsdp", "seq"), None),
            P("fsdp", None),
            P("fsdp", None),
            P("fsdp", None),
            P("fsdp", None),
            P("fsdp", None),
            P("fsdp", None),
            P("fsdp", None),
            P("fsdp"),
            P("fsdp"),
            P("fsdp"),
            P("fsdp"),
            P("fsdp"),
            P("fsdp"),
        ),
        check_vma=False,
    )
```

profile of v0, /device:TPU:0, one launch (start us, length us, event | category | flops | bytes accessed | tf_op | source)
XLA Modules:
  0.0 1135.8 jit_solution(4555185524879732388)
XLA Ops:
  7.3 0.7 all-gather.7.cloned.1.call-update
  8.1 0.7 all-gather.9.cloned.1.call-update
  8.8 0.7 all-gather.11.cloned.1.call-update
  10.7 0.6 dynamic-slice
  14.1 71.3 %all-reduce.12 = (bf16[1152]{0:T(1024)(128)(2,1)S(1)}, bf16[256]{0:T(256)(128)(2,1)S(1)}, bf16[256]{0:T(256)(128)(2,1)S(1)}, bf16[1152]{0:T(1024)(128)(2,1)S(1)}...) all-reduce(bf16[1152]{0:T(1024)(128)(2,1)S(1)} %dynamic-update-slic, ...), channel_id=1, replica_groups=mesh['dp'=4,'fsdp'=16,'seq'=2] {'fsdp'}, use_global_device_ids=true, to_apply=%add.4 | all-reduce | flops 5120 | bytes 20480
  85.7 24.5 %all_gather.51 = bf16[1152,256]{1,0:T(8,128)(2,1)S(1)} all-gather(bf16[72,256]{1,0:T(8,128)(2,1)S(1)} %copy-done.37), channel_id=1, replica_groups=mesh['dp'=4,'fsdp'=16,'seq'=2] {'fsdp'}, dimensions={0}, use_global_device_ids=true | all-gather | bytes 626688 | tf_op jit(solution)/shard_map/all_gather | solution.py:71
  111.5 6.5 all-gather
  117.9 26.9 %all_gather.49 = bf16[1152,256]{1,0:T(8,128)(2,1)S(1)} all-gather(bf16[72,256]{1,0:T(8,128)(2,1)S(1)} %copy-done.38), channel_id=1, replica_groups=mesh['dp'=4,'fsdp'=16,'seq'=2] {'fsdp'}, dimensions={0}, use_global_device_ids=true | all-gather | bytes 626688 | tf_op jit(solution)/shard_map/all_gather | solution.py:72
  145.2 6.8 all_gather.50
  152.0 0.6 convert_add_fusion.3
  152.7 0.6 convert_add_fusion.2
  154.0 3.6 fusion.89
  157.6 1.7 reshape.344
  162.3 1.6 convolution_convert_fusion.6
  163.9 2.8 multiply_reduce_fusion.6
  167.4 0.7 copy-done
  168.2 1.0 multiply_convert_fusion.2
  169.2 53.3 %all-gather.11.cloned.1.call-done = bf16[1152,6912]{1,0:T(8,128)(2,1)} async-done(((bf16[72,6912]{1,0:T(8,128)(2,1)}), bf16[1152,6912]{1,0:T(8,128)(2,1)}) %all-gather.11.cloned.1.call-update) | async-done | bytes 15925264 | tf_op jit(solution)/shard_map/all_gather | solution.py:140
  222.4 13.4 %fusion.96 = f32[256,6912]{1,0:T(8,128)} fusion(bf16[256,1152]{1,0:T(8,128)(2,1)} %multiply_convert_fusion.2, bf16[1152,6912]{1,0:T(8,128)(2,1)} %all-gather.11.cloned.1.call-done), kind=kOutput, calls=%fused_computation.186 | convolution fusion | flops 4076863488 | bytes 23592960 | tf_op jit(solution)/shard_map/dot_general | solution.py:144
  235.8 91.9 %all-gather.13.cloned.1.call-done = bf16[1152,6912]{1,0:T(8,128)(2,1)} async-done(((bf16[72,6912]{1,0:T(8,128)(2,1)}), bf16[1152,6912]{1,0:T(8,128)(2,1)}) %all-gather.13.cloned.1.call-update) | async-done | bytes 15925264 | tf_op jit(solution)/shard_map/all_gather | solution.py:141
  327.7 12.9 %multiply_convert_fusion.1 = (bf16[256,6912]{1,0:T(8,128)(2,1)}, f32[256,6912]{1,0:T(8,128)}) fusion(f32[256,6912]{1,0:T(8,128)} %fusion.96, bf16[256,1152]{1,0:T(8,128)(2,1)} %multiply_convert_fusion.2, bf16[1152,6912]{1,0:T(8,128)(2,1)} %all-gather.13.cloned.1.call-done), kind=kOutput, calls=%fused_computation.18 | convolution fusion | flops 4094558208 | bytes 34209792 | tf_op jit(solution)/shard_map/dot_general | solution.py:145
  340.6 92.4 %all-gather.15.cloned.1.call-done = bf16[6912,1152]{1,0:T(8,128)(2,1)} async-done(((bf16[432,1152]{1,0:T(8,128)(2,1)}), bf16[6912,1152]{1,0:T(8,128)(2,1)}) %all-gather.15.cloned.1.call-update) | async-done | bytes 15925264 | tf_op jit(solution)/shard_map/all_gather | solution.py:155
  433.1 10.4 multiply_reduce_fusion.4
  443.6 1.1 fusion.28
  444.8 1.6 fusion.29
  446.4 17.5 %multiply_convert_fusion = (bf16[256,6912]{1,0:T(8,128)(2,1)}, bf16[256,6912]{1,0:T(8,128)(2,1)}) fusion(f32[256,6912]{1,0:T(8,128)} %fusion.96, f32[256,6912]{1,0:T(8,128)} %get-tuple-element.69, bf16[256,1152]{1,0:T(8,128)(2,1)} %get-tuple-element.54, bf16[6912,1152]{1,0:T(8,128)(2,1)} %all-gather.15.cloned.1.call-done), kind=kOutput, calls=%fused_computation.17 | convolution fusion | flops 4119330816 | bytes 37748736 | tf_op jit(solution)/shard_map/dot_general | solution.py:40
  463.9 12.4 %fusion.97 = f32[256,1152]{1,0:T(8,128)} fusion(bf16[256,6912]{1,0:T(8,128)(2,1)} %get-tuple-element.45, bf16[1152,6912]{1,0:T(8,128)(2,1)} %all-gather.11.cloned.1.call-done), kind=kOutput, calls=%fused_computation.187 | convolution fusion | flops 4076863488 | bytes 20643840 | tf_op jit(solution)/shard_map/dot_general | solution.py:40
  476.3 13.6 %multiply_reduce_fusion = (f32[1152]{0:T(1024)}, f32[256]{0:T(256)S(1)}, f32[256,1152]{1,0:T(8,128)}) fusion(f32[256,1152]{1,0:T(8,128)} %copy-done, f32[256]{0:T(256)S(1)} %fusion.79, f32[1152]{0:T(1024)S(1)} %copy-done.33, f32[256,1152]{1,0:T(8,128)} %fusion.97, bf16[256,6912]{1,0:T(8,128)(2,1)} %get-tuple-element.44, ...), kind=kOutput, calls=%fused_computation.74 | convolution fusion | flops 4078926592 | bytes 23014400 | tf_op jit(solution)/shard_map/dot_general | solution.py:40
  489.9 3.0 multiply_reduce_fusion.1
  493.3 1.8 copy-done.18
  495.1 0.9 convolution_convert_fusion.5
  496.0 1.3 fusion.24
  497.3 3.0 fusion.10
  500.3 10.9 convolution_convert_fusion.1
  511.5 2.2 fusion.12
  513.7 1.2 fusion.23
  514.9 2.1 convolution_convert_fusion.3
  517.0 15.7 %pad_maximum_fusion.1 = bf16[16,496,1152]{2,1,0:T(8,128)(2,1)} fusion(bf16[16,432,1152]{2,1,0:T(8,128)(2,1)} %bitcast.134, bf16[16,64,1152]{2,1,0:T(8,128)(2,1)S(1)} %convolution_convert_fusion.3), kind=kLoop, calls=%fused_computation.3 | loop fusion | flops 36569088 | bytes 36569088 | tf_op jit(solution)/shard_map/concatenate | solution.py:253
  532.8 0.8 copy-done.23
  535.8 16.8 %convolution_convert_fusion = bf16[1152,13824]{1,0:T(8,128)(2,1)} fusion(bf16[256,1152]{1,0:T(8,128)(2,1)S(1)} %copy-done.24, bf16[256,6912]{1,0:T(8,128)(2,1)} %get-tuple-element.44, bf16[256,6912]{1,0:T(8,128)(2,1)} %get-tuple-element.45), kind=kOutput, calls=%fused_computation | convolution fusion | flops 8183808000 | bytes 39518208 | tf_op jit(solution)/shard_map/dot_general | solution.py:34
  552.7 1.1 copy.84
  553.8 1.0 bitcast_convert_fusion
  555.7 3.1 convolution_convert_fusion.2
  558.8 27.8 %pad_maximum_fusion = bf16[1152,15360]{1,0:T(8,128)(2,1)} fusion(bf16[1152,13824]{1,0:T(8,128)(2,1)} %convolution_convert_fusion, bf16[1152,1536]{1,0:T(8,128)(2,1)} %convolution_convert_fusion.2), kind=kLoop, calls=%fused_computation.1 | loop fusion | flops 70778880 | bytes 70778880 | tf_op jit(solution)/shard_map/concatenate | solution.py:240
  586.6 116.9 %reduce-scatter.11.cloned.1.call-done = bf16[496,1152]{1,0:T(8,128)(2,1)} async-done(((bf16[7936,1152]{1,0:T(8,128)(2,1)}), bf16[496,1152]{1,0:T(8,128)(2,1)}) %reduce-scatter.11.cloned.1.call-update) | async-done | bytes 1142800 | tf_op jit(solution)/shard_map/reduce_scatter | solution.py:252
  703.6 258.0 %reduce-scatter.13.cloned.1.call-done = bf16[72,15360]{1,0:T(8,128)(2,1)} async-done(((bf16[1152,15360]{1,0:T(8,128)(2,1)}), bf16[72,15360]{1,0:T(8,128)(2,1)}) %reduce-scatter.13.cloned.1.call-update) | async-done | bytes 2211856
  961.6 2.6 fusion.98
  964.7 0.7 copy-done.15
  965.4 0.6 fusion.26
  966.1 74.9 %all-reduce.11 = (f32[1152]{0:T(1024)S(1)}, f32[1152]{0:T(1024)S(1)}, f32[1152]{0:T(1024)S(1)}, f32[1152]{0:T(1024)S(1)}, f32[256]{0:T(256)S(1)}, /*index=5*/f32[256]{0:T(256)S(1)}) all-reduce(f32[1152]{0:T(1024)S(1)} %get-tuple-element.23, f32[1152]{0:T(1024)S(1)} %copy-done.46, ...), channel_id=1, replica_groups=mesh['dp'=4,'fsdp'=16,'seq'=2] {'dp','fsdp','seq'}, use_global_device_ids=true, to_apply=%region_22.23 | all-reduce | flops 5120 | bytes 40960 | tf_op jit(solution)/shard_map/psum | solution.py:220
  1041.0 0.6 dynamic_slice.18
  1041.6 0.6 dynamic_slice.19
  1042.2 0.6 dynamic_slice.20
  1042.8 0.6 dynamic_slice.21
  1043.4 0.6 dynamic_slice.22
  1044.5 1.2 fusion.32
  1045.7 73.2 %all-reduce.16.cloned.1.call-done = (bf16[72,15360]{1,0:T(8,128)(2,1)}, bf16[1,496,1152]{2,1,0:T(8,128)(2,1)}) async-done(((bf16[72,15360]{1,0:T(8,128)(2,1)}, bf16[1,496,1152]{2,1,0:T(8,128)(2,1)}), (bf16[72,15360]{1,0:T(8,128)(2,1)}, bf16[1,496,1152]{2,1,0:T(8,128)(2,1)})) %all-reduce.16.cloned.1.call-update) | async-done | bytes 3354640 | tf_op jit(solution)/shard_map/psum | solution.py:261
  1118.9 1.4 fusion.95
  1120.4 1.6 slice.48
  1122.0 1.4 reshape.351
  1123.4 0.7 slice_bitcast_fusion.1
  1124.2 1.4 slice_bitcast_fusion
  1125.6 0.9 copy-done.11
  1126.5 2.2 fusion.94
  (218 shorter events, 13.9 us)
Async XLA Ops:
  7.2 3.5 copy-start.70
  7.2 5.4 copy-start.64
  7.2 5.7 copy-start.65
  7.2 5.9 copy-start.66
  7.2 6.2 copy-start.67
  7.2 6.4 copy-start.68
  7.2 6.6 copy-start.69
  7.3 78.2 %copy-start.6 = (bf16[256,1152]{1,0:T(8,128)(2,1)S(1)}, bf16[256,1152]{1,0:T(8,128)(2,1)}, u32[]{:S(2)}) copy-start(bf16[256,1152]{1,0:T(8,128)(2,1)} %param.15) | copy-start | bytes 1769476
  7.3 78.4 %copy-start.37 = (bf16[72,256]{1,0:T(8,128)(2,1)S(1)}, bf16[72,256]{1,0:T(8,128)(2,1)}, u32[]{:S(2)}) copy-start(bf16[72,256]{1,0:T(8,128)(2,1)} %param.17) | copy-start | bytes 110596
  7.3 146.7 %all-gather.7.cloned.1.call-start = ((), (), s32[]{:S(2)}) async-start(), calls=%async_computation.4 | async-start | bytes 2506752 | tf_op jit(solution)/shard_map/all_gather | solution.py:70
  8.0 155.8 %all-gather.9.cloned.1.call-start = ((), (), s32[]{:S(2)}) async-start(), calls=%async_computation.5 | async-start | bytes 2506752 | tf_op jit(solution)/shard_map/all_gather | solution.py:73
  8.8 213.6 %all-gather.11.cloned.1.call-start = ((), (), s32[]{:S(2)}) async-start(), calls=%async_computation.6 | async-start | bytes 16920576 | tf_op jit(solution)/shard_map/all_gather | solution.py:140
  9.5 318.3 %all-gather.13.cloned.1.call-start = ((), (), s32[]{:S(2)}) async-start(), calls=%async_computation.7 | async-start | bytes 16920576 | tf_op jit(solution)/shard_map/all_gather | solution.py:141
  10.1 423.0 %all-gather.15.cloned.1.call-start = ((), (), s32[]{:S(2)}) async-start(), calls=%async_computation.8 | async-start | bytes 16920576 | tf_op jit(solution)/shard_map/all_gather | solution.py:155
  10.7 542.0 %reduce-scatter.9.cloned.1.call-start = ((), (), s32[]{:S(2)}) async-start(), calls=%async_computation.10 | async-start | bytes 393216 | tf_op jit(solution)/shard_map/reduce_scatter | solution.py:202
  85.4 67.9 %copy-start.60 = (f32[128]{0:T(128)}, f32[128]{0:T(128)S(1)}, u32[]{:S(2)}) copy-start(f32[128]{0:T(128)S(1)} %multiply_exponential_fusion) | copy-start | bytes 1540
  85.4 67.9 %copy-start.53 = (f32[256]{0:T(256)}, f32[256]{0:T(256)S(1)}, u32[]{:S(2)}) copy-start(f32[256]{0:T(256)S(1)} %fusion.81) | copy-start | bytes 3076
  85.6 25.1 %copy-start.57 = (f32[256]{0:T(256)}, f32[256]{0:T(256)S(1)}, u32[]{:S(2)}) copy-start(f32[256]{0:T(256)S(1)} %fusion.33) | copy-start | bytes 3076
  85.6 32.3 %copy-start.38 = (bf16[72,256]{1,0:T(8,128)(2,1)S(1)}, bf16[72,256]{1,0:T(8,128)(2,1)}, u32[]{:S(2)}) copy-start(bf16[72,256]{1,0:T(8,128)(2,1)} %param.18) | copy-start | bytes 110596
  85.7 59.2 %copy-start.51 = (f32[256]{0:T(256)}, f32[256]{0:T(256)S(1)}, u32[]{:S(2)}) copy-start(f32[256]{0:T(256)S(1)} %convert_add_fusion.7) | copy-start | bytes 3076
  85.7 68.3 %copy-start.55 = (f32[256]{0:T(256)}, f32[256]{0:T(256)S(1)}, u32[]{:S(2)}) copy-start(f32[256]{0:T(256)S(1)} %fusion.76) | copy-start | bytes 3076
  110.2 35.0 %copy-start.20 = (bf16[1152,256]{1,0:T(8,128)(2,1)}, bf16[1152,256]{1,0:T(8,128)(2,1)S(1)}, u32[]{:S(2)}) copy-start(bf16[1152,256]{1,0:T(8,128)(2,1)S(1)} %all_gather.51) | copy-start | bytes 1769476
  110.7 41.3 %copy-start.16 = (f32[256,256]{0,1:T(8,128)}, f32[256,256]{0,1:T(8,128)S(1)}, u32[]{:S(2)}) copy-start(f32[256,256]{0,1:T(8,128)S(1)} %get-tuple-element.63) | copy-start | bytes 786436
  110.7 41.3 %copy-start.62 = (f32[256]{0:T(256)}, f32[256]{0:T(256)S(1)}, u32[]{:S(2)}) copy-start(f32[256]{0:T(256)S(1)} %get-tuple-element.62) | copy-start | bytes 3076
  110.8 41.2 %copy-start.47 = (f32[256]{0:T(256)}, f32[256]{0:T(256)S(1)}, u32[]{:S(2)}) copy-start(f32[256]{0:T(256)S(1)} %fusion.77) | copy-start | bytes 3076
  117.9 43.2 %copy-start.22 = (bf16[512,1,256]{0,2,1:T(8,128)(2,1)}, bf16[512,1,256]{0,2,1:T(8,128)(2,1)S(1)}, u32[]{:S(2)}) copy-start(bf16[512,1,256]{0,2,1:T(8,128)(2,1)S(1)} %all-gather) | copy-start | bytes 786436
  144.8 7.8 copy-start.14
  152.0 8.1 copy-start.49
  153.9 6.4 copy-start.25
  153.9 6.4 copy-start.27
  161.2 1.1 copy-start.29
  163.9 2.9 copy-start.7
  166.7 1.4 copy-start.33
  167.4 329.9 %copy-start.41 = (f32[4,256]{1,0:T(4,128)}, f32[4,256]{1,0:T(4,128)S(1)}, u32[]{:S(2)}) copy-start(f32[4,256]{1,0:T(4,128)S(1)} %log_add_fusion) | copy-start | bytes 12292
  433.1 10.5 copy-start.12
  433.1 10.5 copy-start.34
  443.5 1.3 copy-start.1
  493.0 3.0 copy-start.4
  493.0 2.1 copy-start.18
  496.0 1.3 copy-start.31
  496.0 1.3 copy-start.30
  497.3 3.0 copy-start.13
  500.3 11.2 copy-start.42
  511.2 42.5 %reduce-scatter.7.cloned.1.call-start = ((), (), s32[]{:S(2)}) async-start(), calls=%async_computation.9 | async-start | bytes 393216 | tf_op jit(solution)/shard_map/reduce_scatter | solution.py:199
  511.5 2.2 copy-start.10
  517.0 186.6 %reduce-scatter.11.cloned.1.call-start = ((), (), s32[]{:S(2)}) async-start(), calls=%async_computation.11 | async-start | bytes 19427328 | tf_op jit(solution)/shard_map/reduce_scatter | solution.py:252
  532.7 1.4 copy-start.26
  532.7 2.0 copy-start.3
  532.8 2.0 copy-start.36
  532.8 428.8 %reduce-scatter.13.cloned.1.call-start = ((), (), s32[]{:S(2)}) async-start(), calls=%async_computation.12 | async-start | bytes 37601280
  534.7 1.1 copy-start.24
  535.8 19.0 %copy-start.54 = (f32[256]{0:T(256)S(1)}, f32[256]{0:T(256)}, u32[]{:S(2)}) copy-start(f32[256]{0:T(256)} %copy-done.53) | copy-start | bytes 3076
  535.8 19.0 %copy-start.61 = (f32[128]{0:T(128)S(1)}, f32[128]{0:T(128)}, u32[]{:S(2)}) copy-start(f32[128]{0:T(128)} %copy-done.60) | copy-start | bytes 1540
  535.8 19.5 %copy-start.17 = (f32[256,256]{0,1:T(8,128)S(1)}, f32[256,256]{0,1:T(8,128)}, u32[]{:S(2)}) copy-start(f32[256,256]{0,1:T(8,128)} %copy-done.16) | copy-start | bytes 786436
  535.8 19.5 %copy-start.48 = (f32[256]{0:T(256)S(1)}, f32[256]{0:T(256)}, u32[]{:S(2)}) copy-start(f32[256]{0:T(256)} %copy-done.47) | copy-start | bytes 3076
  535.8 19.6 %copy-start.52 = (f32[256]{0:T(256)S(1)}, f32[256]{0:T(256)}, u32[]{:S(2)}) copy-start(f32[256]{0:T(256)} %copy-done.51) | copy-start | bytes 3076
  535.8 19.7 %copy-start.63 = (f32[256]{0:T(256)S(1)}, f32[256]{0:T(256)}, u32[]{:S(2)}) copy-start(f32[256]{0:T(256)} %copy-done.62) | copy-start | bytes 3076
  552.7 3.0 copy-start.8
  552.7 3.0 copy-start.56
  586.6 532.3 %all-reduce.16.cloned.1.call-start = ((), (), s32[]{:S(2)}) async-start(), calls=%async_computation.13 | async-start | bytes 6709248 | tf_op jit(solution)/shard_map/psum | solution.py:261
  961.6 2.6 copy-start.21
  965.4 79.2 %copy-start.58 = (f32[256]{0:T(256)S(1)}, f32[256]{0:T(256)}, u32[]{:S(2)}) copy-start(f32[256]{0:T(256)} %copy-done.57) | copy-start | bytes 3076
  965.4 79.2 %copy-start.5 = (f32[256,1152]{1,0:T(8,128)S(1)}, f32[256,1152]{1,0:T(8,128)}, u32[]{:S(2)}) copy-start(f32[256,1152]{1,0:T(8,128)} %copy-done.4) | copy-start | bytes 3538948
  1124.2 2.3 copy-start.11
  (17 other events, 14.2 us)
Sparse Core Ops, SparseCore 0:
  10.6 51.0 all-gather.6
  64.1 47.8 all-gather.8
  114.4 107.9 all-gather.10
  224.7 103.0 all-gather.12
  330.0 103.0 all-gather.14
  511.4 11.7 reduce-scatter.8
  525.6 15.1 reduce-scatter.6
  545.3 158.2 reduce-scatter.10
  708.8 252.7 reduce-scatter.12
  964.1 154.8 all-reduce.15
where the time goes:
time: 1140 us
  waiting for transfers between devices  689 us (60%)
  blocking collectives  211 us (19%)
  matrix products  133 us (12%)
  other arithmetic  62.1 us (5%)
  local copies, waits for them, and re-layouts  23.6 us (2%)
  between operations  16.7 us (1%)
    unnamed x11, waiting for transfers between devices  261 us
    reduce_scatter x1, waiting for transfers between devices, body(): lax.psum_scatter(jnp.concatenate([top_part, bottom_part], axis=1).reshape...  117 us
    all_gather x1, waiting for transfers between devices, body(): lax.all_gather(w_down, 'fsdp', axis=0, tiled=True)  92.4 us
    all_gather x1, waiting for transfers between devices, body(): lax.all_gather(w_up, 'fsdp', axis=0, tiled=True)  91.9 us
    psum x1, blocking collectives, body(): lax.psum((grad_gain_a, grad_gain_b, grad_gain_c, grad_gain_d, grad_query_...  74.9 us
    psum x1, waiting for transfers between devices, body(): lax.psum(in_piece, ('dp', 'seq')).astype(jnp.float32)  73.2 us
    unnamed x1, blocking collectives  71.3 us
    all_gather x1, waiting for transfers between devices, body(): lax.all_gather(w_gate, 'fsdp', axis=0, tiled=True)  53.3 us
  transfers between devices with their start and end apart: 10, of which 6 were waited for; matrix products, arithmetic and copies ran while one was open for 11% of the time, Pallas kernels for 0%

commit v1 on v0

v1 whole, which is shorter than its diff:
```python
import functools
import math

import jax
import jax.numpy as jnp
from jax import lax
from jax.experimental import pallas as pl
from jax.experimental.pallas import tpu as pltpu
from jax.sharding import PartitionSpec as P

F32, BF16 = jnp.float32, jnp.bfloat16
MESH = pl.DeviceIdType.MESH
NN = (((1,), (0,)), ((), ()))
NT = (((1,), (1,)), ((), ()))
TN = (((0,), (0,)), ((), ()))
EPS = 1e-06
MIB = 2**20
PART = 112
CORE_UNITS = 8 * PART


def dot(a, b, dims=NN):
    return lax.dot_general(a, b, dims, preferred_element_type=F32)


class Place:
    def __init__(self):
        shard = lax.axis_index("fsdp")
        self.x = lax.axis_index("dp")
        self.z = shard // 4
        self.yh = lax.rem(shard // 2, 2)
        self.c = lax.rem(shard, 2)
        self.yl = lax.axis_index("seq")

    def to(self, dx=0, dy=0, dz=0, dc=0):
        x, z, yh, yl, c = self.x, self.z, self.yh, self.yl, self.c
        if dx:
            x = lax.rem(x + dx, 4)
        if dz:
            z = lax.rem(z + dz, 4)
        if dy:
            y = lax.rem(yh * 2 + yl + dy, 4)
            yh, yl = y // 2, lax.rem(y, 2)
        if dc:
            c = 1 - c
        return (x, (z * 2 + yh) * 2 + c, yl)

    def mate(self):
        return self.to(dc=1)

    def pair(self):
        return (self.x, (self.z * 2 + self.yh) * 2 + self.c, 1 - self.yl)


def greet(peers):
    barrier = pltpu.get_barrier_semaphore()
    for peer in peers:
        pl.semaphore_signal(barrier, inc=1, device_id=peer, device_id_type=MESH)
    pl.semaphore_wait(barrier, len(peers))


class Lines:
    def __init__(self, send, recv):
        self.send, self.recv, self.used, self.open = send, recv, 0, []

    def copy(self, src, dst, device):
        k = self.used
        self.used += 1
        made = pltpu.make_async_remote_copy(
            src_ref=src,
            dst_ref=dst,
            send_sem=self.send.at[k],
            recv_sem=self.recv.at[k],
            device_id=device,
            device_id_type=MESH,
        )
        made.start()
        self.open.append(made)
        return made

    def drain(self):
        for made in self.open:
            made.wait_send()
        self.open = []


def gate_terms(gate, up):
    k, c = math.sqrt(2.0 / math.pi), 0.044715
    square = gate * gate
    t = jnp.tanh(gate * (k + (k * c) * square))
    half = 0.5 + 0.5 * t
    act = gate * half
    slope = half + 0.5 * gate * (1.0 - t * t) * (k + (3.0 * k * c) * square)
    return act, slope * up, act * up


class RingGather:
    def __init__(self, here, lines, own, full):
        self.here, self.lines, self.own, self.full = here, lines, own, full

    def start(self):
        here, own, full, copy = self.here, self.own, self.full, self.lines.copy
        n = own.shape[0]
        h = n // 2
        right, left = here.to(dx=1), here.to(dx=3)
        lo, hi = pl.ds(0, h), pl.ds(h, h)
        self.core = copy(own, full.at[0, pl.ds(n, n)], here.mate())
        self.a0 = copy(own.at[lo], full.at[3, lo], right)
        self.b0 = copy(own.at[hi], full.at[1, hi], left)
        self.a1 = copy(own.at[hi], full.at[3, hi], right)
        self.b1 = copy(own.at[lo], full.at[1, lo], left)
        full[0, :n] = own[...]

    def ready0(self):
        self.core.wait_recv()

    def relay(self):
        here, full, copy = self.here, self.full, self.lines.copy
        n = self.own.shape[0]
        h = n // 2
        lo, hi, both, other = pl.ds(0, h), pl.ds(h, h), pl.ds(0, n), pl.ds(n, n)
        right, left, mate = here.to(dx=1), here.to(dx=3), here.mate()
        self.a0.wait_recv()
        self.a2 = copy(full.at[3, lo], full.at[2, lo], right)
        self.b0.wait_recv()
        self.b2 = copy(full.at[1, hi], full.at[2, hi], left)
        self.a1.wait_recv()
        self.f3 = copy(full.at[3, both], full.at[3, other], mate)
        self.b1.wait_recv()
        self.f1 = copy(full.at[1, both], full.at[1, other], mate)

    def ready3(self):
        self.f3.wait_recv()

    def ready1(self):
        self.f1.wait_recv()

    def ready2(self):
        n = self.own.shape[0]
        self.a2.wait_recv()
        self.b2.wait_recv()
        f2 = self.lines.copy(
            self.full.at[2, pl.ds(0, n)], self.full.at[2, pl.ds(n, n)], self.here.mate()
        )
        f2.wait_recv()


class RingSum:
    def __init__(self, here, lines, mine, landed, cross, stage_core, stage_ring):
        self.here, self.lines, self.mine = here, lines, mine
        self.landed, self.cross = landed, cross
        self.stage_core, self.stage_ring = stage_core, stage_ring
        self.pending = []

    def add(self, r, term):
        here = self.here
        self.stage_core[r] = term(1).astype(BF16)
        made = self.lines.copy(self.stage_core.at[r], self.cross.at[r], here.mate())
        near = term(0)
        made.wait_recv()
        near = near + self.cross[r].astype(F32)
        if r == 0:
            self.mine[...] = near
        else:
            self.stage_ring[r - 1] = near.astype(BF16)
            self.pending.append(
                self.lines.copy(
                    self.stage_ring.at[r - 1], self.landed.at[3 - r], here.to(dx=r)
                )
            )

    def total(self):
        for made in self.pending:
            made.wait_recv()
        out = self.mine[...]
        for j in range(3):
            out = out + self.landed[j].astype(F32)
        return out


def norm_back(v, u, n):
    r = lax.rsqrt(jnp.sum(v * v, axis=-1, keepdims=True) * (1.0 / n) + EPS)
    inner = jnp.sum(u * v, axis=-1, keepdims=True) * (1.0 / n)
    return r, r * u - v * (r * r * r * inner)


def mlp_kernel(
    own_x, middle, cot, gain_in, gain_out, w_gate, w_up, w_down,
    layer_out, middle_grad, d_gain_in, d_gain_out, d_in, d_down,
    xs, gs, act, slope, hidden, cross_f, cross_b, landed_f, landed_b, stage_core, stage_ring,
    mine, mixed_grad, send, recv,
):
    here = Place()
    greet([here.mate()] + [here.to(dx=d) for d in (1, 2, 3)])
    lines = Lines(send, recv)
    n, width = own_x.shape

    ring = RingGather(here, lines, own_x, xs)
    sums = RingSum(here, lines, mine, landed_f, cross_f, stage_core, stage_ring)
    ring.start()

    def forward(r):
        x = xs[r]
        a, s, h = gate_terms(dot(x, w_gate[...]), dot(x, w_up[...]))
        act[r] = a.astype(BF16)
        slope[r] = s.astype(BF16)
        hidden[r] = h.astype(BF16)
        sums.add(r, lambda q: dot(hidden[r, q * n : (q + 1) * n], w_down[...]))

    ring.ready0()
    forward(0)
    ring.relay()
    ring.ready3()
    forward(3)
    ring.ready1()
    forward(1)
    ring.ready2()
    forward(2)
    mixed = sums.total()
    lines.drain()

    cot_f = cot[...].astype(F32)
    u = cot_f * (1.0 + gain_out[...])
    factor, grad = norm_back(mixed, u, width)
    layer_out[...] = (middle[...] + mixed * factor * (1.0 + gain_out[...])).astype(BF16)
    d_gain_out[...] = jnp.sum(cot_f * mixed * factor, axis=0, keepdims=True)
    mixed_grad[...] = grad.astype(BF16)

    ring = RingGather(here, lines, mixed_grad, gs)
    sums = RingSum(here, lines, mine, landed_b, cross_b, stage_core, stage_ring)
    ring.start()

    def backward(r):
        hidden_grad = dot(gs[r], w_down[...], NT)
        act[r] = (hidden_grad * act[r].astype(F32)).astype(BF16)
        slope[r] = (hidden_grad * slope[r].astype(F32)).astype(BF16)

        def term(q):
            rows = slice(q * n, (q + 1) * n)
            return dot(slope[r, rows], w_gate[...], NT) + dot(act[r, rows], w_up[...], NT)

        sums.add(r, term)

    ring.ready0()
    backward(0)
    ring.relay()
    ring.ready3()
    backward(3)
    ring.ready1()
    backward(1)
    ring.ready2()
    backward(2)

    flat = lambda ref: ref[...].reshape(ref.shape[0] * ref.shape[1], ref.shape[2])
    grad_down = dot(flat(hidden), flat(gs), TN)
    for k in range(8):
        for p in range(4):
            rows = min(32, PART - 32 * p)
            at = PART * k + 32 * p
            d_down[k // 2, k % 2, p // 2, p % 2, :rows] = grad_down[at : at + rows].astype(BF16)
        d_down[k // 2, k % 2, 1, 1, PART - 96 :] = jnp.zeros((128 - PART, width), BF16)
    for mat, side in ((0, slope), (1, act)):
        grad_side = dot(flat(xs), flat(side), TN)
        for f in range(16):
            d_in[f // 4, (f // 2) % 2, mat, f % 2] = grad_side[72 * f : 72 * f + 72].astype(BF16)

    update = sums.total()
    base = middle[...]
    u = update * (1.0 + gain_in[...])
    factor, grad = norm_back(base, u, width)
    d_gain_in[...] = jnp.sum(update * base * factor, axis=0, keepdims=True)
    middle_grad[...] = cot[...].astype(F32) + grad
    lines.drain()


def mlp_block(own_x, middle, cot, gain_in, gain_out, w_gate, w_up, w_down):
    n, width = own_x.shape
    units = w_gate.shape[1]
    vmem = pl.BlockSpec(memory_space=pltpu.VMEM)
    shape = jax.ShapeDtypeStruct
    scratch = (
        [pltpu.VMEM((4, 2 * n, width), BF16)] * 2
        + [pltpu.VMEM((4, 2 * n, units), BF16)] * 3
        + [pltpu.VMEM((4, n, width), BF16)] * 2
        + [pltpu.VMEM((3, n, width), BF16)] * 2
        + [pltpu.VMEM((4, n, width), BF16), pltpu.VMEM((3, n, width), BF16)]
        + [pltpu.VMEM((n, width), F32), pltpu.VMEM((n, width), BF16)]
        + [pltpu.SemaphoreType.DMA((34,)), pltpu.SemaphoreType.DMA((34,))]
    )
    return pl.pallas_call(
        mlp_kernel,
        out_shape=(
            shape((n, width), BF16),
            shape((n, width), F32),
            shape((1, width), F32),
            shape((1, width), F32),
            shape((4, 2, 2, 2, width // 16, units), BF16),
            shape((4, 2, 2, 2, 32, width), BF16),
        ),
        in_specs=[vmem] * 8,
        out_specs=(vmem,) * 6,
        scratch_shapes=scratch,
        compiler_params=pltpu.CompilerParams(
            collective_id=1, has_side_effects=True, vmem_limit_bytes=63 * MIB
        ),
        name="mlp_block",
    )(own_x, middle, cot, gain_in, gain_out, w_gate, w_up, w_down)


def plane_peers(here):
    return [here.to(dz=d) for d in (1, 2, 3)] + [here.to(dy=d) for d in (1, 2, 3)]


def plane_gather_first(here, lines, local, pairs):
    z, yh, yl = here.z, here.yh, here.yl
    hops = []
    for k, (own, full) in enumerate(pairs):
        keep = pltpu.make_async_copy(own.at[yl], full.at[z, yh, yl], local.at[k])
        keep.start()
        by_z = [lines.copy(own.at[yl, 0], full.at[z, yh, yl, 0], here.to(dz=d)) for d in (1, 3, 2)]
        by_y = [lines.copy(own.at[yl, 1], full.at[z, yh, yl, 1], here.to(dy=d)) for d in (1, 3, 2)]
        keep.wait()
        hops.append((by_z, by_y))
    return hops


def plane_gather_second(here, lines, pairs, hops):
    z, yh, yl = here.z, here.yh, here.yl
    last = []
    for (_, full), (by_z, by_y) in zip(pairs, hops):
        for made in by_z:
            made.wait_recv()
        block = full.at[:, yh, yl, 0]
        last += [lines.copy(block, block, here.to(dy=d)) for d in (1, 3, 2)]
        for made in by_y:
            made.wait_recv()
        block = full.at[z, :, :, 1]
        last += [lines.copy(block, block, here.to(dz=d)) for d in (1, 3, 2)]
    return last


def gather_kernel(
    own_qkv, own_out, own_in, own_down, full_qkv, full_out, full_in, full_down,
    chip_in, send, recv, local,
):
    here = Place()
    greet([here.mate()] + plane_peers(here))
    lines = Lines(send, recv)
    c = here.c
    across = lines.copy(own_in.at[1 - c], chip_in.at[:, c], here.mate())
    keep = pltpu.make_async_copy(own_in.at[c], chip_in.at[:, c], local.at[4])
    keep.start()
    attn = [(own_qkv, full_qkv.at[:, :, c]), (own_out, full_out.at[:, :, c])]
    hops = plane_gather_first(here, lines, local, attn)
    keep.wait()
    across.wait_recv()
    mlp = [(chip_in, full_in), (own_down, full_down)]
    last = plane_gather_second(here, lines, attn, hops)
    hops = plane_gather_first(here, lines, local, mlp)
    for made in last:
        made.wait_recv()
    cores = [lines.copy(full.at[:, :, c], full.at[:, :, c], here.mate()) for full in (full_qkv, full_out)]
    last = plane_gather_second(here, lines, mlp, hops)
    for made in last + cores:
        made.wait_recv()
    lines.drain()


def gather_block(own_qkv, own_out, own_in, own_down):
    hbm = pl.BlockSpec(memory_space=pl.ANY)
    shape = lambda *s: jax.ShapeDtypeStruct(s, BF16)
    piece = lambda a: a.shape[2:]
    return pl.pallas_call(
        gather_kernel,
        out_shape=(
            shape(4, 2, 2, 2, 2, *piece(own_qkv)),
            shape(4, 2, 2, 2, 2, *piece(own_out)),
            shape(4, 2, 2, 2, *own_in.shape[2:]),
            shape(4, 2, 2, 2, *piece(own_down)),
        ),
        in_specs=[hbm] * 4,
        out_specs=(hbm,) * 4,
        scratch_shapes=[
            pltpu.VMEM(own_in.shape, BF16),
            pltpu.SemaphoreType.DMA((51,)),
            pltpu.SemaphoreType.DMA((51,)),
            pltpu.SemaphoreType.DMA((5,)),
        ],
        compiler_params=pltpu.CompilerParams(
            collective_id=0, has_side_effects=True, vmem_limit_bytes=60 * MIB
        ),
        name="gather_weights",
    )(own_qkv, own_out, own_in, own_down)


class PlaneSum:
    def __init__(self, here, lines, grads, landed_a, sums_a, landed_b, sums_b, last_a, last_b):
        self.here, self.lines, self.grads = here, lines, grads
        self.landed_a, self.sums_a, self.last_a = landed_a, sums_a, last_a
        self.landed_b, self.sums_b, self.last_b = landed_b, sums_b, last_b

    @staticmethod
    def scratch(piece):
        vm = lambda *lead: pltpu.VMEM((*lead, *piece), BF16)
        return [vm(3, 4), vm(4), vm(3, 2, 2), vm(2, 2), vm(3), vm(3)]

    def first(self):
        here, g, copy = self.here, self.grads, self.lines.copy
        self.a, self.b = [], []
        for d in (1, 3, 2):
            _, shard, yl = here.to(dy=d)
            yh = lax.rem(shard // 2, 2)
            self.a.append(copy(g.at[:, yh, yl, 0], self.landed_a.at[d - 1], here.to(dy=d)))
            z = here.to(dz=d)[1] // 4
            self.b.append(copy(g.at[z, :, :, 1], self.landed_b.at[d - 1], here.to(dz=d)))

    def second(self):
        here, g, copy = self.here, self.grads, self.lines.copy
        for made in self.a:
            made.wait_recv()
        for k in range(4):
            total = g[k, here.yh, here.yl, 0].astype(F32)
            for j in range(3):
                total = total + self.landed_a[j, k].astype(F32)
            self.sums_a[k] = total.astype(BF16)
        self.a = []
        for d in (1, 3, 2):
            z = here.to(dz=d)[1] // 4
            self.a.append(copy(self.sums_a.at[z], self.last_a.at[d - 1], here.to(dz=d)))
        for made in self.b:
            made.wait_recv()
        for k in range(4):
            total = g[here.z, k // 2, k % 2, 1].astype(F32)
            for j in range(3):
                total = total + self.landed_b[j, k // 2, k % 2].astype(F32)
            self.sums_b[k // 2, k % 2] = total.astype(BF16)
        self.b = []
        for d in (1, 3, 2):
            _, shard, yl = here.to(dy=d)
            yh = lax.rem(shard // 2, 2)
            self.b.append(copy(self.sums_b.at[yh, yl], self.last_b.at[d - 1], here.to(dy=d)))

    def result(self, path):
        here = self.here
        for made in (self.a, self.b)[path]:
            made.wait_recv()
        own = self.sums_a[here.z] if path == 0 else self.sums_b[here.yh, here.yl]
        last = (self.last_a, self.last_b)[path]
        total = own.astype(F32)
        for j in range(3):
            total = total + last[j].astype(F32)
        return total


def reduce_kernel(
    g_in, g_down, g_qkv, g_out, o_in, o_down, o_qkv, o_out,
    chip_qkv, chip_out, cross_qkv, cross_out, swap, half_qkv, half_out, land_qkv, land_out, *rest,
):
    here = Place()
    send, recv = rest[-2:]
    x, yl, c = here.x, here.yl, here.c
    greet([here.mate()] + plane_peers(here) + [here.to(dx=d) for d in (1, 2, 3)])
    lines = Lines(send, recv)
    copy = lines.copy
    cross = [
        copy(g.at[:, :, 1 - c], land, here.mate()) for g, land in ((g_qkv, cross_qkv), (g_out, cross_out))
    ]
    sums = [
        PlaneSum(here, lines, g, *rest[6 * k : 6 * k + 6])
        for k, g in enumerate((g_in, g_down, chip_qkv, chip_out))
    ]
    sums[0].first()
    sums[1].first()
    for made, g, land, chip in (
        (cross[0], g_qkv, cross_qkv, chip_qkv),
        (cross[1], g_out, cross_out, chip_out),
    ):
        made.wait_recv()
        for z in range(4):
            for yh in range(2):
                chip[z, yh] = (g[z, yh, c].astype(F32) + land[z, yh].astype(F32)).astype(BF16)
    sums[2].first()
    sums[3].first()
    for part in sums:
        part.second()

    swap[0] = sums[0].result(0).astype(BF16)
    swap[1] = sums[0].result(1).astype(BF16)
    across = copy(swap.at[1 - c], o_in.at[x, yl, c], here.mate())
    o_in[x, yl, c] = swap[c]
    for path in (0, 1):
        o_down[x, yl, path] = sums[1].result(path).astype(BF16)
    to_pair = [copy(o_down.at[x, yl], o_down.at[x, yl], here.pair())]
    across.wait_recv()
    to_pair.append(copy(o_in.at[x, yl], o_in.at[x, yl], here.pair()))
    for path in (0, 1):
        half_qkv[path] = sums[2].result(path).astype(BF16)
        half_out[path] = sums[3].result(path).astype(BF16)
    by_x = []
    for d in (1, 3, 2):
        by_x.append(copy(half_qkv, land_qkv.at[d - 1], here.to(dx=d)))
        by_x.append(copy(half_out, land_out.at[d - 1], here.to(dx=d)))
    for made in to_pair:
        made.wait_recv()
    spread = []
    for d in (1, 3, 2):
        spread.append(copy(o_in.at[x], o_in.at[x], here.to(dx=d)))
        spread.append(copy(o_down.at[x], o_down.at[x], here.to(dx=d)))
    for made in by_x:
        made.wait_recv()
    for half, land, out in ((half_qkv, land_qkv, o_qkv), (half_out, land_out, o_out)):
        for path in (0, 1):
            total = half[path].astype(F32)
            for j in range(3):
                total = total + land[j, path].astype(F32)
            out[yl, path] = total.astype(BF16)
    ends = [copy(o.at[yl], o.at[yl], here.pair()) for o in (o_qkv, o_out)]
    for made in spread + ends:
        made.wait_recv()
    lines.drain()


def reduce_block(g_in, g_down, g_qkv, g_out):
    vmem = pl.BlockSpec(memory_space=pltpu.VMEM)
    shape = lambda *s: jax.ShapeDtypeStruct(s, BF16)
    p_in, p_down, p_qkv, p_out = g_in.shape[4:], g_down.shape[4:], g_qkv.shape[5:], g_out.shape[5:]
    vm = lambda *s: pltpu.VMEM(s, BF16)
    scratch = [vm(4, 2, 2, 2, *p_qkv), vm(4, 2, 2, 2, *p_out)] * 2
    scratch += [vm(2, *p_in), vm(2, *p_qkv), vm(2, *p_out), vm(3, 2, *p_qkv), vm(3, 2, *p_out)]
    for piece in (p_in, p_down, p_qkv, p_out):
        scratch += PlaneSum.scratch(piece)
    scratch += [pltpu.SemaphoreType.DMA((67,))] * 2
    return pl.pallas_call(
        reduce_kernel,
        out_shape=(
            shape(4, 2, 2, *p_in),
            shape(4, 2, 2, *p_down),
            shape(2, 2, *p_qkv),
            shape(2, 2, *p_out),
        ),
        in_specs=[vmem] * 4,
        out_specs=(vmem,) * 4,
        scratch_shapes=scratch,
        compiler_params=pltpu.CompilerParams(
            collective_id=2, has_side_effects=True, vmem_limit_bytes=60 * MIB
        ),
        name="reduce_grads",
    )(g_in, g_down, g_qkv, g_out)


def rms_norm(values, scale_gain):
    factor = lax.rsqrt(jnp.mean(values * values, axis=-1, keepdims=True) + EPS)
    return values * factor * (1.0 + scale_gain)


def rotate(values, positions):
    half_dim = values.shape[-1] // 2
    frequency = jnp.exp(
        jnp.arange(half_dim, dtype=F32) * (-2.0 * math.log(1000000.0) / values.shape[-1])
    )
    angles = positions[:, None] * frequency[None, :]
    cosine = jnp.cos(angles)[:, None, :]
    sine_part = jnp.sin(angles)[:, None, :]
    first_half = values[..., :half_dim]
    second_half = values[..., half_dim:]
    return jnp.concatenate(
        [
            first_half * cosine - second_half * sine_part,
            second_half * cosine + first_half * sine_part,
        ],
        axis=-1,
    )


def swap_pair(value):
    return lax.ppermute(value, "seq", [(0, 1), (1, 0)])


def body(
    tokens,
    w_query,
    w_key,
    w_value,
    w_out,
    w_gate,
    w_up,
    w_down,
    pre_attn_gain,
    post_attn_gain,
    pre_mlp_gain,
    post_mlp_gain,
    query_gain,
    key_gain,
    cotangent,
):
    n, width = tokens.shape
    rows = w_query.shape[0]
    head_dim = w_key.shape[1]
    heads = w_query.shape[1] // head_dim
    units = w_gate.shape[1]
    out_width = heads * head_dim
    block = units // 16
    x_at = lax.axis_index("dp")
    gains = (pre_attn_gain, post_attn_gain, pre_mlp_gain, post_mlp_gain, query_gain, key_gain)

    qkv = jnp.concatenate([w_query, w_key, w_value], axis=1)
    gain_row = jnp.concatenate(gains)
    gain_row = jnp.pad(gain_row, (0, qkv.shape[1] - gain_row.shape[0]))[None, :]
    qkv = jnp.concatenate([qkv, jnp.pad(gain_row, ((0, 7), (0, 0)))], axis=0)
    own_qkv = qkv.reshape(rows + 8, 2, 2, -1).transpose(1, 2, 0, 3)
    own_out = w_out.reshape(2, 2, -1, width)

    def columns(w):
        w = jnp.pad(w.reshape(rows, 8, 2, block), ((0, 0),) * 3 + ((0, 4 * PART - block),))
        w = lax.dynamic_slice_in_dim(w, x_at * PART, PART, axis=3)
        return w.transpose(2, 0, 1, 3).reshape(2, rows, 8 * PART)

    own_in = jnp.stack([columns(w_gate), columns(w_up)], axis=1)
    down = jnp.pad(w_down, ((0, 4 * PART - block), (0, 0)))
    down = lax.dynamic_slice_in_dim(down, x_at * PART, PART, axis=0)
    own_down = jnp.pad(down, ((0, 128 - PART), (0, 0))).reshape(2, 2, 32, width)

    full_qkv, full_out, full_in, full_down = gather_block(own_qkv, own_out, own_in, own_down)
    gain_rows = full_qkv[:, :, :, 0, 0, rows, :].reshape(16, -1).astype(F32)
    piece = width // 16
    gain_set = [gain_rows[:, piece * k : piece * (k + 1)].reshape(1, -1) for k in range(4)]
    piece_h = head_dim // 16
    at = 4 * piece
    gain_set += [
        gain_rows[:, at + piece_h * k : at + piece_h * (k + 1)].reshape(-1) for k in range(2)
    ]
    attn_gain_in, attn_gain_out, mlp_gain_in, mlp_gain_out, query_scale, key_scale = gain_set
    full_qkv = full_qkv[..., :rows, :].reshape(16, 4, rows, -1).transpose(0, 2, 1, 3)
    full_qkv = full_qkv.reshape(width, out_width + 2 * head_dim)
    full_out = full_out.reshape(out_width, width)
    gate_up = full_in.transpose(2, 0, 1, 3, 4, 5).reshape(2, width, CORE_UNITS)
    full_down = full_down.reshape(8, 128, width)[:, :PART].reshape(CORE_UNITS, width)

    seq_start = lax.axis_index("seq") * n
    query_places = seq_start + jnp.arange(n, dtype=jnp.int32)
    positions = query_places.astype(F32)
    inputs = tokens.astype(F32)
    normed_f, attn_in_pull = jax.vjp(rms_norm, inputs, attn_gain_in[0])
    normed = normed_f.astype(BF16)
    qkv_pre = dot(normed, full_qkv)
    query_pre = qkv_pre[:, :out_width].reshape(n, heads, head_dim)
    key_pre = qkv_pre[:, out_width : out_width + head_dim].reshape(n, 1, head_dim)
    value_local = qkv_pre[:, out_width + head_dim :].astype(BF16)

    def shape_heads(query_in, key_in, query_gain_f, key_gain_f):
        query_out = rotate(rms_norm(query_in, query_gain_f), positions) * head_dim ** (-0.5)
        key_out = rotate(rms_norm(key_in, key_gain_f), positions)
        return (query_out, key_out)

    (query_f, key_f), heads_pull = jax.vjp(shape_heads, query_pre, key_pre, query_scale, key_scale)
    queries = query_f.astype(BF16)
    kv_local = jnp.concatenate([key_f[:, 0, :].astype(BF16), value_local], axis=1)
    kv_other = swap_pair(kv_local)
    low_half = lax.axis_index("seq") == 0
    kv = jnp.concatenate(
        [jnp.where(low_half, kv_local, kv_other), jnp.where(low_half, kv_other, kv_local)], axis=0
    )
    key_rows, value_rows = kv[:, :head_dim], kv[:, head_dim:]
    seq_length = kv.shape[0]
    allowed = jnp.arange(seq_length, dtype=jnp.int32)[None, :] <= query_places[:, None]
    scores = jnp.einsum("ihd,jd->hij", queries, key_rows, preferred_element_type=F32)
    scores = jnp.where(allowed[None, :, :], scores, -1e30)
    row_peak = jnp.max(scores, axis=-1, keepdims=True)
    exp_terms = jnp.exp(scores - row_peak)
    row_total = jnp.sum(exp_terms, axis=-1, keepdims=True)
    prob_rows = exp_terms / row_total
    probs_bf = prob_rows.astype(BF16)
    context = jnp.einsum("hij,jd->ihd", probs_bf, value_rows, preferred_element_type=F32)
    context = context.astype(BF16).reshape(n, out_width)
    attended = dot(context, full_out)
    post_attn, attn_out_pull = jax.vjp(rms_norm, attended, attn_gain_out[0])
    middle = inputs + post_attn
    mlp_in = rms_norm(middle, mlp_gain_in[0]).astype(BF16)

    layer_out, middle_grad, grad_gain_c, grad_gain_d, g_in, g_down = mlp_block(
        mlp_in, middle, cotangent, mlp_gain_in, mlp_gain_out, gate_up[0], gate_up[1], full_down
    )

    attended_grad_f, grad_gain_b = attn_out_pull(middle_grad)
    attended_grad = attended_grad_f.astype(BF16)
    context_grad = dot(attended_grad, full_out, NT).astype(BF16).reshape(n, heads, head_dim)
    prob_grad = jnp.einsum("ihd,jd->hij", context_grad, value_rows, preferred_element_type=F32)
    row_dot = jnp.sum(prob_rows * prob_grad, axis=-1, keepdims=True)
    score_grad = (prob_rows * (prob_grad - row_dot)).astype(BF16)
    query_grad = jnp.einsum("hij,jd->ihd", score_grad, key_rows, preferred_element_type=F32)
    query_grad = query_grad.astype(BF16)
    key_part = jnp.einsum("hij,ihd->jd", score_grad, queries, preferred_element_type=F32)
    value_part = jnp.einsum("hij,ihd->jd", probs_bf, context_grad, preferred_element_type=F32)
    kv_part = jnp.concatenate([key_part, value_part], axis=1)
    kept = jnp.where(low_half, kv_part[:n], kv_part[n:])
    given = jnp.where(low_half, kv_part[n:], kv_part[:n]).astype(BF16)
    kv_grad = (kept + swap_pair(given).astype(F32)).astype(BF16)
    key_grad, value_grad = kv_grad[:, :head_dim], kv_grad[:, head_dim:]
    query_pre_grad, key_pre_grad, grad_query_scale, grad_key_scale = heads_pull(
        (query_grad.astype(F32), key_grad.astype(F32)[:, None, :])
    )
    attn_side = jnp.concatenate(
        [
            query_pre_grad.astype(BF16).reshape(n, out_width),
            key_pre_grad.reshape(n, head_dim).astype(BF16),
            value_grad,
        ],
        axis=1,
    )
    normed_grad = dot(attn_side, full_qkv, NT)
    input_part, grad_gain_a = attn_in_pull(normed_grad)
    grad_tokens = (middle_grad + input_part).astype(BF16)

    g_qkv = dot(normed, attn_side, TN).astype(BF16).reshape(16, rows, -1)
    gain_grads = [
        g.reshape(16, -1)
        for g in (grad_gain_a, grad_gain_b, grad_gain_c, grad_gain_d, grad_query_scale, grad_key_scale)
    ]
    gain_grads = jnp.concatenate(gain_grads, axis=1).astype(BF16)
    gain_grads = jnp.pad(gain_grads, ((0, 0), (0, g_qkv.shape[2] - gain_grads.shape[1])))
    gain_grads = jnp.pad(gain_grads[:, None, :], ((0, 0), (0, 7), (0, 0)))
    g_qkv = jnp.concatenate([g_qkv, gain_grads], axis=1)
    g_qkv = g_qkv.reshape(4, 2, 2, rows + 8, 2, 2, -1).transpose(0, 1, 2, 4, 5, 3, 6)
    g_out = dot(context, attended_grad, TN).astype(BF16).reshape(4, 2, 2, 2, 2, -1, width)

    o_in, o_down, o_qkv, o_out = reduce_block(g_in, g_down, g_qkv, g_out)

    o_qkv = o_qkv.astype(F32)
    gain_out = o_qkv[0, 0, rows]
    grad_qkv = o_qkv[:, :, :rows].transpose(2, 0, 1, 3).reshape(rows, -1)
    grad_w_out = o_out.astype(F32).reshape(-1, width)

    def whole(part):
        part = part.reshape(4, 2, rows, 8, PART).transpose(2, 3, 1, 0, 4)
        return part.reshape(rows, 16, 4 * PART)[..., :block].reshape(rows, units).astype(F32)

    grad_w_down = o_down.reshape(4, 128, width)[:, :PART].reshape(-1, width)[:block].astype(F32)
    cuts = [0] + [piece * k for k in range(1, 5)] + [at + piece_h, at + 2 * piece_h]
    gain_outs = [gain_out[a:b] for a, b in zip(cuts[:-1], cuts[1:])]
    return (
        layer_out,
        grad_tokens,
        grad_qkv[:, :out_width],
        grad_qkv[:, out_width : out_width + head_dim],
        grad_qkv[:, out_width + head_dim :],
        grad_w_out,
        whole(o_in[:, 0]),
        whole(o_in[:, 1]),
        grad_w_down,
        *gain_outs,
    )


def solution(mesh):
    tokens = P(("dp", "fsdp", "seq"), None)
    weight, gain = P("fsdp", None), P("fsdp")
    return jax.shard_map(
        body,
        mesh=mesh,
        in_specs=(tokens,) + (weight,) * 7 + (gain,) * 6 + (tokens,),
        out_specs=(tokens,) * 2 + (weight,) * 7 + (gain,) * 6,
        check_vma=False,
    )
```

time: 1140 us -> 467 us (0.41)
  waiting for transfers between devices: 689 us -> 5.41 us
  Pallas kernels: 0 us -> 323 us
  blocking collectives: 211 us -> 0 us
  matrix products: 133 us -> 25 us
  local copies, waits for them, and re-layouts: 23.6 us -> 68.1 us
  other arithmetic: 62.1 us -> 32.9 us
  between operations: 16.7 us -> 1.78 us
    pallas_call x0 -> x3, Pallas kernels: none -> 323 us  [the longest x1 123 us: mlp_block(): pl.pallas_call(mlp_kernel, out_shape=(shape((n, width), BF16), shape((n,...]
    unnamed x11 -> x0, waiting for transfers between devices: 261 us -> none
    all_gather x5 -> x0, waiting for transfers between devices: 238 us -> none  [the longest x1 92.4 us: body(): lax.all_gather(w_down, 'fsdp', axis=0, tiled=True)]
    reduce_scatter x3 -> x0, waiting for transfers between devices: 117 us -> none  [the longest x1 117 us: body(): lax.psum_scatter(jnp.concatenate([top_part, bottom_part], axis=1).reshape...]
    dot_general x23 -> x10, matrix products: 130 us -> 22.4 us  [the longest x6 15.9 us: dot(): return lax.dot_general(a, b, dims, preferred_element_type=F32)]
    psum x1 -> x0, blocking collectives: 74.9 us -> none  [body(): lax.psum((grad_gain_a, grad_gain_b, grad_gain_c, grad_gain_d, grad_query_...]
    psum x1 -> x0, waiting for transfers between devices: 73.2 us -> none  [body(): lax.psum(in_piece, ('dp', 'seq')).astype(jnp.float32)]
    unnamed x1 -> x0, blocking collectives: 71.3 us -> none
  transfers between devices with their start and end apart: 10 -> 2, of which waited for: 6 -> 1; matrix products, arithmetic and copies ran while one was open for 11% -> 3% of each run, Pallas kernels for 0% -> 0%
where the time goes in v1:
time: 467 us; the launch traced here: 458 us
  Pallas kernels  323 us (69%)
  local copies, waits for them, and re-layouts  68.1 us (15%)
  other arithmetic  32.9 us (7%)
  matrix products  25 us (5%)
  waiting for transfers between devices  5.41 us (1%)
    pallas_call x1, Pallas kernels, mlp_block(): pl.pallas_call(mlp_kernel, out_shape=(shape((n, width), BF16), shape((n,...  123 us
    pallas_call x1, Pallas kernels, reduce_block(): pl.pallas_call(reduce_kernel, out_shape=(shape(4, 2, 2, *p_in), shape(4,...  122 us
    pallas_call x1, Pallas kernels, gather_block(): pl.pallas_call(gather_kernel, out_shape=(shape(4, 2, 2, 2, 2, *piece(own_...  77.6 us
    dot_general x6, matrix products, dot(): return lax.dot_general(a, b, dims, preferred_element_type=F32)  15.9 us
    unnamed x96, local copies, waits for them, and re-layouts  9.49 us
  transfers between devices with their start and end apart: 2, of which 1 were waited for; matrix products, arithmetic and copies ran while one was open for 3% of the time, Pallas kernels for 0%

profile of v1, /device:TPU:0, one launch (start us, length us, event | category | flops | bytes accessed | tf_op | source)
XLA Modules:
  0.0 457.9 jit_solution(16881174870707178712)
XLA Ops:
  1.2 4.1 concatenate.41
  5.3 1.1 fusion.33
  7.2 0.7 pad.48
  7.9 2.5 reshape.429
  10.7 1.0 copy-done.28
  11.7 2.5 reshape.430
  15.3 0.8 pad_maximum_fusion.3.own_in
  16.1 77.6 %gather_weights.1 = (bf16[4,2,2,2,2,80,384]{6,5,4,3,2,1,0:T(8,128)(2,1)}, bf16[4,2,2,2,2,16,1152]{6,5,4,3,2,1,0:T(8,128)(2,1)}, bf16[4,2,2,2,72,896]{5,4,3,2,1,0:T(8,128)(2,1)}, bf16[4,2,2,2,32,1152]{5,4,3,2,1,0:T(8,128)(2,1)}) custom-call(bf16[2,2,80,384]{3,2,1,0:T(8,128)(2,1)} %bitcast.156, bf16[2,2,16,1152]{3,2,1,0:T(8,128)(2,1)} %bitcast.162, ...), custom_call_target="tpu_custom_call" | custom-call | tf_op jit(solution)/shard_map/gather_weights/pallas_call | solution.py:373
  93.8 1.6 convert_reduce_fusion
  95.3 2.4 slice.152
  97.7 1.4 reshape.457
  99.1 1.4 slice_add_fusion.1
  100.5 1.5 fusion.78
  102.0 1.3 fusion.15
  103.9 1.4 copy.165
  105.3 2.5 copy.207
  107.9 3.2 fusion.44
  112.9 0.9 collective-permute-start
  114.3 1.3 slice.204
  116.9 4.9 %fusion.75 = (bf16[1,4,2,2,72,896]{5,4,3,0,2,1:T(8,128)(2,1)}, bf16[1,4,2,2,72,896]{5,4,3,0,2,1:T(8,128)(2,1)}) fusion(bf16[2,4,2,2,72,896]{5,4,3,0,2,1:T(8,128)(2,1)} %bitcast.146), kind=kLoop, calls=%fused_computation.168 | loop fusion | bytes 8257536 | tf_op jit(solution)/shard_map/slice | solution.py:681
  124.9 3.5 slice.213
  128.4 1.0 broadcast_select_fusion
  129.5 2.1 fusion.79
  131.6 2.2 convolution_convert_fusion.4
  133.9 1.0 multiply_reduce_fusion.3
  135.3 1.1 multiply_convert_fusion.own_x
  136.5 122.9 %mlp_block.1 = (bf16[256,1152]{1,0:T(8,128)(2,1)}, f32[256,1152]{1,0:T(8,128)}, f32[1,1152]{1,0:T(1,128)}, f32[1,1152]{1,0:T(1,128)}, bf16[4,2,2,2,72,896]{5,4,3...) custom-call(bf16[256,1152]{1,0:T(8,128)(2,1)} %multiply_convert_fusion.own_x, f32[256,1152]{1,0:T(8,128)} %copy-done.6, ...), custom_call_target="tpu_custom_call" | custom-call | tf_op jit(solution)/shard_map/mlp_block/pallas_call | solution.py:290
  259.4 2.0 multiply_reduce_fusion
  262.0 1.2 copy-done.15
  263.2 2.1 convolution_convert_fusion.3
  265.3 2.2 convolution_convert_fusion.1
  267.5 2.0 copy.206
  269.6 2.4 convolution_bitcast_fusion
  272.9 0.7 copy-done.11
  274.1 1.4 fusion.9
  275.9 1.3 multiply_add_fusion.1
  277.3 0.8 copy-done.8
  278.5 1.2 select_convert_fusion
  279.7 1.4 collective-permute-start.1
  281.0 1.0 fusion.17
  282.1 5.4 %collective-permute-done.1 = bf16[256,512]{1,0:T(8,128)(2,1)S(1)} collective-permute-done((bf16[256,512]{1,0:T(8,128)(2,1)S(1)}, bf16[256,512]{1,0:T(8,128)(2,1)S(1)}, u32[]{:S(2)}, u32[]{:S(2)}) %collective-permute-start.1) | collective-permute-done | bytes 262176 | tf_op jit(solution)/shard_map/ppermute | solution.py:576
  288.2 1.1 fusion.31
  289.3 1.1 fusion.53
  290.7 4.4 fusion.11
  295.0 3.1 convolution_convert_fusion
  298.5 1.1 copy.186
  299.7 7.1 %concatenate.49 = bf16[4,2,2,72,2,2,384]{6,5,4,3,2,1,0:T(2,128)(2,1)S(1)} reshape(bf16[1152,1536]{1,0:T(8,128)(2,1)} %convolution_convert_fusion) | data formatting | bytes 7077888 | tf_op jit(solution)/shard_map/concatenate | solution.py:722
  307.8 2.4 maximum_bitcast_fusion.g_qkv
  310.2 122.0 %reduce_grads.1 = (bf16[4,2,2,72,896]{4,3,2,1,0:T(8,128)(2,1)}, bf16[4,2,2,32,1152]{4,3,2,1,0:T(8,128)(2,1)}, bf16[2,2,80,384]{3,2,1,0:T(8,128)(2,1)}, bf16[2,2,16,1152]{3,2,1,0:T(8,128)(2,1)}) custom-call(bf16[4,2,2,2,72,896]{5,4,3,2,1,0:T(8,128)(2,1)} %get-tuple-element.35.g_in, bf16[4,2,2,2,32,1152]{5,4,3,2,1,0:T(8,128)(2,1)} %get-tuple-element.36.g_down, ...), custom_call_target="tpu_custom_call" | custom-call | tf_op jit(solution)/shard_map/reduce_grads/pallas_call | solution.py:533
  432.2 1.0 convert_element_type.144
  436.4 0.7 bitcast_convert_fusion
  437.3 1.4 slice_convert_fusion.2
  438.7 0.9 copy-done.20
  439.6 1.1 fusion.76
  440.7 1.4 reshape_squeeze.8
  442.1 1.5 copy.211
  443.6 0.7 reshape.454
  444.7 2.6 reshape.462
  447.4 1.6 reshape_squeeze.7
  448.9 1.5 copy.212
  450.5 0.7 reshape.453
  451.6 2.6 reshape.461
  454.2 2.7 fusion.14
  456.9 0.8 copy.215
  (169 shorter events, 19.4 us)
Async XLA Ops:
  0.6 6.5 %copy-start.26 = (bf16[432,1152]{1,0:T(8,128)(2,1)S(1)}, bf16[432,1152]{1,0:T(8,128)(2,1)}, u32[]{:S(2)}) copy-start(bf16[432,1152]{1,0:T(8,128)(2,1)} %param.22) | copy-start | bytes 2985988
  5.3 2.6 copy-start.27
  10.5 1.2 copy-start.28
  103.3 2.0 copy-start.40
  105.3 2.5 copy-start.37
  105.3 2.6 copy-start.7
  105.3 2.6 copy-start.45
  107.9 3.4 copy-start.39
  107.9 3.6 copy-start.42
  111.2 2.6 copy-start.13
  112.9 15.5 %collective-permute-start = (bf16[256,512]{1,0:T(8,128)(2,1)}, bf16[256,512]{1,0:T(8,128)(2,1)}, u32[]{:S(2)}, u32[]{:S(2)}) collective-permute-start(bf16[256,512]{1,0:T(8,128)(2,1)} %pad_maximum_fusion.7), channel_id=1, source_target_pairs={{0,1},{1,0},{2,3},{3,2},{4,5},{5,4},{6,7},{7,6},{8,9},{9,8},{10,11... | collective-permute-start | bytes 786440 | tf_op jit(solution)/shard_map/ppermute | solution.py:576
  116.9 5.0 %copy-start.2 = (f32[256,4,256]{0,2,1:T(8,128)}, f32[256,4,256]{0,2,1:T(8,128)S(1)}, u32[]{:S(2)}) copy-start(f32[256,4,256]{0,2,1:T(8,128)S(1)} %copy.167) | copy-start | bytes 3145732
  116.9 4.9 %copy-start.38 = (f32[16,16]{1,0:T(8,128)S(1)}, f32[16,16]{1,0:T(8,128)}, u32[]{:S(2)}) copy-start(f32[16,16]{1,0:T(8,128)} %get-tuple-element.82) | copy-start | bytes 3076
  122.3 0.7 copy-start.36
  122.3 1.4 copy-start.35
  122.3 2.1 copy-start.34
  124.9 4.6 %copy-start.10 = (f32[256,4,256]{2,0,1:T(8,128)}, f32[256,4,256]{2,0,1:T(8,128)S(1)}, u32[]{:S(2)}) copy-start(f32[256,4,256]{2,0,1:T(8,128)S(1)} %copy.168) | copy-start | bytes 3145732
  129.5 2.1 copy-start.22
  129.5 2.1 copy-start.24
  131.6 2.3 copy-start.14
  133.9 1.0 copy-start.18
  134.9 1.6 copy-start
  135.3 1.2 copy-start.6
  259.4 2.1 copy-start.1
  259.4 2.3 copy-start.4
  261.5 1.7 copy-start.15
  263.2 2.1 copy-start.19
  265.3 4.3 copy-start.16
  269.6 2.4 copy-start.23
  269.6 2.4 copy-start.25
  269.6 2.4 copy-start.32
  272.4 1.2 copy-start.11
  274.1 1.5 copy-start.44
  274.1 1.6 copy-start.43
  275.6 2.5 copy-start.3
  277.3 0.8 copy-start.8
  278.5 2.6 copy-start.9
  279.6 7.8 %copy-start.17 = (f32[512,256]{1,0:T(8,128)S(1)}, f32[512,256]{1,0:T(8,128)}, u32[]{:S(2)}) copy-start(f32[512,256]{1,0:T(8,128)} %convolution_bitcast_fusion) | copy-start | bytes 1572868
  279.7 7.8 %collective-permute-start.1 = (bf16[256,512]{1,0:T(8,128)(2,1)S(1)}, bf16[256,512]{1,0:T(8,128)(2,1)S(1)}, u32[]{:S(2)}, u32[]{:S(2)}) collective-permute-start(bf16[256,512]{1,0:T(8,128)(2,1)S(1)} %select_convert_fusion), channel_id=1, source_target_pairs={{0,1},{1,0},{2,3},{3,2},{4,5},{5,4},{6,7},{7,6},{8,9},{9,8},{10,11... | collective-permute-start | bytes 786440 | tf_op jit(solution)/shard_map/ppermute | solution.py:576
  287.6 3.1 copy-start.31
  306.8 1.0 copy-start.21
  434.4 2.0 copy-start.41
  434.4 2.1 copy-start.33
  434.4 2.8 copy-start.29
  437.3 2.3 copy-start.20
  444.7 2.7 copy-start.12
  451.6 2.7 copy-start.5
  451.6 2.7 copy-start.46
  454.2 2.7 copy-start.30

commit v2 on v1

--- a/solution.py
+++ b/solution.py
@@ -339,58 +339,142 @@
     return last
 
 
-def gather_kernel(
-    own_qkv, own_out, own_in, own_down, full_qkv, full_out, full_in, full_down,
-    chip_in, send, recv, local,
+def head_forward(pre, scale, cosine, sine, factor):
+    r = lax.rsqrt(jnp.mean(pre * pre, axis=-1, keepdims=True) + EPS)
+    v = pre * r * (1.0 + scale)
+    half = v.shape[1] // 2
+    a, b = v[:, :half], v[:, half:]
+    turned = jnp.concatenate([a * cosine - b * sine, b * cosine + a * sine], axis=1)
+    return (turned * factor).astype(BF16)
+
+
+def head_backward(grad, pre, scale, cosine, sine, factor):
+    grad = grad * factor
+    half = grad.shape[1] // 2
+    a, b = grad[:, :half], grad[:, half:]
+    dy = jnp.concatenate([a * cosine + b * sine, b * cosine - a * sine], axis=1)
+    r, out = norm_back(pre, dy * (1.0 + scale), pre.shape[1])
+    return out.astype(BF16), jnp.sum(dy * pre * r, axis=0, keepdims=True)
+
+
+def attend_kernel(
+    tokens, cosine, sine, own_qkv, own_out, own_in, own_down,
+    full_in, full_down, w_qkv, w_out, gains, normed, queries, kv, probs, context, attended, qkv_pre,
+    middle, mlp_in,
+    full_qkv, chip_in, send, recv, local,
 ):
     here = Place()
     greet([here.mate()] + plane_peers(here))
     lines = Lines(send, recv)
-    c = here.c
+    c, yl = here.c, here.yl
+    n, width = tokens.shape
+    head_dim = 2 * cosine.shape[1]
+    heads = queries.shape[1] // head_dim
+    rows = width // 16
     across = lines.copy(own_in.at[1 - c], chip_in.at[:, c], here.mate())
-    keep = pltpu.make_async_copy(own_in.at[c], chip_in.at[:, c], local.at[4])
-    keep.start()
-    attn = [(own_qkv, full_qkv.at[:, :, c]), (own_out, full_out.at[:, :, c])]
-    hops = plane_gather_first(here, lines, local, attn)
-    keep.wait()
+    qkv, out = (own_qkv, full_qkv.at[:, :, c]), (own_out, w_out.at[:, :, c])
+    mlp = [(chip_in, full_in), (own_down, full_down)]
+    hops = plane_gather_first(here, lines, local, [qkv, out])
+    chip_in[:, c] = own_in[c]
+    x = tokens[...].astype(F32)
+    lean = x * lax.rsqrt(jnp.mean(x * x, axis=-1, keepdims=True) + EPS)
+    last_qkv = plane_gather_second(here, lines, [qkv], hops[:1])
+    last_out = plane_gather_second(here, lines, [out], hops[1:])
     across.wait_recv()
-    mlp = [(chip_in, full_in), (own_down, full_down)]
-    last = plane_gather_second(here, lines, attn, hops)
     hops = plane_gather_first(here, lines, local, mlp)
-    for made in last:
+    for made in last_qkv:
         made.wait_recv()
-    cores = [lines.copy(full.at[:, :, c], full.at[:, :, c], here.mate()) for full in (full_qkv, full_out)]
-    last = plane_gather_second(here, lines, mlp, hops)
-    for made in last + cores:
+    core_qkv = lines.copy(full_qkv.at[:, :, c], full_qkv.at[:, :, c], here.mate())
+    last_in = plane_gather_second(here, lines, mlp[:1], hops[:1])
+    last_down = plane_gather_second(here, lines, mlp[1:], hops[1:])
+    core_qkv.wait_recv()
+    for p in range(4):
+        total = jnp.zeros((8, full_qkv.shape[-1]), F32)
+        cols = slice(p * full_qkv.shape[-1], (p + 1) * full_qkv.shape[-1])
+        for f in range(16):
+            part = full_qkv[f // 4, (f // 2) % 2, f % 2, p // 2, p % 2]
+            w_qkv[rows * f : rows * f + rows, cols] = part[:rows]
+            total = total + part.astype(F32)[rows : rows + 8]
+        gains[:, cols] = total
+    normed[...] = (lean * (1.0 + gains[0:1, :width])).astype(BF16)
+    qkv_pre[...] = dot(normed[...], w_qkv[...])
+    cos_v, sin_v = cosine[...], sine[...]
+    q_scale, k_scale = (gains[k : k + 1, width : width + head_dim] for k in (0, 1))
+    at = heads * head_dim
+    key = head_forward(qkv_pre[:, at : at + head_dim], k_scale, cos_v, sin_v, 1.0)
+    kv[yl, :, :head_dim] = key
+    kv[yl, :, head_dim:] = qkv_pre[:, at + head_dim :].astype(BF16)
+    kv_sent = lines.copy(kv.at[yl], kv.at[yl], here.pair())
+    for h in range(heads):
+        cols = slice(h * head_dim, (h + 1) * head_dim)
+        queries[:, cols] = head_forward(qkv_pre[:, cols], q_scale, cos_v, sin_v, head_dim**-0.5)
+    for made in last_out:
+        made.wait_recv()
+    core_out = lines.copy(w_out.at[:, :, c], w_out.at[:, :, c], here.mate())
+    kv_sent.wait_recv()
+    keys = kv[:, :, :head_dim].reshape(2 * n, head_dim)
+    values = kv[:, :, head_dim:].reshape(2 * n, head_dim)
+    row = lax.broadcasted_iota(jnp.int32, (n, 2 * n), 0) + yl * n
+    allowed = lax.broadcasted_iota(jnp.int32, (n, 2 * n), 1) <= row
+    for h in range(heads):
+        cols = slice(h * head_dim, (h + 1) * head_dim)
+        scores = jnp.where(allowed, dot(queries[:, cols], keys, NT), -1e30)
+        terms = jnp.exp(scores - jnp.max(scores, axis=-1, keepdims=True))
+        low = (terms * (1.0 / jnp.sum(terms, axis=-1, keepdims=True))).astype(BF16)
+        probs[h] = low
+        context[:, cols] = dot(low, values).astype(BF16)
+    core_out.wait_recv()
+    att = dot(context[...], w_out[...].reshape(heads * head_dim, width))
+    attended[...] = att
+    r = lax.rsqrt(jnp.mean(att * att, axis=-1, keepdims=True) + EPS)
+    mid = x + att * r * (1.0 + gains[1:2, :width])
+    middle[...] = mid
+    r = lax.rsqrt(jnp.mean(mid * mid, axis=-1, keepdims=True) + EPS)
+    mlp_in[...] = (mid * r * (1.0 + gains[2:3, :width])).astype(BF16)
+    for made in last_in + last_down:
         made.wait_recv()
     lines.drain()
 
 
-def gather_block(own_qkv, own_out, own_in, own_down):
-    hbm = pl.BlockSpec(memory_space=pl.ANY)
-    shape = lambda *s: jax.ShapeDtypeStruct(s, BF16)
-    piece = lambda a: a.shape[2:]
+def attend_block(tokens, cosine, sine, own_qkv, own_out, own_in, own_down):
+    n, width = tokens.shape
+    vmem, hbm = pl.BlockSpec(memory_space=pltpu.VMEM), pl.BlockSpec(memory_space=pl.ANY)
+    shape = jax.ShapeDtypeStruct
+    p_qkv, p_out, p_in, p_down = own_qkv.shape[2:], own_out.shape[2:], own_in.shape[2:], own_down.shape[2:]
+    cols, head_dim = 4 * p_qkv[1], 2 * cosine.shape[1]
+    out_width = cols - 2 * head_dim
     return pl.pallas_call(
-        gather_kernel,
+        attend_kernel,
         out_shape=(
-            shape(4, 2, 2, 2, 2, *piece(own_qkv)),
-            shape(4, 2, 2, 2, 2, *piece(own_out)),
-            shape(4, 2, 2, 2, *own_in.shape[2:]),
-            shape(4, 2, 2, 2, *piece(own_down)),
+            shape((4, 2, 2, 2, *p_in), BF16),
+            shape((4, 2, 2, 2, *p_down), BF16),
+            shape((width, cols), BF16),
+            shape((4, 2, 2, 2, 2, *p_out), BF16),
+            shape((8, cols), F32),
+            shape((n, width), BF16),
+            shape((n, out_width), BF16),
+            shape((2, n, 2 * head_dim), BF16),
+            shape((out_width // head_dim, n, 2 * n), BF16),
+            shape((n, out_width), BF16),
+            shape((n, width), F32),
+            shape((n, cols), F32),
+            shape((n, width), F32),
+            shape((n, width), BF16),
         ),
-        in_specs=[hbm] * 4,
-        out_specs=(hbm,) * 4,
+        in_specs=[vmem] * 7,
+        out_specs=(hbm,) * 2 + (vmem,) * 12,
         scratch_shapes=[
+            pltpu.VMEM((4, 2, 2, 2, 2, *p_qkv), BF16),
             pltpu.VMEM(own_in.shape, BF16),
-            pltpu.SemaphoreType.DMA((51,)),
-            pltpu.SemaphoreType.DMA((51,)),
-            pltpu.SemaphoreType.DMA((5,)),
+            pltpu.SemaphoreType.DMA((52,)),
+            pltpu.SemaphoreType.DMA((52,)),
+            pltpu.SemaphoreType.DMA((2,)),
         ],
         compiler_params=pltpu.CompilerParams(
             collective_id=0, has_side_effects=True, vmem_limit_bytes=60 * MIB
         ),
-        name="gather_weights",
-    )(own_qkv, own_out, own_in, own_down)
+        name="attend",
+    )(tokens, cosine, sine, own_qkv, own_out, own_in, own_down)
 
 
 class PlaneSum:
@@ -452,8 +536,11 @@
         return total
 
 
-def reduce_kernel(
-    g_in, g_down, g_qkv, g_out, o_in, o_down, o_qkv, o_out,
+def retreat_kernel(
+    middle_grad, attended, context, probs, kv, queries, qkv_pre, normed, tokens, cosine, sine,
+    w_qkv, w_out, gains, d_gain_in, d_gain_out, g_in, g_down,
+    grad_tokens, o_in, o_down, o_qkv, o_out,
+    context_grad, attn_side, kv_part, kv_give, kv_land, g_qkv, g_out, d_gains,
     chip_qkv, chip_out, cross_qkv, cross_out, swap, half_qkv, half_out, land_qkv, land_out, *rest,
 ):
     here = Place()
@@ -462,27 +549,93 @@
     greet([here.mate()] + plane_peers(here) + [here.to(dx=d) for d in (1, 2, 3)])
     lines = Lines(send, recv)
     copy = lines.copy
-    cross = [
-        copy(g.at[:, :, 1 - c], land, here.mate()) for g, land in ((g_qkv, cross_qkv), (g_out, cross_out))
-    ]
+    n, width = middle_grad.shape
+    head_dim = 2 * cosine.shape[1]
+    heads = queries.shape[1] // head_dim
+    rows = width // 16
+    at = heads * head_dim
     sums = [
         PlaneSum(here, lines, g, *rest[6 * k : 6 * k + 6])
         for k, g in enumerate((g_in, g_down, chip_qkv, chip_out))
     ]
     sums[0].first()
     sums[1].first()
-    for made, g, land, chip in (
-        (cross[0], g_qkv, cross_qkv, chip_qkv),
-        (cross[1], g_out, cross_out, chip_out),
-    ):
-        made.wait_recv()
-        for z in range(4):
-            for yh in range(2):
-                chip[z, yh] = (g[z, yh, c].astype(F32) + land[z, yh].astype(F32)).astype(BF16)
-    sums[2].first()
+
+    att, dy = attended[...], middle_grad[...]
+    r, grad = norm_back(att, dy * (1.0 + gains[1:2, :width]), width)
+    d_gains[...] = jnp.zeros_like(d_gains)
+    d_gains[1:2, :width] = jnp.sum(dy * att * r, axis=0, keepdims=True)
+    d_gains[2:3, :width] = d_gain_in[...]
+    d_gains[3:4, :width] = d_gain_out[...]
+    attended_grad = grad.astype(BF16)
+    out_full = w_out[...].reshape(at, width)
+    context_grad[...] = dot(attended_grad, out_full, NT).astype(BF16)
+    grad_out = dot(context[...], attended_grad, TN)
+    g_out[...] = grad_out.astype(BF16).reshape(g_out.shape)
+    give_out = copy(g_out.at[:, :, 1 - c], cross_out, here.mate())
+
+    keys = kv[:, :, :head_dim].reshape(2 * n, head_dim)
+    values = kv[:, :, head_dim:].reshape(2 * n, head_dim)
+    cos_v, sin_v = cosine[...], sine[...]
+    q_scale, k_scale = (gains[k : k + 1, width : width + head_dim] for k in (0, 1))
+    d_query = jnp.zeros((1, head_dim), F32)
+    for h in range(heads):
+        cols = slice(h * head_dim, (h + 1) * head_dim)
+        low = probs[h]
+        high = low.astype(F32)
+        prob_grad = dot(context_grad[:, cols], values, NT)
+        inner = jnp.sum(high * prob_grad, axis=-1, keepdims=True)
+        score_grad = (high * (prob_grad - inner)).astype(BF16)
+        key_part = dot(score_grad, queries[:, cols], TN)
+        value_part = dot(low, context_grad[:, cols], TN)
+        if h == 0:
+            kv_part[:, :, :head_dim] = key_part.reshape(2, n, head_dim)
+            kv_part[:, :, head_dim:] = value_part.reshape(2, n, head_dim)
+        else:
+            kv_part[:, :, :head_dim] += key_part.reshape(2, n, head_dim)
+            kv_part[:, :, head_dim:] += value_part.reshape(2, n, head_dim)
+        query_grad = dot(score_grad, keys).astype(BF16).astype(F32)
+        side, d_scale = head_backward(
+            query_grad, qkv_pre[:, cols], q_scale, cos_v, sin_v, head_dim**-0.5
+        )
+        attn_side[:, cols] = side
+        d_query = d_query + d_scale
+    kv_give[...] = kv_part[1 - yl].astype(BF16)
+    kv_sent = copy(kv_give, kv_land, here.pair())
+    sums[0].second()
+    sums[1].second()
+    kv_sent.wait_recv()
+    kv_grad = (kv_part[yl] + kv_land[...].astype(F32)).astype(BF16)
+    side, d_key = head_backward(
+        kv_grad[:, :head_dim].astype(F32), qkv_pre[:, at : at + head_dim], k_scale, cos_v, sin_v, 1.0
+    )
+    attn_side[:, at : at + head_dim] = side
+    attn_side[:, at + head_dim :] = kv_grad[:, head_dim:]
+    d_gains[0:1, width : width + head_dim] = d_query
+    d_gains[1:2, width : width + head_dim] = d_key
+
+    give_out.wait_recv()
+    for z in range(4):
+        for yh in range(2):
+            chip_out[z, yh] = (g_out[z, yh, c].astype(F32) + cross_out[z, yh].astype(F32)).astype(BF16)
     sums[3].first()
-    for part in sums:
-        part.second()
+
+    normed_grad = dot(attn_side[...], w_qkv[...], NT)
+    tok = tokens[...].astype(F32)
+    r, grad = norm_back(tok, normed_grad * (1.0 + gains[0:1, :width]), width)
+    grad_tokens[...] = (middle_grad[...] + grad).astype(BF16)
+    d_gains[0:1, :width] = jnp.sum(normed_grad * tok * r, axis=0, keepdims=True)
+    grad_qkv = dot(normed[...], attn_side[...], TN)
+    for p in range(4):
+        cols = slice(p * g_qkv.shape[-1], (p + 1) * g_qkv.shape[-1])
+        tail = d_gains[:, cols].astype(BF16)
+        for f in range(16):
+            spot = (f // 4, (f // 2) % 2, f % 2, p // 2, p % 2)
+            block = jnp.concatenate(
+                [grad_qkv[rows * f : rows * f + rows, cols], d_gains[:, cols]], axis=0
+            )
+            g_qkv[spot] = block.astype(BF16)
+    give_qkv = copy(g_qkv.at[:, :, 1 - c], cross_qkv, here.mate())
 
     swap[0] = sums[0].result(0).astype(BF16)
     swap[1] = sums[0].result(1).astype(BF16)
@@ -493,19 +646,27 @@
     to_pair = [copy(o_down.at[x, yl], o_down.at[x, yl], here.pair())]
     across.wait_recv()
     to_pair.append(copy(o_in.at[x, yl], o_in.at[x, yl], here.pair()))
-    for path in (0, 1):
-        half_qkv[path] = sums[2].result(path).astype(BF16)
-        half_out[path] = sums[3].result(path).astype(BF16)
-    by_x = []
-    for d in (1, 3, 2):
-        by_x.append(copy(half_qkv, land_qkv.at[d - 1], here.to(dx=d)))
-        by_x.append(copy(half_out, land_out.at[d - 1], here.to(dx=d)))
+
+    give_qkv.wait_recv()
+    for z in range(4):
+        for yh in range(2):
+            chip_qkv[z, yh] = (g_qkv[z, yh, c].astype(F32) + cross_qkv[z, yh].astype(F32)).astype(BF16)
+    sums[2].first()
     for made in to_pair:
         made.wait_recv()
     spread = []
     for d in (1, 3, 2):
         spread.append(copy(o_in.at[x], o_in.at[x], here.to(dx=d)))
         spread.append(copy(o_down.at[x], o_down.at[x], here.to(dx=d)))
+    sums[3].second()
+    sums[2].second()
+    for path in (0, 1):
+        half_out[path] = sums[3].result(path).astype(BF16)
+        half_qkv[path] = sums[2].result(path).astype(BF16)
+    by_x = []
+    for d in (1, 3, 2):
+        by_x.append(copy(half_qkv, land_qkv.at[d - 1], here.to(dx=d)))
+        by_x.append(copy(half_out, land_out.at[d - 1], here.to(dx=d)))
     for made in by_x:
         made.wait_recv()
     for half, land, out in ((half_qkv, land_qkv, o_qkv), (half_out, land_out, o_out)):
@@ -520,60 +681,42 @@
     lines.drain()
 
 
-def reduce_block(g_in, g_down, g_qkv, g_out):
+def retreat_block(*args):
     vmem = pl.BlockSpec(memory_space=pltpu.VMEM)
-    shape = lambda *s: jax.ShapeDtypeStruct(s, BF16)
-    p_in, p_down, p_qkv, p_out = g_in.shape[4:], g_down.shape[4:], g_qkv.shape[5:], g_out.shape[5:]
+    shape = jax.ShapeDtypeStruct
+    n, width = args[0].shape
+    out_width, head_dim = args[5].shape[1], 2 * args[9].shape[1]
+    cols = args[6].shape[1]
+    g_in, g_down, w_out = args[-2], args[-1], args[12]
+    p_in, p_down, p_out = g_in.shape[4:], g_down.shape[4:], w_out.shape[5:]
+    p_qkv = (width // 16 + 8, cols // 4)
     vm = lambda *s: pltpu.VMEM(s, BF16)
-    scratch = [vm(4, 2, 2, 2, *p_qkv), vm(4, 2, 2, 2, *p_out)] * 2
+    scratch = [vm(n, out_width), vm(n, cols), pltpu.VMEM((2, n, 2 * head_dim), F32)]
+    scratch += [vm(n, 2 * head_dim)] * 2
+    scratch += [vm(4, 2, 2, 2, 2, *p_qkv), vm(4, 2, 2, 2, 2, *p_out), pltpu.VMEM((8, cols), F32)]
+    scratch += [vm(4, 2, 2, 2, *p_qkv), vm(4, 2, 2, 2, *p_out)] * 2
     scratch += [vm(2, *p_in), vm(2, *p_qkv), vm(2, *p_out), vm(3, 2, *p_qkv), vm(3, 2, *p_out)]
     for piece in (p_in, p_down, p_qkv, p_out):
         scratch += PlaneSum.scratch(piece)
-    scratch += [pltpu.SemaphoreType.DMA((67,))] * 2
+    scratch += [pltpu.SemaphoreType.DMA((68,))] * 2
+    low = lambda *s: shape(s, BF16)
     return pl.pallas_call(
-        reduce_kernel,
+        retreat_kernel,
         out_shape=(
-            shape(4, 2, 2, *p_in),
-            shape(4, 2, 2, *p_down),
-            shape(2, 2, *p_qkv),
-            shape(2, 2, *p_out),
+            low(n, width),
+            low(4, 2, 2, *p_in),
+            low(4, 2, 2, *p_down),
+            low(2, 2, *p_qkv),
+            low(2, 2, *p_out),
         ),
-        in_specs=[vmem] * 4,
-        out_specs=(vmem,) * 4,
+        in_specs=[vmem] * len(args),
+        out_specs=(vmem,) * 5,
         scratch_shapes=scratch,
         compiler_params=pltpu.CompilerParams(
-            collective_id=2, has_side_effects=True, vmem_limit_bytes=60 * MIB
+            collective_id=2, has_side_effects=True, vmem_limit_bytes=63 * MIB
         ),
-        name="reduce_grads",
-    )(g_in, g_down, g_qkv, g_out)
-
-
-def rms_norm(values, scale_gain):
-    factor = lax.rsqrt(jnp.mean(values * values, axis=-1, keepdims=True) + EPS)
-    return values * factor * (1.0 + scale_gain)
-
-
-def rotate(values, positions):
-    half_dim = values.shape[-1] // 2
-    frequency = jnp.exp(
-        jnp.arange(half_dim, dtype=F32) * (-2.0 * math.log(1000000.0) / values.shape[-1])
-    )
-    angles = positions[:, None] * frequency[None, :]
-    cosine = jnp.cos(angles)[:, None, :]
-    sine_part = jnp.sin(angles)[:, None, :]
-    first_half = values[..., :half_dim]
-    second_half = values[..., half_dim:]
-    return jnp.concatenate(
-        [
-            first_half * cosine - second_half * sine_part,
-            second_half * cosine + first_half * sine_part,
-        ],
-        axis=-1,
-    )
-
-
-def swap_pair(value):
-    return lax.ppermute(value, "seq", [(0, 1), (1, 0)])
+        name="retreat",
+    )(*args)
 
 
 def body(
@@ -596,18 +739,25 @@
     n, width = tokens.shape
     rows = w_query.shape[0]
     head_dim = w_key.shape[1]
-    heads = w_query.shape[1] // head_dim
+    out_width = w_query.shape[1]
     units = w_gate.shape[1]
-    out_width = heads * head_dim
     block = units // 16
-    x_at = lax.axis_index("dp")
-    gains = (pre_attn_gain, post_attn_gain, pre_mlp_gain, post_mlp_gain, query_gain, key_gain)
-
+    x_at, shard = lax.axis_index("dp"), lax.axis_index("fsdp")
+
+    mine = jnp.arange(16) == shard
+    spread = lambda g: jnp.where(mine[:, None], g[None, :], 0).reshape(1, -1)
+    gains_d = [spread(g) for g in (pre_attn_gain, post_attn_gain, pre_mlp_gain, post_mlp_gain)]
+    gains_h = jnp.concatenate([spread(query_gain), spread(key_gain)], axis=0)
+    tail = jnp.concatenate(
+        [
+            jnp.pad(jnp.concatenate(gains_d, axis=0), ((0, 4), (0, 0))),
+            jnp.pad(gains_h, ((0, 6), (0, out_width + head_dim - width))),
+        ],
+        axis=1,
+    )
     qkv = jnp.concatenate([w_query, w_key, w_value], axis=1)
-    gain_row = jnp.concatenate(gains)
-    gain_row = jnp.pad(gain_row, (0, qkv.shape[1] - gain_row.shape[0]))[None, :]
-    qkv = jnp.concatenate([qkv, jnp.pad(gain_row, ((0, 7), (0, 0)))], axis=0)
-    own_qkv = qkv.reshape(rows + 8, 2, 2, -1).transpose(1, 2, 0, 3)
+    own_qkv = jnp.concatenate([qkv, tail], axis=0)
+    own_qkv = own_qkv.reshape(rows + 8, 2, 2, -1).transpose(1, 2, 0, 3)
     own_out = w_out.reshape(2, 2, -1, width)
 
     def columns(w):
@@ -620,123 +770,42 @@
     down = lax.dynamic_slice_in_dim(down, x_at * PART, PART, axis=0)
     own_down = jnp.pad(down, ((0, 128 - PART), (0, 0))).reshape(2, 2, 32, width)
 
-    full_qkv, full_out, full_in, full_down = gather_block(own_qkv, own_out, own_in, own_down)
-    gain_rows = full_qkv[:, :, :, 0, 0, rows, :].reshape(16, -1).astype(F32)
-    piece = width // 16
-    gain_set = [gain_rows[:, piece * k : piece * (k + 1)].reshape(1, -1) for k in range(4)]
-    piece_h = head_dim // 16
-    at = 4 * piece
-    gain_set += [
-        gain_rows[:, at + piece_h * k : at + piece_h * (k + 1)].reshape(-1) for k in range(2)
-    ]
-    attn_gain_in, attn_gain_out, mlp_gain_in, mlp_gain_out, query_scale, key_scale = gain_set
-    full_qkv = full_qkv[..., :rows, :].reshape(16, 4, rows, -1).transpose(0, 2, 1, 3)
-    full_qkv = full_qkv.reshape(width, out_width + 2 * head_dim)
-    full_out = full_out.reshape(out_width, width)
+    positions = (lax.axis_index("seq") * n + jnp.arange(n, dtype=jnp.int32)).astype(F32)
+    frequency = jnp.exp(
+        jnp.arange(head_dim // 2, dtype=F32) * (-2.0 * math.log(1000000.0) / head_dim)
+    )
+    angles = positions[:, None] * frequency[None, :]
+    cosine, sine = jnp.cos(angles), jnp.sin(angles)
+
+    (
+        full_in, full_down, w_qkv, w_out_full, gains, normed, queries, kv, probs, context, attended,
+        qkv_pre, middle, mlp_in,
+    ) = attend_block(tokens, cosine, sine, own_qkv, own_out, own_in, own_down)
     gate_up = full_in.transpose(2, 0, 1, 3, 4, 5).reshape(2, width, CORE_UNITS)
     full_down = full_down.reshape(8, 128, width)[:, :PART].reshape(CORE_UNITS, width)
 
-    seq_start = lax.axis_index("seq") * n
-    query_places = seq_start + jnp.arange(n, dtype=jnp.int32)
-    positions = query_places.astype(F32)
-    inputs = tokens.astype(F32)
-    normed_f, attn_in_pull = jax.vjp(rms_norm, inputs, attn_gain_in[0])
-    normed = normed_f.astype(BF16)
-    qkv_pre = dot(normed, full_qkv)
-    query_pre = qkv_pre[:, :out_width].reshape(n, heads, head_dim)
-    key_pre = qkv_pre[:, out_width : out_width + head_dim].reshape(n, 1, head_dim)
-    value_local = qkv_pre[:, out_width + head_dim :].astype(BF16)
-
-    def shape_heads(query_in, key_in, query_gain_f, key_gain_f):
-        query_out = rotate(rms_norm(query_in, query_gain_f), positions) * head_dim ** (-0.5)
-        key_out = rotate(rms_norm(key_in, key_gain_f), positions)
-        return (query_out, key_out)
-
-    (query_f, key_f), heads_pull = jax.vjp(shape_heads, query_pre, key_pre, query_scale, key_scale)
-    queries = query_f.astype(BF16)
-    kv_local = jnp.concatenate([key_f[:, 0, :].astype(BF16), value_local], axis=1)
-    kv_other = swap_pair(kv_local)
-    low_half = lax.axis_index("seq") == 0
-    kv = jnp.concatenate(
-        [jnp.where(low_half, kv_local, kv_other), jnp.where(low_half, kv_other, kv_local)], axis=0
+    layer_out, middle_grad, d_gain_in, d_gain_out, g_in, g_down = mlp_block(
+        mlp_in, middle, cotangent, gains[2:3, :width], gains[3:4, :width],
+        gate_up[0], gate_up[1], full_down,
     )
-    key_rows, value_rows = kv[:, :head_dim], kv[:, head_dim:]
-    seq_length = kv.shape[0]
-    allowed = jnp.arange(seq_length, dtype=jnp.int32)[None, :] <= query_places[:, None]
-    scores = jnp.einsum("ihd,jd->hij", queries, key_rows, preferred_element_type=F32)
-    scores = jnp.where(allowed[None, :, :], scores, -1e30)
-    row_peak = jnp.max(scores, axis=-1, keepdims=True)
-    exp_terms = jnp.exp(scores - row_peak)
-    row_total = jnp.sum(exp_terms, axis=-1, keepdims=True)
-    prob_rows = exp_terms / row_total
-    probs_bf = prob_rows.astype(BF16)
-    context = jnp.einsum("hij,jd->ihd", probs_bf, value_rows, preferred_element_type=F32)
-    context = context.astype(BF16).reshape(n, out_width)
-    attended = dot(context, full_out)
-    post_attn, attn_out_pull = jax.vjp(rms_norm, attended, attn_gain_out[0])
-    middle = inputs + post_attn
-    mlp_in = rms_norm(middle, mlp_gain_in[0]).astype(BF16)
-
-    layer_out, middle_grad, grad_gain_c, grad_gain_d, g_in, g_down = mlp_block(
-        mlp_in, middle, cotangent, mlp_gain_in, mlp_gain_out, gate_up[0], gate_up[1], full_down
+    grad_tokens, o_in, o_down, o_qkv, o_out = retreat_block(
+        middle_grad, attended, context, probs, kv, queries, qkv_pre, normed, tokens, cosine, sine,
+        w_qkv, w_out_full, gains, d_gain_in, d_gain_out, g_in, g_down,
     )
 
-    attended_grad_f, grad_gain_b = attn_out_pull(middle_grad)
-    attended_grad = attended_grad_f.astype(BF16)
-    context_grad = dot(attended_grad, full_out, NT).astype(BF16).reshape(n, heads, head_dim)
-    prob_grad = jnp.einsum("ihd,jd->hij", context_grad, value_rows, preferred_element_type=F32)
-    row_dot = jnp.sum(prob_rows * prob_grad, axis=-1, keepdims=True)
-    score_grad = (prob_rows * (prob_grad - row_dot)).astype(BF16)
-    query_grad = jnp.einsum("hij,jd->ihd", score_grad, key_rows, preferred_element_type=F32)
-    query_grad = query_grad.astype(BF16)
-    key_part = jnp.einsum("hij,ihd->jd", score_grad, queries, preferred_element_type=F32)
-    value_part = jnp.einsum("hij,ihd->jd", probs_bf, context_grad, preferred_element_type=F32)
-    kv_part = jnp.concatenate([key_part, value_part], axis=1)
-    kept = jnp.where(low_half, kv_part[:n], kv_part[n:])
-    given = jnp.where(low_half, kv_part[n:], kv_part[:n]).astype(BF16)
-    kv_grad = (kept + swap_pair(given).astype(F32)).astype(BF16)
-    key_grad, value_grad = kv_grad[:, :head_dim], kv_grad[:, head_dim:]
-    query_pre_grad, key_pre_grad, grad_query_scale, grad_key_scale = heads_pull(
-        (query_grad.astype(F32), key_grad.astype(F32)[:, None, :])
-    )
-    attn_side = jnp.concatenate(
-        [
-            query_pre_grad.astype(BF16).reshape(n, out_width),
-            key_pre_grad.reshape(n, head_dim).astype(BF16),
-            value_grad,
-        ],
-        axis=1,
-    )
-    normed_grad = dot(attn_side, full_qkv, NT)
-    input_part, grad_gain_a = attn_in_pull(normed_grad)
-    grad_tokens = (middle_grad + input_part).astype(BF16)
-
-    g_qkv = dot(normed, attn_side, TN).astype(BF16).reshape(16, rows, -1)
-    gain_grads = [
-        g.reshape(16, -1)
-        for g in (grad_gain_a, grad_gain_b, grad_gain_c, grad_gain_d, grad_query_scale, grad_key_scale)
-    ]
-    gain_grads = jnp.concatenate(gain_grads, axis=1).astype(BF16)
-    gain_grads = jnp.pad(gain_grads, ((0, 0), (0, g_qkv.shape[2] - gain_grads.shape[1])))
-    gain_grads = jnp.pad(gain_grads[:, None, :], ((0, 0), (0, 7), (0, 0)))
-    g_qkv = jnp.concatenate([g_qkv, gain_grads], axis=1)
-    g_qkv = g_qkv.reshape(4, 2, 2, rows + 8, 2, 2, -1).transpose(0, 1, 2, 4, 5, 3, 6)
-    g_out = dot(context, attended_grad, TN).astype(BF16).reshape(4, 2, 2, 2, 2, -1, width)
-
-    o_in, o_down, o_qkv, o_out = reduce_block(g_in, g_down, g_qkv, g_out)
-
     o_qkv = o_qkv.astype(F32)
-    gain_out = o_qkv[0, 0, rows]
     grad_qkv = o_qkv[:, :, :rows].transpose(2, 0, 1, 3).reshape(rows, -1)
+    tail = o_qkv[:, :, rows:].transpose(2, 0, 1, 3).reshape(8, -1)
     grad_w_out = o_out.astype(F32).reshape(-1, width)
+    gain_outs = [lax.dynamic_slice_in_dim(tail[k], shard * rows, rows) for k in range(4)]
+    piece = head_dim // 16
+    gain_outs += [lax.dynamic_slice_in_dim(tail[k], width + shard * piece, piece) for k in range(2)]
 
     def whole(part):
         part = part.reshape(4, 2, rows, 8, PART).transpose(2, 3, 1, 0, 4)
         return part.reshape(rows, 16, 4 * PART)[..., :block].reshape(rows, units).astype(F32)
 
     grad_w_down = o_down.reshape(4, 128, width)[:, :PART].reshape(-1, width)[:block].astype(F32)
-    cuts = [0] + [piece * k for k in range(1, 5)] + [at + piece_h, at + 2 * piece_h]
-    gain_outs = [gain_out[a:b] for a, b in zip(cuts[:-1], cuts[1:])]
     return (
         layer_out,
         grad_tokens,

time: 467 us -> 391 us (0.84)
  local copies, waits for them, and re-layouts: 68.1 us -> 39.8 us
  other arithmetic: 32.9 us -> 7.59 us
  matrix products: 25 us -> 0 us
  Pallas kernels: 323 us -> 337 us
  waiting for transfers between devices: 5.41 us -> 0 us
    dot_general x11 -> x0, matrix products: 22.9 us -> none  [the longest x6 15.9 us: dot(): return lax.dot_general(a, b, dims, preferred_element_type=F32)]
    pallas_call x2, Pallas kernels: 200 us -> 214 us  [the longest x1 127 us: retreat_block(): pl.pallas_call(retreat_kernel, out_shape=(low(n, width), low(4, 2, 2, *p_...]
    concatenate x7 -> x0, local copies, waits for them, and re-layouts: 13.3 us -> none  [the longest x4 8.79 us: body(): g_qkv = jnp.concatenate([g_qkv, gain_grads], axis=1)]
    convert_element_type x11 -> x1, other arithmetic: 9.54 us -> 0.01 us  [body(): (lax.axis_index('seq') * n + jnp.arange(n, dtype=jnp.int32)).astype(F32)]
    unnamed x96 -> x22, local copies, waits for them, and re-layouts: 9.49 us -> 2.68 us
    reduce_sum x7 -> x0, other arithmetic: 5.59 us -> none  [the longest x3 3.49 us: rms_norm(): return values * factor * (1.0 + scale_gain)]
    reshape x13 -> x2, local copies, waits for them, and re-layouts: 6.31 us -> 0.78 us  [body(): own_qkv = own_qkv.reshape(rows + 8, 2, 2, -1).transpose(1, 2, 0, 3)]
    ppermute x2 -> x0, waiting for transfers between devices: 5.41 us -> none  [swap_pair(): return lax.ppermute(value, 'seq', [(0, 1), (1, 0)])]
  transfers between devices with their start and end apart: 2 -> 0, of which waited for: 1 -> 0; matrix products, arithmetic and copies ran while one was open for 3% -> 0% of each run, Pallas kernels for 0% -> 0%
where the time goes in v2:
time: 391 us; the launch traced here: 386 us
  Pallas kernels  337 us (86%)
  local copies, waits for them, and re-layouts  39.8 us (10%)
  other arithmetic  7.59 us (2%)
    pallas_call x1, Pallas kernels, retreat_block(): pl.pallas_call(retreat_kernel, out_shape=(low(n, width), low(4, 2, 2, *p_...  127 us
    pallas_call x1, Pallas kernels, mlp_block(): pl.pallas_call(mlp_kernel, out_shape=(shape((n, width), BF16), shape((n,...  123 us
    pallas_call x1, Pallas kernels, attend_block(): pl.pallas_call(attend_kernel, out_shape=(shape((4, 2, 2, 2, *p_in), BF16)...  87.1 us

profile of v2, /device:TPU:0, one launch (start us, length us, event | category | flops | bytes accessed | tf_op | source)
XLA Modules:
  0.0 385.7 jit_solution(11752141421658475218)
XLA Ops:
  0.7 0.9 broadcast_select_fusion.5
  1.5 0.1 select_n.100
  1.6 0.1 select_n.102
  1.7 0.1 select_n.96
  1.8 0.1 select_n.98
  2.0 0.7 broadcast_select_fusion.1
  2.7 0.1 select_n.104
  2.8 0.1 select_n.106
  2.9 1.0 maximum_maximum_fusion
  3.9 0.1 reshape.256
  4.0 0.7 copy.43
  4.7 2.5 reshape.258
  7.2 0.0 copy-start.3
  7.2 0.2 copy.33
  7.4 1.0 copy-done.3
  8.4 2.5 reshape.259
  11.0 0.2 copy.34
  11.2 0.4 fusion
  11.6 0.0 copy-start.4
  11.6 0.2 stack_reshape.6
  11.8 0.2 stack_reshape.7
  12.1 0.8 pad_maximum_fusion.own_in
  12.9 0.0 copy-done.4
  13.0 0.7 pad.28
  13.7 1.2 multiply_sine_fusion
  14.9 87.1 %attend.1 = (bf16[4,2,2,2,72,896]{5,4,3,2,1,0:T(8,128)(2,1)}, bf16[4,2,2,2,32,1152]{5,4,3,2,1,0:T(8,128)(2,1)}, bf16[1152,1536]{1,0:T(8,128)(2,1)}, bf16[4,2,2,2...) custom-call(bf16[256,1152]{1,0:T(8,128)(2,1)} %tokens.3, ...), custom_call_target="tpu_custom_call" | custom-call | tf_op jit(solution)/shard_map/attend/pallas_call | solution.py:446
  102.0 1.4 fusion.18
  103.5 4.6 %fusion.15 = (bf16[1,4,2,2,72,896]{5,4,3,0,2,1:T(8,128)(2,1)}, bf16[1,4,2,2,72,896]{5,4,3,0,2,1:T(8,128)(2,1)}) fusion(bf16[2,4,2,2,72,896]{5,4,3,0,2,1:T(8,128)(2,1)} %bitcast.42), kind=kLoop, calls=%fused_computation.47 | loop fusion | bytes 8257536 | tf_op jit(solution)/shard_map/slice | solution.py:789
  108.1 1.5 slice.90
  109.6 122.6 %mlp_block.1 = (bf16[256,1152]{1,0:T(8,128)(2,1)}, f32[256,1152]{1,0:T(8,128)}, f32[1,1152]{1,0:T(1,128)}, f32[1,1152]{1,0:T(1,128)}, bf16[4,2,2,2,72,896]{5,4,3...) custom-call(bf16[256,1152]{1,0:T(8,128)(2,1)} %get-tuple-element.40.own_x, f32[256,1152]{1,0:T(8,128)} %get-tuple-element.41.middle, ...), custom_call_target="tpu_custom_call" | custom-call | tf_op jit(solution)/shard_map/mlp_block/pallas_call | solution.py:290
  232.2 127.2 %retreat.1 = (bf16[256,1152]{1,0:T(8,128)(2,1)}, bf16[4,2,2,72,896]{4,3,2,1,0:T(8,128)(2,1)}, bf16[4,2,2,32,1152]{4,3,2,1,0:T(8,128)(2,1)}, bf16[2,2,80,384]{3,2,1,0:T(8,128)(2,1)}, bf16[2,2,16,1152]{3,2,1,0:T(8,128)(2,1)}) custom-call(f32[256,1152]{1,0:T(8,128)} %get-tuple-element.46.middle_grad, f32[256,1152]{1,0:T(8,128)} %get-tuple-element.47.attended, ...), custom_call_target="tpu_custom_call" | custom-call | tf_op jit(solution)/shard_map/retreat/pallas_call | solution.py:703
  359.4 2.7 fusion.16
  362.1 1.4 reshape_squeeze.6
  363.5 1.5 copy.42
  365.0 1.0 reshape.266
  366.0 0.3 slice_convert_fusion.1
  366.3 0.0 copy-start
  366.3 2.6 reshape.272
  369.0 1.4 reshape_squeeze.7
  370.4 1.5 copy.41
  371.9 0.7 reshape.267
  372.6 0.3 slice_convert_fusion
  373.0 0.0 copy-start.5
  373.0 2.6 reshape.273
  375.6 0.0 copy-done.5
  375.6 0.1 slice.97
  375.7 1.4 slice_convert_fusion.2
  377.1 0.0 copy-done.8
  377.2 0.0 copy-start.9
  377.2 0.0 copy-start.6
  377.2 0.2 copy.35
  377.5 0.4 reshape.263
  377.8 0.7 slice.92
  378.6 0.7 fusion.17
  379.2 0.1 slice_reduce_fusion
  379.3 0.6 dynamic_slice.34
  379.9 0.6 dynamic_slice.35
  380.5 0.6 dynamic_slice.30
  381.1 0.6 dynamic_slice.31
  381.7 0.6 dynamic_slice.32
  382.3 0.6 dynamic_slice.33
  382.9 0.7 bitcast_convert_fusion
  383.6 0.8 copy.46
  384.5 0.8 copy.47
  (23 shorter events, 0.2 us)
Async XLA Ops:
  0.6 4.1 %copy-start.2 = (bf16[72,6912]{1,0:T(8,128)(2,1)S(1)}, bf16[72,6912]{1,0:T(8,128)(2,1)}, u32[]{:S(2)}) copy-start(bf16[72,6912]{1,0:T(8,128)(2,1)} %param.20) | copy-start | bytes 2985988
  7.2 1.2 copy-start.3
  11.6 1.4 copy-start.4
  103.5 4.6 %copy-start.1 = (bf16[4,2,2,2,32,1152]{5,4,3,2,1,0:T(8,128)(2,1)S(1)}, bf16[4,2,2,2,32,1152]{5,4,3,2,1,0:T(8,128)(2,1)}, u32[]{:S(2)}) copy-start(bf16[4,2,2,2,32,1152]{5,4,3,2,1,0:T(8,128)(2,1)} %get-tuple-element.44) | copy-start | bytes 7077892
  366.3 2.7 copy-start
  373.0 2.7 copy-start.5
  375.7 1.4 copy-start.8
  377.2 5.7 %copy-start.9 = (bf16[2,2,16,1152]{3,2,1,0:T(8,128)(2,1)S(1)}, bf16[2,2,16,1152]{3,2,1,0:T(8,128)(2,1)}, u32[]{:S(2)}) copy-start(bf16[2,2,16,1152]{3,2,1,0:T(8,128)(2,1)} %get-tuple-element.62) | copy-start | bytes 442372
  377.2 6.4 %copy-start.6 = (bf16[256,1152]{1,0:T(8,128)(2,1)S(1)}, bf16[256,1152]{1,0:T(8,128)(2,1)}, u32[]{:S(2)}) copy-start(bf16[256,1152]{1,0:T(8,128)(2,1)} %get-tuple-element.102) | copy-start | bytes 1769476
  377.8 6.6 %copy-start.7 = (bf16[256,1152]{1,0:T(8,128)(2,1)S(1)}, bf16[256,1152]{1,0:T(8,128)(2,1)}, u32[]{:S(2)}) copy-start(bf16[256,1152]{1,0:T(8,128)(2,1)} %get-tuple-element.103) | copy-start | bytes 1769476

commit v3 on v2

--- a/solution.py
+++ b/solution.py
@@ -57,6 +57,25 @@
     for peer in peers:
         pl.semaphore_signal(barrier, inc=1, device_id=peer, device_id_type=MESH)
     pl.semaphore_wait(barrier, len(peers))
+
+
+class Moves:
+    def __init__(self, sems):
+        self.sems, self.used, self.open = sems, 0, []
+
+    def start(self, src, dst):
+        made = pltpu.make_async_copy(src, dst, self.sems.at[self.used])
+        self.used += 1
+        made.start()
+        return made
+
+    def store(self, src, dst):
+        self.open.append(self.start(src, dst))
+
+    def drain(self):
+        for made in self.open:
+            made.wait()
+        self.open = []
 
 
 class Lines:
@@ -185,19 +204,26 @@
 
 
 def mlp_kernel(
-    own_x, middle, cot, gain_in, gain_out, w_gate, w_up, w_down,
-    layer_out, middle_grad, d_gain_in, d_gain_out, d_in, d_down,
-    xs, gs, act, slope, hidden, cross_f, cross_b, landed_f, landed_b, stage_core, stage_ring,
-    mine, mixed_grad, send, recv,
+    xs_h, middle_h, cot_h, gains, w_gate_h, w_up_h, w_down_h,
+    layer_out, middle_grad, d_gain_in, d_gain_out, d_in_h, half_down,
+    xs, middle, cot, w_gate, w_up, w_down, d_in, gs, act, slope, hidden, cross_f, cross_b, landed_f, landed_b, stage_core, stage_ring,
+    mine, mixed_grad, d_down, *rest,
 ):
     here = Place()
-    greet([here.mate()] + [here.to(dx=d) for d in (1, 2, 3)])
-    lines = Lines(send, recv)
-    n, width = own_x.shape
-
-    ring = RingGather(here, lines, own_x, xs)
+    moves = Moves(rest[-1])
+    load_first = [
+        moves.start(a, b)
+        for a, b in ((xs_h.at[2], xs.at[2]), (w_gate_h, w_gate), (w_up_h, w_up), (w_down_h, w_down))
+    ]
+    load_xs = {r: moves.start(xs_h.at[r], xs.at[r]) for r in (3, 1, 0)}
+    load_last = [moves.start(a, b) for a, b in ((middle_h, middle), (cot_h, cot))]
+    greet([here.mate()] + [here.to(dx=d) for d in (1, 2, 3)] + plane_peers(here))
+    lines = Lines(*rest[-3:-1])
+    n, width = middle.shape
+    gain_in, gain_out = gains[2:3, :width], gains[3:4, :width]
+
     sums = RingSum(here, lines, mine, landed_f, cross_f, stage_core, stage_ring)
-    ring.start()
+    down_sum = PlaneSum(here, lines, d_down, *rest[:6])
 
     def forward(r):
         x = xs[r]
@@ -207,22 +233,21 @@
         hidden[r] = h.astype(BF16)
         sums.add(r, lambda q: dot(hidden[r, q * n : (q + 1) * n], w_down[...]))
 
-    ring.ready0()
-    forward(0)
-    ring.relay()
-    ring.ready3()
-    forward(3)
-    ring.ready1()
-    forward(1)
-    ring.ready2()
+    for made in load_first:
+        made.wait()
     forward(2)
+    for r in (3, 1, 0):
+        load_xs[r].wait()
+        forward(r)
+    for made in load_last:
+        made.wait()
     mixed = sums.total()
     lines.drain()
 
     cot_f = cot[...].astype(F32)
-    u = cot_f * (1.0 + gain_out[...])
+    u = cot_f * (1.0 + gain_out)
     factor, grad = norm_back(mixed, u, width)
-    layer_out[...] = (middle[...] + mixed * factor * (1.0 + gain_out[...])).astype(BF16)
+    layer_out[...] = (middle[...] + mixed * factor * (1.0 + gain_out)).astype(BF16)
     d_gain_out[...] = jnp.sum(cot_f * mixed * factor, axis=0, keepdims=True)
     mixed_grad[...] = grad.astype(BF16)
 
@@ -259,33 +284,44 @@
             at = PART * k + 32 * p
             d_down[k // 2, k % 2, p // 2, p % 2, :rows] = grad_down[at : at + rows].astype(BF16)
         d_down[k // 2, k % 2, 1, 1, PART - 96 :] = jnp.zeros((128 - PART, width), BF16)
+    down_sum.first()
     for mat, side in ((0, slope), (1, act)):
         grad_side = dot(flat(xs), flat(side), TN)
         for f in range(16):
             d_in[f // 4, (f // 2) % 2, mat, f % 2] = grad_side[72 * f : 72 * f + 72].astype(BF16)
+        moves.store(d_in.at[:, :, mat], d_in_h.at[:, :, mat])
+    down_sum.second()
 
     update = sums.total()
     base = middle[...]
-    u = update * (1.0 + gain_in[...])
+    u = update * (1.0 + gain_in)
     factor, grad = norm_back(base, u, width)
     d_gain_in[...] = jnp.sum(update * base * factor, axis=0, keepdims=True)
     middle_grad[...] = cot[...].astype(F32) + grad
+    for path in (0, 1):
+        half_down[path] = down_sum.result(path).astype(BF16)
     lines.drain()
-
-
-def mlp_block(own_x, middle, cot, gain_in, gain_out, w_gate, w_up, w_down):
-    n, width = own_x.shape
+    moves.drain()
+
+
+def mlp_block(xs, middle, cot, gains, w_gate, w_up, w_down):
+    n, width = middle.shape
     units = w_gate.shape[1]
-    vmem = pl.BlockSpec(memory_space=pltpu.VMEM)
+    vmem, hbm = pl.BlockSpec(memory_space=pltpu.VMEM), pl.BlockSpec(memory_space=pl.ANY)
     shape = jax.ShapeDtypeStruct
+    d_in = shape((4, 2, 2, 2, width // 16, units), BF16)
     scratch = (
-        [pltpu.VMEM((4, 2 * n, width), BF16)] * 2
+        [pltpu.VMEM(a.shape, a.dtype) for a in (xs, middle, cot, w_gate, w_up, w_down, d_in)]
+        + [pltpu.VMEM((4, 2 * n, width), BF16)]
         + [pltpu.VMEM((4, 2 * n, units), BF16)] * 3
         + [pltpu.VMEM((4, n, width), BF16)] * 2
         + [pltpu.VMEM((3, n, width), BF16)] * 2
         + [pltpu.VMEM((4, n, width), BF16), pltpu.VMEM((3, n, width), BF16)]
         + [pltpu.VMEM((n, width), F32), pltpu.VMEM((n, width), BF16)]
-        + [pltpu.SemaphoreType.DMA((34,)), pltpu.SemaphoreType.DMA((34,))]
+        + [pltpu.VMEM((4, 2, 2, 2, 32, width), BF16)]
+        + PlaneSum.scratch((32, width))
+        + [pltpu.SemaphoreType.DMA((36,))] * 2
+        + [pltpu.SemaphoreType.DMA((11,))]
     )
     return pl.pallas_call(
         mlp_kernel,
@@ -294,49 +330,82 @@
             shape((n, width), F32),
             shape((1, width), F32),
             shape((1, width), F32),
-            shape((4, 2, 2, 2, width // 16, units), BF16),
-            shape((4, 2, 2, 2, 32, width), BF16),
+            d_in,
+            shape((2, 32, width), BF16),
         ),
-        in_specs=[vmem] * 8,
-        out_specs=(vmem,) * 6,
+        in_specs=[hbm] * 3 + [vmem] + [hbm] * 3,
+        out_specs=(vmem,) * 4 + (hbm, vmem),
         scratch_shapes=scratch,
         compiler_params=pltpu.CompilerParams(
             collective_id=1, has_side_effects=True, vmem_limit_bytes=63 * MIB
         ),
         name="mlp_block",
-    )(own_x, middle, cot, gain_in, gain_out, w_gate, w_up, w_down)
+    )(xs, middle, cot, gains, w_gate, w_up, w_down)
 
 
 def plane_peers(here):
     return [here.to(dz=d) for d in (1, 2, 3)] + [here.to(dy=d) for d in (1, 2, 3)]
 
 
-def plane_gather_first(here, lines, local, pairs):
-    z, yh, yl = here.z, here.yh, here.yl
-    hops = []
-    for k, (own, full) in enumerate(pairs):
-        keep = pltpu.make_async_copy(own.at[yl], full.at[z, yh, yl], local.at[k])
+class PlaneGather:
+    def __init__(self, here, lines, local, own, full):
+        self.here, self.lines, self.local, self.own, self.full = here, lines, local, own, full
+
+    def first(self):
+        here, own, full, copy = self.here, self.own, self.full, self.lines.copy
+        z, yh, yl = here.z, here.yh, here.yl
+        keep = pltpu.make_async_copy(own.at[yl], full.at[z, yh, yl], self.local)
         keep.start()
-        by_z = [lines.copy(own.at[yl, 0], full.at[z, yh, yl, 0], here.to(dz=d)) for d in (1, 3, 2)]
-        by_y = [lines.copy(own.at[yl, 1], full.at[z, yh, yl, 1], here.to(dy=d)) for d in (1, 3, 2)]
+        self.a, self.b = [], []
+        for d in (1, 3, 2):
+            self.a.append(copy(own.at[yl, 0], full.at[z, yh, yl, 0], here.to(dz=d)))
+            self.b.append(copy(own.at[yl, 1], full.at[z, yh, yl, 1], here.to(dy=d)))
         keep.wait()
-        hops.append((by_z, by_y))
-    return hops
-
-
-def plane_gather_second(here, lines, pairs, hops):
-    z, yh, yl = here.z, here.yh, here.yl
-    last = []
-    for (_, full), (by_z, by_y) in zip(pairs, hops):
-        for made in by_z:
+
+    def blocks(self, dy, dz):
+        _, shard, yl = self.here.to(dy=dy)
+        yh = lax.rem(shard // 2, 2)
+        z = self.here.to(dz=dz)[1] // 4
+        full = self.full
+        return (
+            [full.at[pl.ds(0, 2), yh, yl, 0], full.at[pl.ds(2, 2), yh, yl, 0]],
+            [full.at[z, 0, :, 1], full.at[z, 1, :, 1]],
+        )
+
+    def second(self):
+        here, copy = self.here, self.lines.copy
+        for made in self.a + self.b:
             made.wait_recv()
-        block = full.at[:, yh, yl, 0]
-        last += [lines.copy(block, block, here.to(dy=d)) for d in (1, 3, 2)]
-        for made in by_y:
+        by_y, by_z = self.blocks(0, 0)
+        self.early, self.late = [], []
+        for block, up, down in (
+            (by_y, here.to(dy=1), here.to(dy=3)),
+            (by_z, here.to(dz=1), here.to(dz=3)),
+        ):
+            self.early.append(copy(block[0], block[0], up))
+            self.early.append(copy(block[1], block[1], down))
+        for block, up, down in (
+            (by_y, here.to(dy=1), here.to(dy=3)),
+            (by_z, here.to(dz=1), here.to(dz=3)),
+        ):
+            self.late.append(copy(block[1], block[1], up))
+            self.late.append(copy(block[0], block[0], down))
+
+    def relay(self):
+        here, copy = self.here, self.lines.copy
+        left_y, left_z = self.blocks(3, 3)
+        right_y, right_z = self.blocks(1, 1)
+        for made, block, to in zip(
+            self.early,
+            (left_y[0], right_y[1], left_z[0], right_z[1]),
+            (here.to(dy=1), here.to(dy=3), here.to(dz=1), here.to(dz=3)),
+        ):
             made.wait_recv()
-        block = full.at[z, :, :, 1]
-        last += [lines.copy(block, block, here.to(dz=d)) for d in (1, 3, 2)]
-    return last
+            self.late.append(copy(block, block, to))
+
+    def wait(self):
+        for made in self.late:
+            made.wait_recv()
 
 
 def head_forward(pre, scale, cosine, sine, factor):
@@ -358,60 +427,114 @@
 
 
 def attend_kernel(
-    tokens, cosine, sine, own_qkv, own_out, own_in, own_down,
-    full_in, full_down, w_qkv, w_out, gains, normed, queries, kv, probs, context, attended, qkv_pre,
-    middle, mlp_in,
-    full_qkv, chip_in, send, recv, local,
+    tokens, cosine, sine, tail, w_query, w_key, w_value, own_out, w_gate, w_up, w_down,
+    *refs,
 ):
+    kept = refs[:14]
+    gains = refs[14]
+    held = refs[15:29]
+    (
+        xs, gate_full, up_full, down_full, w_qkv, w_out, normed, queries, kv, probs, context,
+        attended, qkv_pre, middle,
+    ) = held
+    mlp_in, own_qkv, own_in, own_down, full_qkv, full_in, full_down, chip_in = refs[29:37]
+    send, recv, local, moved = refs[37:]
+    moves = Moves(moved)
+    place = {id(a): b for a, b in zip(held, kept)}
+    keep = lambda ref: moves.store(ref, place[id(ref)])
     here = Place()
-    greet([here.mate()] + plane_peers(here))
+    x_at, c, yl = here.x, here.c, here.yl
+    n, width = tokens.shape
+    rows, units = w_gate.shape
+    block = units // 16
+    head_dim = w_key.shape[1]
+    at = w_query.shape[1]
+    heads = at // head_dim
+    wide = own_qkv.shape[-1]
     lines = Lines(send, recv)
-    c, yl = here.c, here.yl
-    n, width = tokens.shape
-    head_dim = 2 * cosine.shape[1]
-    heads = queries.shape[1] // head_dim
-    rows = width // 16
+    gather = [
+        PlaneGather(here, lines, local.at[k], own, full)
+        for k, (own, full) in enumerate(
+            (
+                (own_qkv, full_qkv.at[:, :, c]),
+                (own_out, w_out.at[:, :, c]),
+                (chip_in, full_in),
+                (own_down, full_down),
+            )
+        )
+    ]
+
+    sides = [(w_query, 0), (w_key, at), (w_value, at + head_dim)]
+    for p in range(4):
+        for side, start in sides:
+            lo, hi = max(p * wide, start), min((p + 1) * wide, start + side.shape[1])
+            if lo < hi:
+                own_qkv[p // 2, p % 2, :rows, lo - p * wide : hi - p * wide] = side[
+                    :, lo - start : hi - start
+                ]
+        own_qkv[p // 2, p % 2, rows:] = tail[:, p * wide : (p + 1) * wide]
+    greet([here.mate()] + plane_peers(here) + [here.to(dx=d) for d in (1, 2, 3)])
+    gather[0].first()
+    gather[1].first()
+    lane = lax.broadcasted_iota(jnp.int32, (rows, PART), 1)
+    inside = lane < block - x_at * PART
+    for mat, weight in ((0, w_gate), (1, w_up)):
+        turned = pltpu.roll(weight[...].astype(F32), lax.rem(units - PART * x_at, units), 1)
+        for core in range(2):
+            parts = [
+                jnp.where(inside, turned[:, block * f : block * f + PART], 0.0)
+                for f in range(core, 16, 2)
+            ]
+            own_in[core, mat] = jnp.concatenate(parts, axis=1).astype(BF16)
     across = lines.copy(own_in.at[1 - c], chip_in.at[:, c], here.mate())
-    qkv, out = (own_qkv, full_qkv.at[:, :, c]), (own_out, w_out.at[:, :, c])
-    mlp = [(chip_in, full_in), (own_down, full_down)]
-    hops = plane_gather_first(here, lines, local, [qkv, out])
     chip_in[:, c] = own_in[c]
+    gather[0].second()
+    for p in range(3):
+        start = pl.multiple_of(PART * x_at + 32 * p, 16)
+        own_down[p // 2, p % 2] = w_down[pl.ds(start, 32)]
+    start = pl.multiple_of(jnp.minimum(PART * x_at + 96, block - 16), 16)
+    last = w_down[pl.ds(start, 16)].astype(F32)
+    own_down[1, 1, :16] = jnp.where(x_at < 3, last, 0.0).astype(BF16)
+    own_down[1, 1, 16:] = jnp.zeros((16, width), BF16)
     x = tokens[...].astype(F32)
     lean = x * lax.rsqrt(jnp.mean(x * x, axis=-1, keepdims=True) + EPS)
-    last_qkv = plane_gather_second(here, lines, [qkv], hops[:1])
-    last_out = plane_gather_second(here, lines, [out], hops[1:])
+    gather[0].relay()
+    gather[1].second()
     across.wait_recv()
-    hops = plane_gather_first(here, lines, local, mlp)
-    for made in last_qkv:
-        made.wait_recv()
+    gather[2].first()
+    gather[3].first()
+    gather[0].wait()
     core_qkv = lines.copy(full_qkv.at[:, :, c], full_qkv.at[:, :, c], here.mate())
-    last_in = plane_gather_second(here, lines, mlp[:1], hops[:1])
-    last_down = plane_gather_second(here, lines, mlp[1:], hops[1:])
     core_qkv.wait_recv()
     for p in range(4):
-        total = jnp.zeros((8, full_qkv.shape[-1]), F32)
-        cols = slice(p * full_qkv.shape[-1], (p + 1) * full_qkv.shape[-1])
+        total = jnp.zeros((8, wide), F32)
+        cols = slice(p * wide, (p + 1) * wide)
         for f in range(16):
             part = full_qkv[f // 4, (f // 2) % 2, f % 2, p // 2, p % 2]
             w_qkv[rows * f : rows * f + rows, cols] = part[:rows]
             total = total + part.astype(F32)[rows : rows + 8]
         gains[:, cols] = total
+    gather[1].relay()
+    gather[2].second()
+    keep(w_qkv)
     normed[...] = (lean * (1.0 + gains[0:1, :width])).astype(BF16)
     qkv_pre[...] = dot(normed[...], w_qkv[...])
     cos_v, sin_v = cosine[...], sine[...]
     q_scale, k_scale = (gains[k : k + 1, width : width + head_dim] for k in (0, 1))
-    at = heads * head_dim
     key = head_forward(qkv_pre[:, at : at + head_dim], k_scale, cos_v, sin_v, 1.0)
     kv[yl, :, :head_dim] = key
     kv[yl, :, head_dim:] = qkv_pre[:, at + head_dim :].astype(BF16)
     kv_sent = lines.copy(kv.at[yl], kv.at[yl], here.pair())
+    keep(normed)
+    keep(qkv_pre)
     for h in range(heads):
         cols = slice(h * head_dim, (h + 1) * head_dim)
         queries[:, cols] = head_forward(qkv_pre[:, cols], q_scale, cos_v, sin_v, head_dim**-0.5)
-    for made in last_out:
-        made.wait_recv()
+    gather[1].wait()
     core_out = lines.copy(w_out.at[:, :, c], w_out.at[:, :, c], here.mate())
     kv_sent.wait_recv()
+    keep(queries)
+    keep(kv)
     keys = kv[:, :, :head_dim].reshape(2 * n, head_dim)
     values = kv[:, :, head_dim:].reshape(2 * n, head_dim)
     row = lax.broadcasted_iota(jnp.int32, (n, 2 * n), 0) + yl * n
@@ -424,62 +547,102 @@
         probs[h] = low
         context[:, cols] = dot(low, values).astype(BF16)
     core_out.wait_recv()
-    att = dot(context[...], w_out[...].reshape(heads * head_dim, width))
+    att = dot(context[...], w_out[...].reshape(at, width))
     attended[...] = att
     r = lax.rsqrt(jnp.mean(att * att, axis=-1, keepdims=True) + EPS)
     mid = x + att * r * (1.0 + gains[1:2, :width])
     middle[...] = mid
     r = lax.rsqrt(jnp.mean(mid * mid, axis=-1, keepdims=True) + EPS)
     mlp_in[...] = (mid * r * (1.0 + gains[2:3, :width])).astype(BF16)
-    for made in last_in + last_down:
-        made.wait_recv()
+    ring = RingGather(here, lines, mlp_in, xs)
+    ring.start()
+    for ref in (probs, context, w_out, attended, middle):
+        keep(ref)
+    gather[2].relay()
+    gather[3].second()
+    gather[2].wait()
+    for f in range(16):
+        for mat, whole in ((0, gate_full), (1, up_full)):
+            whole[rows * f : rows * f + rows] = full_in[f // 4, (f // 2) % 2, mat, f % 2]
+    keep(gate_full)
+    keep(up_full)
+    gather[3].relay()
+    ring.ready0()
+    ring.relay()
+    gather[3].wait()
+    for k in range(8):
+        for p in range(4):
+            count = min(32, PART - 32 * p)
+            down_full[PART * k + 32 * p : PART * k + 32 * p + count] = full_down[
+                k // 2, k % 2, p // 2, p % 2, :count
+            ]
+    keep(down_full)
+    ring.ready3()
+    ring.ready1()
+    ring.ready2()
+    keep(xs)
     lines.drain()
-
-
-def attend_block(tokens, cosine, sine, own_qkv, own_out, own_in, own_down):
+    moves.drain()
+
+
+def attend_block(tokens, cosine, sine, tail, w_query, w_key, w_value, own_out, w_gate, w_up, w_down):
     n, width = tokens.shape
-    vmem, hbm = pl.BlockSpec(memory_space=pltpu.VMEM), pl.BlockSpec(memory_space=pl.ANY)
+    vmem = pl.BlockSpec(memory_space=pltpu.VMEM)
     shape = jax.ShapeDtypeStruct
-    p_qkv, p_out, p_in, p_down = own_qkv.shape[2:], own_out.shape[2:], own_in.shape[2:], own_down.shape[2:]
-    cols, head_dim = 4 * p_qkv[1], 2 * cosine.shape[1]
-    out_width = cols - 2 * head_dim
+    low = lambda *s: shape(s, BF16)
+    rows, out_width = w_query.shape
+    head_dim, cols = w_key.shape[1], tail.shape[1]
+    p_qkv, p_out = (rows + 8, cols // 4), own_out.shape[2:]
+    p_in, p_down = (rows, CORE_UNITS), (32, width)
+    vm = lambda *s: pltpu.VMEM(s, BF16)
+    held = (
+        low(4, 2 * n, width),
+        low(width, CORE_UNITS),
+        low(width, CORE_UNITS),
+        low(CORE_UNITS, width),
+        low(width, cols),
+        low(4, 2, 2, 2, 2, *p_out),
+        low(n, width),
+        low(n, out_width),
+        low(2, n, 2 * head_dim),
+        low(out_width // head_dim, n, 2 * n),
+        low(n, out_width),
+        shape((n, width), F32),
+        shape((n, cols), F32),
+        shape((n, width), F32),
+    )
     return pl.pallas_call(
         attend_kernel,
-        out_shape=(
-            shape((4, 2, 2, 2, *p_in), BF16),
-            shape((4, 2, 2, 2, *p_down), BF16),
-            shape((width, cols), BF16),
-            shape((4, 2, 2, 2, 2, *p_out), BF16),
-            shape((8, cols), F32),
-            shape((n, width), BF16),
-            shape((n, out_width), BF16),
-            shape((2, n, 2 * head_dim), BF16),
-            shape((out_width // head_dim, n, 2 * n), BF16),
-            shape((n, out_width), BF16),
-            shape((n, width), F32),
-            shape((n, cols), F32),
-            shape((n, width), F32),
-            shape((n, width), BF16),
-        ),
-        in_specs=[vmem] * 7,
-        out_specs=(hbm,) * 2 + (vmem,) * 12,
-        scratch_shapes=[
-            pltpu.VMEM((4, 2, 2, 2, 2, *p_qkv), BF16),
-            pltpu.VMEM(own_in.shape, BF16),
-            pltpu.SemaphoreType.DMA((52,)),
-            pltpu.SemaphoreType.DMA((52,)),
-            pltpu.SemaphoreType.DMA((2,)),
+        out_shape=held + (shape((8, cols), F32),),
+        in_specs=[vmem] * 11,
+        out_specs=(pl.BlockSpec(memory_space=pl.ANY),) * 14 + (vmem,),
+        scratch_shapes=[pltpu.VMEM(a.shape, a.dtype) for a in held]
+        + [
+            vm(n, width),
+            vm(2, 2, *p_qkv),
+            vm(2, 2, *p_in),
+            vm(2, 2, *p_down),
+            vm(4, 2, 2, 2, 2, *p_qkv),
+            vm(4, 2, 2, 2, *p_in),
+            vm(4, 2, 2, 2, *p_down),
+            vm(2, 2, *p_in),
+            pltpu.SemaphoreType.DMA((86,)),
+            pltpu.SemaphoreType.DMA((86,)),
+            pltpu.SemaphoreType.DMA((4,)),
+            pltpu.SemaphoreType.DMA((14,)),
         ],
         compiler_params=pltpu.CompilerParams(
-            collective_id=0, has_side_effects=True, vmem_limit_bytes=60 * MIB
+            collective_id=0, has_side_effects=True, vmem_limit_bytes=62 * MIB
         ),
         name="attend",
-    )(tokens, cosine, sine, own_qkv, own_out, own_in, own_down)
+    )(tokens, cosine, sine, tail, w_query, w_key, w_value, own_out, w_gate, w_up, w_down)
 
 
 class PlaneSum:
-    def __init__(self, here, lines, grads, landed_a, sums_a, landed_b, sums_b, last_a, last_b):
-        self.here, self.lines, self.grads = here, lines, grads
+    def __init__(
+        self, here, lines, grads, landed_a, sums_a, landed_b, sums_b, last_a, last_b, held=None
+    ):
+        self.here, self.lines, self.grads, self.held = here, lines, grads, held
         self.landed_a, self.sums_a, self.last_a = landed_a, sums_a, last_a
         self.landed_b, self.sums_b, self.last_b = landed_b, sums_b, last_b
 
@@ -503,7 +666,8 @@
         for made in self.a:
             made.wait_recv()
         for k in range(4):
-            total = g[k, here.yh, here.yl, 0].astype(F32)
+            own = self.held[0][k] if self.held else g[k, here.yh, here.yl, 0]
+            total = own.astype(F32)
             for j in range(3):
                 total = total + self.landed_a[j, k].astype(F32)
             self.sums_a[k] = total.astype(BF16)
@@ -514,7 +678,8 @@
         for made in self.b:
             made.wait_recv()
         for k in range(4):
-            total = g[here.z, k // 2, k % 2, 1].astype(F32)
+            own = self.held[1][k // 2, k % 2] if self.held else g[here.z, k // 2, k % 2, 1]
+            total = own.astype(F32)
             for j in range(3):
                 total = total + self.landed_b[j, k // 2, k % 2].astype(F32)
             self.sums_b[k // 2, k % 2] = total.astype(BF16)
@@ -537,15 +702,41 @@
 
 
 def retreat_kernel(
-    middle_grad, attended, context, probs, kv, queries, qkv_pre, normed, tokens, cosine, sine,
-    w_qkv, w_out, gains, d_gain_in, d_gain_out, g_in, g_down,
+    middle_grad_h, attended_h, context_h, probs_h, kv_h, queries_h, qkv_pre_h, normed_h, tokens_h,
+    w_qkv_h, w_out_h, g_in, cosine, sine, gains, d_gain_in, d_gain_out, half_down,
     grad_tokens, o_in, o_down, o_qkv, o_out,
+    middle_grad, attended, context, probs, kv, queries, qkv_pre, normed, tokens, w_qkv, w_out,
+    held_a, held_b,
     context_grad, attn_side, kv_part, kv_give, kv_land, g_qkv, g_out, d_gains,
     chip_qkv, chip_out, cross_qkv, cross_out, swap, half_qkv, half_out, land_qkv, land_out, *rest,
 ):
     here = Place()
-    send, recv = rest[-2:]
+    send, recv, moved = rest[-3:]
     x, yl, c = here.x, here.yl, here.c
+    moves = Moves(moved)
+    loads = {
+        name: moves.start(a, b)
+        for name, a, b in (
+            ("attended", attended_h, attended),
+            ("middle_grad", middle_grad_h, middle_grad),
+            ("w_out", w_out_h, w_out),
+            ("context", context_h, context),
+            ("probs", probs_h, probs),
+            ("kv", kv_h, kv),
+            ("queries", queries_h, queries),
+            ("qkv_pre", qkv_pre_h, qkv_pre),
+            ("w_qkv", w_qkv_h, w_qkv),
+            ("normed", normed_h, normed),
+            ("tokens", tokens_h, tokens),
+            ("held_a", g_in.at[:, here.yh, yl, 0], held_a),
+            ("held_b", g_in.at[here.z, :, :, 1], held_b),
+        )
+    }
+
+    def ready(*names):
+        for name in names:
+            loads[name].wait()
+
     greet([here.mate()] + plane_peers(here) + [here.to(dx=d) for d in (1, 2, 3)])
     lines = Lines(send, recv)
     copy = lines.copy
@@ -555,11 +746,13 @@
     rows = width // 16
     at = heads * head_dim
     sums = [
-        PlaneSum(here, lines, g, *rest[6 * k : 6 * k + 6])
-        for k, g in enumerate((g_in, g_down, chip_qkv, chip_out))
+        PlaneSum(here, lines, g, *rest[6 * k : 6 * k + 6], held)
+        for k, (g, held) in enumerate(((g_in, (held_a, held_b)), (chip_qkv, None), (chip_out, None)))
     ]
     sums[0].first()
-    sums[1].first()
+    o_down[x, yl] = half_down[...]
+    down_pair = copy(half_down, o_down.at[x, yl], here.pair())
+    ready("attended", "middle_grad", "w_out", "context")
 
     att, dy = attended[...], middle_grad[...]
     r, grad = norm_back(att, dy * (1.0 + gains[1:2, :width]), width)
@@ -573,7 +766,10 @@
     grad_out = dot(context[...], attended_grad, TN)
     g_out[...] = grad_out.astype(BF16).reshape(g_out.shape)
     give_out = copy(g_out.at[:, :, 1 - c], cross_out, here.mate())
-
+    down_pair.wait_recv()
+    down_x = [copy(o_down.at[x], o_down.at[x], here.to(dx=d)) for d in (1, 3, 2)]
+
+    ready("probs", "kv", "queries", "qkv_pre")
     keys = kv[:, :, :head_dim].reshape(2 * n, head_dim)
     values = kv[:, :, head_dim:].reshape(2 * n, head_dim)
     cos_v, sin_v = cosine[...], sine[...]
@@ -602,8 +798,11 @@
         d_query = d_query + d_scale
     kv_give[...] = kv_part[1 - yl].astype(BF16)
     kv_sent = copy(kv_give, kv_land, here.pair())
-    sums[0].second()
-    sums[1].second()
+    give_out.wait_recv()
+    for z in range(4):
+        for yh in range(2):
+            chip_out[z, yh] = (g_out[z, yh, c].astype(F32) + cross_out[z, yh].astype(F32)).astype(BF16)
+    sums[2].first()
     kv_sent.wait_recv()
     kv_grad = (kv_part[yl] + kv_land[...].astype(F32)).astype(BF16)
     side, d_key = head_backward(
@@ -614,12 +813,7 @@
     d_gains[0:1, width : width + head_dim] = d_query
     d_gains[1:2, width : width + head_dim] = d_key
 
-    give_out.wait_recv()
-    for z in range(4):
-        for yh in range(2):
-            chip_out[z, yh] = (g_out[z, yh, c].astype(F32) + cross_out[z, yh].astype(F32)).astype(BF16)
-    sums[3].first()
-
+    ready("w_qkv", "normed", "tokens", "held_a", "held_b")
     normed_grad = dot(attn_side[...], w_qkv[...], NT)
     tok = tokens[...].astype(F32)
     r, grad = norm_back(tok, normed_grad * (1.0 + gains[0:1, :width]), width)
@@ -637,36 +831,34 @@
             g_qkv[spot] = block.astype(BF16)
     give_qkv = copy(g_qkv.at[:, :, 1 - c], cross_qkv, here.mate())
 
+    sums[0].second()
+    give_qkv.wait_recv()
+    for z in range(4):
+        for yh in range(2):
+            chip_qkv[z, yh] = (g_qkv[z, yh, c].astype(F32) + cross_qkv[z, yh].astype(F32)).astype(BF16)
+    sums[1].first()
+    sums[2].second()
     swap[0] = sums[0].result(0).astype(BF16)
     swap[1] = sums[0].result(1).astype(BF16)
     across = copy(swap.at[1 - c], o_in.at[x, yl, c], here.mate())
     o_in[x, yl, c] = swap[c]
+    across.wait_recv()
+    in_pair = copy(o_in.at[x, yl], o_in.at[x, yl], here.pair())
     for path in (0, 1):
-        o_down[x, yl, path] = sums[1].result(path).astype(BF16)
-    to_pair = [copy(o_down.at[x, yl], o_down.at[x, yl], here.pair())]
-    across.wait_recv()
-    to_pair.append(copy(o_in.at[x, yl], o_in.at[x, yl], here.pair()))
-
-    give_qkv.wait_recv()
-    for z in range(4):
-        for yh in range(2):
-            chip_qkv[z, yh] = (g_qkv[z, yh, c].astype(F32) + cross_qkv[z, yh].astype(F32)).astype(BF16)
-    sums[2].first()
-    for made in to_pair:
+        half_out[path] = sums[2].result(path).astype(BF16)
+    by_x = [copy(half_out, land_out.at[d - 1], here.to(dx=d)) for d in (1, 3, 2)]
+    in_pair.wait_recv()
+    right, left = here.to(dx=1), here.to(dx=3)
+    own = [o_in.at[x, m] for m in (0, 1)]
+    early = [copy(own[0], own[0], right), copy(own[1], own[1], left)]
+    late = [copy(own[1], own[1], right), copy(own[0], own[0], left)]
+    sums[1].second()
+    for made, at_x, m, to in ((early[0], left[0], 0, right), (early[1], right[0], 1, left)):
         made.wait_recv()
-    spread = []
-    for d in (1, 3, 2):
-        spread.append(copy(o_in.at[x], o_in.at[x], here.to(dx=d)))
-        spread.append(copy(o_down.at[x], o_down.at[x], here.to(dx=d)))
-    sums[3].second()
-    sums[2].second()
+        late.append(copy(o_in.at[at_x, m], o_in.at[at_x, m], to))
     for path in (0, 1):
-        half_out[path] = sums[3].result(path).astype(BF16)
-        half_qkv[path] = sums[2].result(path).astype(BF16)
-    by_x = []
-    for d in (1, 3, 2):
-        by_x.append(copy(half_qkv, land_qkv.at[d - 1], here.to(dx=d)))
-        by_x.append(copy(half_out, land_out.at[d - 1], here.to(dx=d)))
+        half_qkv[path] = sums[1].result(path).astype(BF16)
+    by_x += [copy(half_qkv, land_qkv.at[d - 1], here.to(dx=d)) for d in (1, 3, 2)]
     for made in by_x:
         made.wait_recv()
     for half, land, out in ((half_qkv, land_qkv, o_qkv), (half_out, land_out, o_out)):
@@ -676,29 +868,34 @@
                 total = total + land[j, path].astype(F32)
             out[yl, path] = total.astype(BF16)
     ends = [copy(o.at[yl], o.at[yl], here.pair()) for o in (o_qkv, o_out)]
-    for made in spread + ends:
+    for made in down_x + late + ends:
         made.wait_recv()
     lines.drain()
 
 
 def retreat_block(*args):
-    vmem = pl.BlockSpec(memory_space=pltpu.VMEM)
+    (
+        middle_grad, attended, context, probs, kv, queries, qkv_pre, normed, tokens, w_qkv, w_out,
+        g_in, cosine, _, _, _, _, half_down,
+    ) = args
+    vmem, hbm = pl.BlockSpec(memory_space=pltpu.VMEM), pl.BlockSpec(memory_space=pl.ANY)
     shape = jax.ShapeDtypeStruct
-    n, width = args[0].shape
-    out_width, head_dim = args[5].shape[1], 2 * args[9].shape[1]
-    cols = args[6].shape[1]
-    g_in, g_down, w_out = args[-2], args[-1], args[12]
-    p_in, p_down, p_out = g_in.shape[4:], g_down.shape[4:], w_out.shape[5:]
+    n, width = middle_grad.shape
+    out_width, head_dim = queries.shape[1], 2 * cosine.shape[1]
+    cols = qkv_pre.shape[1]
+    p_in, p_down, p_out = g_in.shape[4:], half_down.shape[1:], w_out.shape[5:]
     p_qkv = (width // 16 + 8, cols // 4)
     vm = lambda *s: pltpu.VMEM(s, BF16)
-    scratch = [vm(n, out_width), vm(n, cols), pltpu.VMEM((2, n, 2 * head_dim), F32)]
+    scratch = [pltpu.VMEM(a.shape, a.dtype) for a in args[:11]]
+    scratch += [vm(4, *p_in), vm(2, 2, *p_in)]
+    scratch += [vm(n, out_width), vm(n, cols), pltpu.VMEM((2, n, 2 * head_dim), F32)]
     scratch += [vm(n, 2 * head_dim)] * 2
     scratch += [vm(4, 2, 2, 2, 2, *p_qkv), vm(4, 2, 2, 2, 2, *p_out), pltpu.VMEM((8, cols), F32)]
     scratch += [vm(4, 2, 2, 2, *p_qkv), vm(4, 2, 2, 2, *p_out)] * 2
     scratch += [vm(2, *p_in), vm(2, *p_qkv), vm(2, *p_out), vm(3, 2, *p_qkv), vm(3, 2, *p_out)]
-    for piece in (p_in, p_down, p_qkv, p_out):
+    for piece in (p_in, p_qkv, p_out):
         scratch += PlaneSum.scratch(piece)
-    scratch += [pltpu.SemaphoreType.DMA((68,))] * 2
+    scratch += [pltpu.SemaphoreType.DMA((60,))] * 2 + [pltpu.SemaphoreType.DMA((13,))]
     low = lambda *s: shape(s, BF16)
     return pl.pallas_call(
         retreat_kernel,
@@ -709,7 +906,7 @@
             low(2, 2, *p_qkv),
             low(2, 2, *p_out),
         ),
-        in_specs=[vmem] * len(args),
+        in_specs=[hbm] * 12 + [vmem] * 6,
         out_specs=(vmem,) * 5,
         scratch_shapes=scratch,
         compiler_params=pltpu.CompilerParams(
@@ -717,6 +914,63 @@
         ),
         name="retreat",
     )(*args)
+
+
+def finish_kernel(
+    o_in, o_down, o_qkv, o_out, shown, taken,
+    layer_out, grad_tokens, out_query, out_key, out_value, out_out, out_gate, out_up, out_down,
+    *out_gains,
+):
+    rows, units = out_gate.shape
+    block = units // 16
+    wide = o_qkv.shape[-1]
+    at, head_dim = out_query.shape[1], out_key.shape[1]
+    for m, out in ((0, out_gate), (1, out_up)):
+        for k in range(4):
+            count = min(PART, block - PART * k)
+            for f in range(16):
+                piece = o_in[k, m, f % 2].astype(F32)[:, PART * (f // 2) : PART * (f // 2) + count]
+                out[:, block * f + PART * k : block * f + PART * k + count] = piece
+    for k in range(4):
+        for p in range(4):
+            start = PART * k + 32 * p
+            count = min(32, PART - 32 * p, block - start)
+            if count > 0:
+                out_down[start : start + count] = o_down[k, p // 2, p % 2, :count].astype(F32)
+    tail = []
+    for p in range(4):
+        piece = o_qkv[p // 2, p % 2].astype(F32)
+        for out, start in ((out_query, 0), (out_key, at), (out_value, at + head_dim)):
+            lo, hi = max(p * wide, start), min((p + 1) * wide, start + out.shape[1])
+            if lo < hi:
+                out[:, lo - start : hi - start] = piece[:rows, lo - p * wide : hi - p * wide]
+        tail.append(piece[rows:])
+        height = o_out.shape[2]
+        out_out[p * height : (p + 1) * height] = o_out[p // 2, p % 2].astype(F32)
+    tail = jnp.concatenate(tail, axis=1)
+    width = layer_out.shape[1]
+    shard = lax.axis_index("fsdp")
+    turned = pltpu.roll(tail[:, :width], lax.rem(width - rows * shard, width), 1)
+    for k in range(4):
+        out_gains[k][...] = turned[k, :rows]
+    piece = head_dim // 16
+    turned = pltpu.roll(tail[:, width : width + head_dim], lax.rem(head_dim - piece * shard, head_dim), 1)
+    for k in range(2):
+        out_gains[4 + k][...] = turned[k, :piece]
+    layer_out[...] = shown[...]
+    grad_tokens[...] = taken[...]
+
+
+def finish_block(o_in, o_down, o_qkv, o_out, layer_out, grad_tokens, out_shape):
+    vmem = pl.BlockSpec(memory_space=pltpu.VMEM)
+    return pl.pallas_call(
+        finish_kernel,
+        out_shape=out_shape,
+        in_specs=[vmem] * 6,
+        out_specs=(vmem,) * len(out_shape),
+        compiler_params=pltpu.CompilerParams(vmem_limit_bytes=48 * MIB),
+        name="finish",
+    )(o_in, o_down, o_qkv, o_out, layer_out, grad_tokens)
 
 
 def body(
@@ -740,9 +994,7 @@
     rows = w_query.shape[0]
     head_dim = w_key.shape[1]
     out_width = w_query.shape[1]
-    units = w_gate.shape[1]
-    block = units // 16
-    x_at, shard = lax.axis_index("dp"), lax.axis_index("fsdp")
+    shard = lax.axis_index("fsdp")
 
     mine = jnp.arange(16) == shard
     spread = lambda g: jnp.where(mine[:, None], g[None, :], 0).reshape(1, -1)
@@ -755,21 +1007,7 @@
         ],
         axis=1,
     )
-    qkv = jnp.concatenate([w_query, w_key, w_value], axis=1)
-    own_qkv = jnp.concatenate([qkv, tail], axis=0)
-    own_qkv = own_qkv.reshape(rows + 8, 2, 2, -1).transpose(1, 2, 0, 3)
     own_out = w_out.reshape(2, 2, -1, width)
-
-    def columns(w):
-        w = jnp.pad(w.reshape(rows, 8, 2, block), ((0, 0),) * 3 + ((0, 4 * PART - block),))
-        w = lax.dynamic_slice_in_dim(w, x_at * PART, PART, axis=3)
-        return w.transpose(2, 0, 1, 3).reshape(2, rows, 8 * PART)
-
-    own_in = jnp.stack([columns(w_gate), columns(w_up)], axis=1)
-    down = jnp.pad(w_down, ((0, 4 * PART - block), (0, 0)))
-    down = lax.dynamic_slice_in_dim(down, x_at * PART, PART, axis=0)
-    own_down = jnp.pad(down, ((0, 128 - PART), (0, 0))).reshape(2, 2, 32, width)
-
     positions = (lax.axis_index("seq") * n + jnp.arange(n, dtype=jnp.int32)).astype(F32)
     frequency = jnp.exp(
         jnp.arange(head_dim // 2, dtype=F32) * (-2.0 * math.log(1000000.0) / head_dim)
@@ -778,46 +1016,23 @@
     cosine, sine = jnp.cos(angles), jnp.sin(angles)
 
     (
-        full_in, full_down, w_qkv, w_out_full, gains, normed, queries, kv, probs, context, attended,
-        qkv_pre, middle, mlp_in,
-    ) = attend_block(tokens, cosine, sine, own_qkv, own_out, own_in, own_down)
-    gate_up = full_in.transpose(2, 0, 1, 3, 4, 5).reshape(2, width, CORE_UNITS)
-    full_down = full_down.reshape(8, 128, width)[:, :PART].reshape(CORE_UNITS, width)
-
-    layer_out, middle_grad, d_gain_in, d_gain_out, g_in, g_down = mlp_block(
-        mlp_in, middle, cotangent, gains[2:3, :width], gains[3:4, :width],
-        gate_up[0], gate_up[1], full_down,
+        xs, gate_full, up_full, down_full, w_qkv, w_out_full, normed, queries, kv, probs, context,
+        attended, qkv_pre, middle, gains,
+    ) = attend_block(
+        tokens, cosine, sine, tail, w_query, w_key, w_value, own_out, w_gate, w_up, w_down
+    )
+    layer_out, middle_grad, d_gain_in, d_gain_out, g_in, half_down = mlp_block(
+        xs, middle, cotangent, gains, gate_full, up_full, down_full
     )
     grad_tokens, o_in, o_down, o_qkv, o_out = retreat_block(
-        middle_grad, attended, context, probs, kv, queries, qkv_pre, normed, tokens, cosine, sine,
-        w_qkv, w_out_full, gains, d_gain_in, d_gain_out, g_in, g_down,
+        middle_grad, attended, context, probs, kv, queries, qkv_pre, normed, tokens, w_qkv,
+        w_out_full, g_in, cosine, sine, gains, d_gain_in, d_gain_out, half_down,
     )
-
-    o_qkv = o_qkv.astype(F32)
-    grad_qkv = o_qkv[:, :, :rows].transpose(2, 0, 1, 3).reshape(rows, -1)
-    tail = o_qkv[:, :, rows:].transpose(2, 0, 1, 3).reshape(8, -1)
-    grad_w_out = o_out.astype(F32).reshape(-1, width)
-    gain_outs = [lax.dynamic_slice_in_dim(tail[k], shard * rows, rows) for k in range(4)]
-    piece = head_dim // 16
-    gain_outs += [lax.dynamic_slice_in_dim(tail[k], width + shard * piece, piece) for k in range(2)]
-
-    def whole(part):
-        part = part.reshape(4, 2, rows, 8, PART).transpose(2, 3, 1, 0, 4)
-        return part.reshape(rows, 16, 4 * PART)[..., :block].reshape(rows, units).astype(F32)
-
-    grad_w_down = o_down.reshape(4, 128, width)[:, :PART].reshape(-1, width)[:block].astype(F32)
-    return (
-        layer_out,
-        grad_tokens,
-        grad_qkv[:, :out_width],
-        grad_qkv[:, out_width : out_width + head_dim],
-        grad_qkv[:, out_width + head_dim :],
-        grad_w_out,
-        whole(o_in[:, 0]),
-        whole(o_in[:, 1]),
-        grad_w_down,
-        *gain_outs,
-    )
+    like = lambda a, kind: jax.ShapeDtypeStruct(a.shape, kind)
+    weights = (w_query, w_key, w_value, w_out, w_gate, w_up, w_down)
+    gain_args = (pre_attn_gain, post_attn_gain, pre_mlp_gain, post_mlp_gain, query_gain, key_gain)
+    shapes = [like(tokens, BF16)] * 2 + [like(a, F32) for a in weights + gain_args]
+    return tuple(finish_block(o_in, o_down, o_qkv, o_out, layer_out, grad_tokens, shapes))
 
 
 def solution(mesh):

time: 391 us -> 303 us (0.77)
  Pallas kernels: 337 us -> 289 us
  local copies, waits for them, and re-layouts: 39.8 us -> 6.32 us
  other arithmetic: 7.59 us -> 3.45 us
    pallas_call x1, Pallas kernels: 127 us -> 101 us  [retreat_block(): pl.pallas_call(retreat_kernel, out_shape=(low(n, width), low(4, 2, 2, *p_...]
    pallas_call x1, Pallas kernels: 123 us -> 104 us  [mlp_block(): pl.pallas_call(mlp_kernel, out_shape=(shape((n, width), BF16), shape((n,...]
    slice x8 -> x0, local copies, waits for them, and re-layouts: 11.8 us -> none  [the longest x1 4.63 us: body(): gate_up[1]]
    reshape x9 -> x0, local copies, waits for them, and re-layouts: 8.29 us -> none  [the longest x4 5.42 us: columns(): w.reshape(rows, 8, 2, block)]
    another operation x6 -> x0, local copies, waits for them, and re-layouts: 6.27 us -> none  [the longest x4 5.79 us: whole(): part = part.reshape(4, 2, rows, 8, PART).transpose(2, 3, 1, 0, 4)]
    convert_element_type x2 -> x0, local copies, waits for them, and re-layouts: 5.28 us -> none  [whole(): part.reshape(rows, 16, 4 * PART)[..., :block].reshape(rows, units)]
    pallas_call x1 -> x2, Pallas kernels: 87.1 us -> 84.1 us  [the longest x1 79.8 us: attend_block(): pl.pallas_call(attend_kernel, out_shape=held + (shape((8, cols), F32),),...]
where the time goes in v3:
time: 303 us; the launch traced here: 300 us
  Pallas kernels  289 us (95%)
  local copies, waits for them, and re-layouts  6.32 us (2%)
  other arithmetic  3.45 us (1%)
    pallas_call x1, Pallas kernels, mlp_block(): pl.pallas_call(mlp_kernel, out_shape=(shape((n, width), BF16), shape((n,...  104 us
    pallas_call x1, Pallas kernels, retreat_block(): pl.pallas_call(retreat_kernel, out_shape=(low(n, width), low(4, 2, 2, *p_...  101 us
    pallas_call x1, Pallas kernels, attend_block(): pl.pallas_call(attend_kernel, out_shape=held + (shape((8, cols), F32),),...  79.8 us

profile of v3, /device:TPU:0, one launch (start us, length us, event | category | flops | bytes accessed | tf_op | source)
XLA Modules:
  0.0 299.5 jit_solution(16492987800165925295)
XLA Ops:
  0.7 0.7 broadcast_select_fusion.1
  1.4 0.1 select_n.89
  1.5 0.1 select_n.91
  1.6 0.8 broadcast_select_fusion.5
  2.4 0.1 select_n.81
  2.5 0.1 select_n.83
  2.6 0.1 select_n.85
  2.7 0.1 select_n.87
  2.9 0.6 pad_maximum_fusion.tail
  3.5 1.2 multiply_sine_fusion
  4.7 79.8 %attend.1 = (bf16[4,512,1152]{2,1,0:T(8,128)(2,1)}, bf16[1152,896]{1,0:T(8,128)(2,1)}, bf16[1152,896]{1,0:T(8,128)(2,1)}, bf16[896,1152]{1,0:T(8,128)(2,1)}, bf1...) custom-call(bf16[256,1152]{1,0:T(8,128)(2,1)} %tokens_h.1, ...), custom_call_target="tpu_custom_call" | custom-call | tf_op jit(solution)/shard_map/attend/pallas_call | solution.py:614
  84.6 103.6 %mlp_block.1 = (bf16[256,1152]{1,0:T(8,128)(2,1)}, f32[256,1152]{1,0:T(8,128)}, f32[1,1152]{1,0:T(1,128)}, f32[1,1152]{1,0:T(1,128)}, bf16[4,2,2,2,72,896]{5,4,3...) custom-call(bf16[4,512,1152]{2,1,0:T(8,128)(2,1)} %get-tuple-element.41.xs_h, f32[256,1152]{1,0:T(8,128)} %get-tuple-element.42.middle_h, ...), custom_call_target="tpu_custom_call" | custom-call | tf_op jit(solution)/shard_map/mlp_block/pallas_call | solution.py:326
  188.1 0.0 copy-start.2
  188.2 100.9 %retreat.1 = (bf16[256,1152]{1,0:T(8,128)(2,1)}, bf16[4,2,2,72,896]{4,3,2,1,0:T(8,128)(2,1)}, bf16[4,2,2,32,1152]{4,3,2,1,0:T(8,128)(2,1)}, bf16[2,2,80,384]{3,2,1,0:T(8,128)(2,1)}, bf16[2,2,16,1152]{3,2,1,0:T(8,128)(2,1)}) custom-call(f32[256,1152]{1,0:T(8,128)} %get-tuple-element.47.middle_grad_h, f32[256,1152]{1,0:T(8,128)} %get-tuple-element.48.attended_h, ...), custom_call_target="tpu_custom_call" | custom-call | tf_op jit(solution)/shard_map/retreat/pallas_call | solution.py:900
  289.1 0.0 copy-done.2
  289.1 0.0 copy-start
  289.1 1.6 copy-done
  290.7 0.0 copy-start.1
  290.7 1.3 copy-done.1
  292.0 0.0 copy-start.3
  292.0 1.1 copy-done.3
  293.0 0.0 copy-start.4
  293.0 0.9 copy-done.4
  294.0 0.0 copy-start.5
  294.0 0.9 copy-done.5
  294.9 4.2 %finish.1 = (bf16[256,1152]{1,0:T(8,128)(2,1)}, bf16[256,1152]{1,0:T(8,128)(2,1)}, f32[72,1024]{1,0:T(8,128)}, f32[72,256]{1,0:T(8,128)}, f32[72,256]{1,0:T(8,12...) custom-call(bf16[4,2,2,72,896]{4,3,2,1,0:T(8,128)(2,1)S(1)} %copy-do, ...), custom_call_target="tpu_custom_call" | custom-call | tf_op jit(solution)/shard_map/finish/pallas_call | solution.py:966
  (5 shorter events, 0.1 us)
Async XLA Ops:
  188.1 101.0 %copy-start.2 = (bf16[256,1152]{1,0:T(8,128)(2,1)S(1)}, bf16[256,1152]{1,0:T(8,128)(2,1)}, u32[]{:S(2)}) copy-start(bf16[256,1152]{1,0:T(8,128)(2,1)} %get-tuple-element.65.shown) | copy-start | bytes 1769476
  289.1 1.6 copy-start
  290.7 1.3 copy-start.1
  292.0 1.1 copy-start.3
  293.0 0.9 copy-start.4
  294.0 0.9 copy-start.5

commit v4 on v3

--- a/solution.py
+++ b/solution.py
@@ -137,12 +137,18 @@
         here, full, copy = self.here, self.full, self.lines.copy
         n = self.own.shape[0]
         h = n // 2
-        lo, hi, both, other = pl.ds(0, h), pl.ds(h, h), pl.ds(0, n), pl.ds(n, n)
-        right, left, mate = here.to(dx=1), here.to(dx=3), here.mate()
+        lo, hi = pl.ds(0, h), pl.ds(h, h)
+        right, left = here.to(dx=1), here.to(dx=3)
         self.a0.wait_recv()
         self.a2 = copy(full.at[3, lo], full.at[2, lo], right)
         self.b0.wait_recv()
         self.b2 = copy(full.at[1, hi], full.at[2, hi], left)
+
+    def forward(self):
+        full, copy = self.full, self.lines.copy
+        n = self.own.shape[0]
+        both, other = pl.ds(0, n), pl.ds(n, n)
+        mate = self.here.mate()
         self.a1.wait_recv()
         self.f3 = copy(full.at[3, both], full.at[3, other], mate)
         self.b1.wait_recv()
@@ -205,9 +211,9 @@
 
 def mlp_kernel(
     xs_h, middle_h, cot_h, gains, w_gate_h, w_up_h, w_down_h,
-    layer_out, middle_grad, d_gain_in, d_gain_out, d_in_h, half_down,
+    layer_out, middle_grad, d_gain_in, d_gain_out, half_in, d_down_h,
     xs, middle, cot, w_gate, w_up, w_down, d_in, gs, act, slope, hidden, cross_f, cross_b, landed_f, landed_b, stage_core, stage_ring,
-    mine, mixed_grad, d_down, *rest,
+    mine, mixed_grad, d_down, swap, *rest,
 ):
     here = Place()
     moves = Moves(rest[-1])
@@ -223,7 +229,7 @@
     gain_in, gain_out = gains[2:3, :width], gains[3:4, :width]
 
     sums = RingSum(here, lines, mine, landed_f, cross_f, stage_core, stage_ring)
-    down_sum = PlaneSum(here, lines, d_down, *rest[:6])
+    in_sum = PlaneSum(here, lines, d_in, *rest[:8])
 
     def forward(r):
         x = xs[r]
@@ -269,6 +275,7 @@
     ring.ready0()
     backward(0)
     ring.relay()
+    ring.forward()
     ring.ready3()
     backward(3)
     ring.ready1()
@@ -277,6 +284,11 @@
     backward(2)
 
     flat = lambda ref: ref[...].reshape(ref.shape[0] * ref.shape[1], ref.shape[2])
+    for mat, side in ((0, slope), (1, act)):
+        grad_side = dot(flat(xs), flat(side), TN)
+        for f in range(16):
+            d_in[f // 4, (f // 2) % 2, mat, f % 2] = grad_side[72 * f : 72 * f + 72].astype(BF16)
+    in_sum.first()
     grad_down = dot(flat(hidden), flat(gs), TN)
     for k in range(8):
         for p in range(4):
@@ -284,13 +296,8 @@
             at = PART * k + 32 * p
             d_down[k // 2, k % 2, p // 2, p % 2, :rows] = grad_down[at : at + rows].astype(BF16)
         d_down[k // 2, k % 2, 1, 1, PART - 96 :] = jnp.zeros((128 - PART, width), BF16)
-    down_sum.first()
-    for mat, side in ((0, slope), (1, act)):
-        grad_side = dot(flat(xs), flat(side), TN)
-        for f in range(16):
-            d_in[f // 4, (f // 2) % 2, mat, f % 2] = grad_side[72 * f : 72 * f + 72].astype(BF16)
-        moves.store(d_in.at[:, :, mat], d_in_h.at[:, :, mat])
-    down_sum.second()
+    moves.store(d_down, d_down_h)
+    in_sum.middle()
 
     update = sums.total()
     base = middle[...]
@@ -298,8 +305,12 @@
     factor, grad = norm_back(base, u, width)
     d_gain_in[...] = jnp.sum(update * base * factor, axis=0, keepdims=True)
     middle_grad[...] = cot[...].astype(F32) + grad
+    in_sum.second()
     for path in (0, 1):
-        half_down[path] = down_sum.result(path).astype(BF16)
+        swap[path] = in_sum.result(path).astype(BF16)
+    across = lines.copy(swap.at[1 - here.c], half_in.at[here.c], here.mate())
+    half_in[here.c] = swap[here.c]
+    across.wait_recv()
     lines.drain()
     moves.drain()
 
@@ -310,6 +321,7 @@
     vmem, hbm = pl.BlockSpec(memory_space=pltpu.VMEM), pl.BlockSpec(memory_space=pl.ANY)
     shape = jax.ShapeDtypeStruct
     d_in = shape((4, 2, 2, 2, width // 16, units), BF16)
+    d_down = shape((4, 2, 2, 2, 32, width), BF16)
     scratch = (
         [pltpu.VMEM(a.shape, a.dtype) for a in (xs, middle, cot, w_gate, w_up, w_down, d_in)]
         + [pltpu.VMEM((4, 2 * n, width), BF16)]
@@ -318,10 +330,10 @@
         + [pltpu.VMEM((3, n, width), BF16)] * 2
         + [pltpu.VMEM((4, n, width), BF16), pltpu.VMEM((3, n, width), BF16)]
         + [pltpu.VMEM((n, width), F32), pltpu.VMEM((n, width), BF16)]
-        + [pltpu.VMEM((4, 2, 2, 2, 32, width), BF16)]
-        + PlaneSum.scratch((32, width))
-        + [pltpu.SemaphoreType.DMA((36,))] * 2
-        + [pltpu.SemaphoreType.DMA((11,))]
+        + [pltpu.VMEM(d_down.shape, BF16), pltpu.VMEM((2, *d_in.shape[4:]), BF16)]
+        + PlaneSum.scratch(d_in.shape[4:])
+        + [pltpu.SemaphoreType.DMA((43,))] * 2
+        + [pltpu.SemaphoreType.DMA((10,))]
     )
     return pl.pallas_call(
         mlp_kernel,
@@ -330,11 +342,11 @@
             shape((n, width), F32),
             shape((1, width), F32),
             shape((1, width), F32),
-            d_in,
-            shape((2, 32, width), BF16),
+            shape((2, *d_in.shape[4:]), BF16),
+            d_down,
         ),
         in_specs=[hbm] * 3 + [vmem] + [hbm] * 3,
-        out_specs=(vmem,) * 4 + (hbm, vmem),
+        out_specs=(vmem,) * 5 + (hbm,),
         scratch_shapes=scratch,
         compiler_params=pltpu.CompilerParams(
             collective_id=1, has_side_effects=True, vmem_limit_bytes=63 * MIB
@@ -502,11 +514,16 @@
     gather[1].second()
     across.wait_recv()
     gather[2].first()
-    gather[3].first()
     gather[0].wait()
-    core_qkv = lines.copy(full_qkv.at[:, :, c], full_qkv.at[:, :, c], here.mate())
-    core_qkv.wait_recv()
+    core_qkv = [
+        lines.copy(full_qkv.at[:, :, c, k], full_qkv.at[:, :, c, k], here.mate()) for k in (0, 1)
+    ]
     for p in range(4):
+        if p % 2 == 0:
+            core_qkv[p // 2].wait_recv()
+        if p == 1:
+            gather[1].relay()
+            gather[2].second()
         total = jnp.zeros((8, wide), F32)
         cols = slice(p * wide, (p + 1) * wide)
         for f in range(16):
@@ -514,8 +531,6 @@
             w_qkv[rows * f : rows * f + rows, cols] = part[:rows]
             total = total + part.astype(F32)[rows : rows + 8]
         gains[:, cols] = total
-    gather[1].relay()
-    gather[2].second()
     keep(w_qkv)
     normed[...] = (lean * (1.0 + gains[0:1, :width])).astype(BF16)
     qkv_pre[...] = dot(normed[...], w_qkv[...])
@@ -540,6 +555,8 @@
     row = lax.broadcasted_iota(jnp.int32, (n, 2 * n), 0) + yl * n
     allowed = lax.broadcasted_iota(jnp.int32, (n, 2 * n), 1) <= row
     for h in range(heads):
+        if h == 1:
+            gather[3].first()
         cols = slice(h * head_dim, (h + 1) * head_dim)
         scores = jnp.where(allowed, dot(queries[:, cols], keys, NT), -1e30)
         terms = jnp.exp(scores - jnp.max(scores, axis=-1, keepdims=True))
@@ -556,19 +573,20 @@
     mlp_in[...] = (mid * r * (1.0 + gains[2:3, :width])).astype(BF16)
     ring = RingGather(here, lines, mlp_in, xs)
     ring.start()
+    gather[2].relay()
+    gather[3].second()
     for ref in (probs, context, w_out, attended, middle):
         keep(ref)
-    gather[2].relay()
-    gather[3].second()
+    ring.relay()
     gather[2].wait()
     for f in range(16):
         for mat, whole in ((0, gate_full), (1, up_full)):
             whole[rows * f : rows * f + rows] = full_in[f // 4, (f // 2) % 2, mat, f % 2]
     keep(gate_full)
     keep(up_full)
+    ring.forward()
     gather[3].relay()
     ring.ready0()
-    ring.relay()
     gather[3].wait()
     for k in range(8):
         for p in range(4):
@@ -626,8 +644,8 @@
             vm(4, 2, 2, 2, *p_in),
             vm(4, 2, 2, 2, *p_down),
             vm(2, 2, *p_in),
-            pltpu.SemaphoreType.DMA((86,)),
-            pltpu.SemaphoreType.DMA((86,)),
+            pltpu.SemaphoreType.DMA((87,)),
+            pltpu.SemaphoreType.DMA((87,)),
             pltpu.SemaphoreType.DMA((4,)),
             pltpu.SemaphoreType.DMA((14,)),
         ],
@@ -640,35 +658,72 @@
 
 class PlaneSum:
     def __init__(
-        self, here, lines, grads, landed_a, sums_a, landed_b, sums_b, last_a, last_b, held=None
+        self, here, lines, grads, landed_a, half_a, sums_a, landed_b, half_b, sums_b, last_a, last_b
     ):
-        self.here, self.lines, self.grads, self.held = here, lines, grads, held
-        self.landed_a, self.sums_a, self.last_a = landed_a, sums_a, last_a
-        self.landed_b, self.sums_b, self.last_b = landed_b, sums_b, last_b
+        self.here, self.lines, self.grads = here, lines, grads
+        self.landed_a, self.half_a, self.sums_a, self.last_a = landed_a, half_a, sums_a, last_a
+        self.landed_b, self.half_b, self.sums_b, self.last_b = landed_b, half_b, sums_b, last_b
 
     @staticmethod
     def scratch(piece):
         vm = lambda *lead: pltpu.VMEM((*lead, *piece), BF16)
-        return [vm(3, 4), vm(4), vm(3, 2, 2), vm(2, 2), vm(3), vm(3)]
+        return [vm(2, 4), vm(2, 2), vm(4), vm(2, 2, 2), vm(2, 2), vm(2, 2), vm(3), vm(3)]
+
+    def spots(self, d):
+        _, shard, yl = self.here.to(dy=d)
+        yh = lax.rem(shard // 2, 2)
+        z = self.here.to(dz=d)[1] // 4
+        low, high = pl.ds(0, 2), pl.ds(2, 2)
+        return ((low, yh, yl, 0), (high, yh, yl, 0)), ((z, 0, slice(None), 1), (z, 1, slice(None), 1))
 
     def first(self):
         here, g, copy = self.here, self.grads, self.lines.copy
-        self.a, self.b = [], []
-        for d in (1, 3, 2):
-            _, shard, yl = here.to(dy=d)
-            yh = lax.rem(shard // 2, 2)
-            self.a.append(copy(g.at[:, yh, yl, 0], self.landed_a.at[d - 1], here.to(dy=d)))
-            z = here.to(dz=d)[1] // 4
-            self.b.append(copy(g.at[z, :, :, 1], self.landed_b.at[d - 1], here.to(dz=d)))
+        up_y, down_y, up_z, down_z = here.to(dy=1), here.to(dy=3), here.to(dz=1), here.to(dz=3)
+        low, high = pl.ds(0, 2), pl.ds(2, 2)
+        a, b = self.spots(2)
+        self.half = [
+            copy(g.at[a[0]], self.half_a.at[0], up_y),
+            copy(g.at[a[1]], self.half_a.at[1], down_y),
+            copy(g.at[b[0]], self.half_b.at[0], up_z),
+            copy(g.at[b[1]], self.half_b.at[1], down_z),
+        ]
+        (a1, b1), (a3, b3) = self.spots(1), self.spots(3)
+        self.a = [
+            copy(g.at[a1[1]], self.landed_a.at[0, high], up_y),
+            copy(g.at[a3[0]], self.landed_a.at[1, low], down_y),
+        ]
+        self.b = [
+            copy(g.at[b1[1]], self.landed_b.at[0, 1], up_z),
+            copy(g.at[b3[0]], self.landed_b.at[1, 0], down_z),
+        ]
+
+    def middle(self):
+        here, g, copy = self.here, self.grads, self.lines.copy
+        low, high = pl.ds(0, 2), pl.ds(2, 2)
+        (a1, b1), (a3, b3) = self.spots(1), self.spots(3)
+        for made, spot, half in zip(
+            self.half,
+            (a1[0], a3[1], b1[0], b3[1]),
+            (self.half_a.at[0], self.half_a.at[1], self.half_b.at[0], self.half_b.at[1]),
+        ):
+            made.wait_recv()
+            g[spot] = (g[spot].astype(F32) + half[...].astype(F32)).astype(BF16)
+        self.a += [
+            copy(g.at[a1[0]], self.landed_a.at[0, low], here.to(dy=1)),
+            copy(g.at[a3[1]], self.landed_a.at[1, high], here.to(dy=3)),
+        ]
+        self.b += [
+            copy(g.at[b1[0]], self.landed_b.at[0, 0], here.to(dz=1)),
+            copy(g.at[b3[1]], self.landed_b.at[1, 1], here.to(dz=3)),
+        ]
 
     def second(self):
         here, g, copy = self.here, self.grads, self.lines.copy
         for made in self.a:
             made.wait_recv()
         for k in range(4):
-            own = self.held[0][k] if self.held else g[k, here.yh, here.yl, 0]
-            total = own.astype(F32)
-            for j in range(3):
+            total = g[k, here.yh, here.yl, 0].astype(F32)
+            for j in range(2):
                 total = total + self.landed_a[j, k].astype(F32)
             self.sums_a[k] = total.astype(BF16)
         self.a = []
@@ -678,9 +733,8 @@
         for made in self.b:
             made.wait_recv()
         for k in range(4):
-            own = self.held[1][k // 2, k % 2] if self.held else g[here.z, k // 2, k % 2, 1]
-            total = own.astype(F32)
-            for j in range(3):
+            total = g[here.z, k // 2, k % 2, 1].astype(F32)
+            for j in range(2):
                 total = total + self.landed_b[j, k // 2, k % 2].astype(F32)
             self.sums_b[k // 2, k % 2] = total.astype(BF16)
         self.b = []
@@ -703,12 +757,12 @@
 
 def retreat_kernel(
     middle_grad_h, attended_h, context_h, probs_h, kv_h, queries_h, qkv_pre_h, normed_h, tokens_h,
-    w_qkv_h, w_out_h, g_in, cosine, sine, gains, d_gain_in, d_gain_out, half_down,
+    w_qkv_h, w_out_h, g_down_h, cosine, sine, gains, d_gain_in, d_gain_out, half_in,
     grad_tokens, o_in, o_down, o_qkv, o_out,
     middle_grad, attended, context, probs, kv, queries, qkv_pre, normed, tokens, w_qkv, w_out,
-    held_a, held_b,
+    g_down,
     context_grad, attn_side, kv_part, kv_give, kv_land, g_qkv, g_out, d_gains,
-    chip_qkv, chip_out, cross_qkv, cross_out, swap, half_qkv, half_out, land_qkv, land_out, *rest,
+    chip_qkv, chip_out, cross_qkv, cross_out, half_qkv, half_out, land_qkv, land_out, *rest,
 ):
     here = Place()
     send, recv, moved = rest[-3:]
@@ -717,6 +771,7 @@
     loads = {
         name: moves.start(a, b)
         for name, a, b in (
+            ("g_down", g_down_h, g_down),
             ("attended", attended_h, attended),
             ("middle_grad", middle_grad_h, middle_grad),
             ("w_out", w_out_h, w_out),
@@ -728,8 +783,6 @@
             ("w_qkv", w_qkv_h, w_qkv),
             ("normed", normed_h, normed),
             ("tokens", tokens_h, tokens),
-            ("held_a", g_in.at[:, here.yh, yl, 0], held_a),
-            ("held_b", g_in.at[here.z, :, :, 1], held_b),
         )
     }
 
@@ -746,12 +799,13 @@
     rows = width // 16
     at = heads * head_dim
     sums = [
-        PlaneSum(here, lines, g, *rest[6 * k : 6 * k + 6], held)
-        for k, (g, held) in enumerate(((g_in, (held_a, held_b)), (chip_qkv, None), (chip_out, None)))
+        PlaneSum(here, lines, g, *rest[8 * k : 8 * k + 8])
+        for k, g in enumerate((g_down, chip_qkv, chip_out))
     ]
+    o_in[x, yl] = half_in[...]
+    in_pair = copy(half_in, o_in.at[x, yl], here.pair())
+    ready("g_down")
     sums[0].first()
-    o_down[x, yl] = half_down[...]
-    down_pair = copy(half_down, o_down.at[x, yl], here.pair())
     ready("attended", "middle_grad", "w_out", "context")
 
     att, dy = attended[...], middle_grad[...]
@@ -766,8 +820,12 @@
     grad_out = dot(context[...], attended_grad, TN)
     g_out[...] = grad_out.astype(BF16).reshape(g_out.shape)
     give_out = copy(g_out.at[:, :, 1 - c], cross_out, here.mate())
-    down_pair.wait_recv()
-    down_x = [copy(o_down.at[x], o_down.at[x], here.to(dx=d)) for d in (1, 3, 2)]
+    in_pair.wait_recv()
+    right, left = here.to(dx=1), here.to(dx=3)
+    own = [o_in.at[x, m] for m in (0, 1)]
+    early = [copy(own[0], own[0], right), copy(own[1], own[1], left)]
+    late = [copy(own[1], own[1], right), copy(own[0], own[0], left)]
+    sums[0].middle()
 
     ready("probs", "kv", "queries", "qkv_pre")
     keys = kv[:, :, :head_dim].reshape(2 * n, head_dim)
@@ -803,6 +861,7 @@
         for yh in range(2):
             chip_out[z, yh] = (g_out[z, yh, c].astype(F32) + cross_out[z, yh].astype(F32)).astype(BF16)
     sums[2].first()
+    sums[0].second()
     kv_sent.wait_recv()
     kv_grad = (kv_part[yl] + kv_land[...].astype(F32)).astype(BF16)
     side, d_key = head_backward(
@@ -813,7 +872,7 @@
     d_gains[0:1, width : width + head_dim] = d_query
     d_gains[1:2, width : width + head_dim] = d_key
 
-    ready("w_qkv", "normed", "tokens", "held_a", "held_b")
+    ready("w_qkv", "normed", "tokens")
     normed_grad = dot(attn_side[...], w_qkv[...], NT)
     tok = tokens[...].astype(F32)
     r, grad = norm_back(tok, normed_grad * (1.0 + gains[0:1, :width]), width)
@@ -831,31 +890,26 @@
             g_qkv[spot] = block.astype(BF16)
     give_qkv = copy(g_qkv.at[:, :, 1 - c], cross_qkv, here.mate())
 
-    sums[0].second()
+    for made, at_x, m, to in ((early[0], left[0], 0, right), (early[1], right[0], 1, left)):
+        made.wait_recv()
+        late.append(copy(o_in.at[at_x, m], o_in.at[at_x, m], to))
     give_qkv.wait_recv()
     for z in range(4):
         for yh in range(2):
             chip_qkv[z, yh] = (g_qkv[z, yh, c].astype(F32) + cross_qkv[z, yh].astype(F32)).astype(BF16)
     sums[1].first()
+    for path in (0, 1):
+        o_down[x, yl, path] = sums[0].result(path).astype(BF16)
+    down_pair = copy(o_down.at[x, yl], o_down.at[x, yl], here.pair())
+    sums[2].middle()
+    sums[1].middle()
+    down_pair.wait_recv()
+    down_x = [copy(o_down.at[x], o_down.at[x], here.to(dx=d)) for d in (1, 3, 2)]
     sums[2].second()
-    swap[0] = sums[0].result(0).astype(BF16)
-    swap[1] = sums[0].result(1).astype(BF16)
-    across = copy(swap.at[1 - c], o_in.at[x, yl, c], here.mate())
-    o_in[x, yl, c] = swap[c]
-    across.wait_recv()
-    in_pair = copy(o_in.at[x, yl], o_in.at[x, yl], here.pair())
     for path in (0, 1):
         half_out[path] = sums[2].result(path).astype(BF16)
     by_x = [copy(half_out, land_out.at[d - 1], here.to(dx=d)) for d in (1, 3, 2)]
-    in_pair.wait_recv()
-    right, left = here.to(dx=1), here.to(dx=3)
-    own = [o_in.at[x, m] for m in (0, 1)]
-    early = [copy(own[0], own[0], right), copy(own[1], own[1], left)]
-    late = [copy(own[1], own[1], right), copy(own[0], own[0], left)]
     sums[1].second()
-    for made, at_x, m, to in ((early[0], left[0], 0, right), (early[1], right[0], 1, left)):
-        made.wait_recv()
-        late.append(copy(o_in.at[at_x, m], o_in.at[at_x, m], to))
     for path in (0, 1):
         half_qkv[path] = sums[1].result(path).astype(BF16)
     by_x += [copy(half_qkv, land_qkv.at[d - 1], here.to(dx=d)) for d in (1, 3, 2)]
@@ -876,26 +930,26 @@
 def retreat_block(*args):
     (
         middle_grad, attended, context, probs, kv, queries, qkv_pre, normed, tokens, w_qkv, w_out,
-        g_in, cosine, _, _, _, _, half_down,
+        g_down, cosine, _, _, _, _, half_in,
     ) = args
     vmem, hbm = pl.BlockSpec(memory_space=pltpu.VMEM), pl.BlockSpec(memory_space=pl.ANY)
     shape = jax.ShapeDtypeStruct
     n, width = middle_grad.shape
     out_width, head_dim = queries.shape[1], 2 * cosine.shape[1]
     cols = qkv_pre.shape[1]
-    p_in, p_down, p_out = g_in.shape[4:], half_down.shape[1:], w_out.shape[5:]
+    p_in, p_down, p_out = half_in.shape[1:], g_down.shape[4:], w_out.shape[5:]
     p_qkv = (width // 16 + 8, cols // 4)
     vm = lambda *s: pltpu.VMEM(s, BF16)
     scratch = [pltpu.VMEM(a.shape, a.dtype) for a in args[:11]]
-    scratch += [vm(4, *p_in), vm(2, 2, *p_in)]
+    scratch += [vm(*g_down.shape)]
     scratch += [vm(n, out_width), vm(n, cols), pltpu.VMEM((2, n, 2 * head_dim), F32)]
     scratch += [vm(n, 2 * head_dim)] * 2
     scratch += [vm(4, 2, 2, 2, 2, *p_qkv), vm(4, 2, 2, 2, 2, *p_out), pltpu.VMEM((8, cols), F32)]
     scratch += [vm(4, 2, 2, 2, *p_qkv), vm(4, 2, 2, 2, *p_out)] * 2
-    scratch += [vm(2, *p_in), vm(2, *p_qkv), vm(2, *p_out), vm(3, 2, *p_qkv), vm(3, 2, *p_out)]
-    for piece in (p_in, p_qkv, p_out):
+    scratch += [vm(2, *p_qkv), vm(2, *p_out), vm(3, 2, *p_qkv), vm(3, 2, *p_out)]
+    for piece in (p_down, p_qkv, p_out):
         scratch += PlaneSum.scratch(piece)
-    scratch += [pltpu.SemaphoreType.DMA((60,))] * 2 + [pltpu.SemaphoreType.DMA((13,))]
+    scratch += [pltpu.SemaphoreType.DMA((76,))] * 2 + [pltpu.SemaphoreType.DMA((12,))]
     low = lambda *s: shape(s, BF16)
     return pl.pallas_call(
         retreat_kernel,
@@ -917,26 +971,42 @@
 
 
 def finish_kernel(
-    o_in, o_down, o_qkv, o_out, shown, taken,
-    layer_out, grad_tokens, out_query, out_key, out_value, out_out, out_gate, out_up, out_down,
-    *out_gains,
+    o_in_h, o_down_h, o_qkv_h, o_out_h, shown_h, taken_h,
+    layer_out_h, grad_tokens_h, out_query, out_key, out_value, out_out, out_gate_h, out_up_h, out_down_h,
+    *rest,
 ):
+    out_gains = rest[:6]
+    o_in, o_down, o_qkv, o_out, out_gate, out_up, out_down, shown, taken, moved = rest[6:]
+    moves = Moves(moved)
+    load_in = [moves.start(o_in_h.at[:, m], o_in.at[:, m]) for m in (0, 1)]
+    load_tokens = [moves.start(shown_h, shown), moves.start(taken_h, taken)]
+    load_down = moves.start(o_down_h, o_down)
+    load_rest = [moves.start(o_qkv_h, o_qkv), moves.start(o_out_h, o_out)]
     rows, units = out_gate.shape
     block = units // 16
     wide = o_qkv.shape[-1]
     at, head_dim = out_query.shape[1], out_key.shape[1]
-    for m, out in ((0, out_gate), (1, out_up)):
+    for m, out, out_h in ((0, out_gate, out_gate_h), (1, out_up, out_up_h)):
+        load_in[m].wait()
         for k in range(4):
             count = min(PART, block - PART * k)
             for f in range(16):
                 piece = o_in[k, m, f % 2].astype(F32)[:, PART * (f // 2) : PART * (f // 2) + count]
                 out[:, block * f + PART * k : block * f + PART * k + count] = piece
+        moves.store(out, out_h)
+    for made, held, out_h in zip(load_tokens, (shown, taken), (layer_out_h, grad_tokens_h)):
+        made.wait()
+        moves.store(held, out_h)
+    load_down.wait()
     for k in range(4):
         for p in range(4):
             start = PART * k + 32 * p
             count = min(32, PART - 32 * p, block - start)
             if count > 0:
                 out_down[start : start + count] = o_down[k, p // 2, p % 2, :count].astype(F32)
+    moves.store(out_down, out_down_h)
+    for made in load_rest:
+        made.wait()
     tail = []
     for p in range(4):
         piece = o_qkv[p // 2, p % 2].astype(F32)
@@ -948,7 +1018,7 @@
         height = o_out.shape[2]
         out_out[p * height : (p + 1) * height] = o_out[p // 2, p % 2].astype(F32)
     tail = jnp.concatenate(tail, axis=1)
-    width = layer_out.shape[1]
+    width = out_out.shape[1]
     shard = lax.axis_index("fsdp")
     turned = pltpu.roll(tail[:, :width], lax.rem(width - rows * shard, width), 1)
     for k in range(4):
@@ -957,18 +1027,20 @@
     turned = pltpu.roll(tail[:, width : width + head_dim], lax.rem(head_dim - piece * shard, head_dim), 1)
     for k in range(2):
         out_gains[4 + k][...] = turned[k, :piece]
-    layer_out[...] = shown[...]
-    grad_tokens[...] = taken[...]
+    moves.drain()
 
 
 def finish_block(o_in, o_down, o_qkv, o_out, layer_out, grad_tokens, out_shape):
-    vmem = pl.BlockSpec(memory_space=pltpu.VMEM)
+    vmem, hbm = pl.BlockSpec(memory_space=pltpu.VMEM), pl.BlockSpec(memory_space=pl.ANY)
+    big = out_shape[6:9]
     return pl.pallas_call(
         finish_kernel,
         out_shape=out_shape,
-        in_specs=[vmem] * 6,
-        out_specs=(vmem,) * len(out_shape),
-        compiler_params=pltpu.CompilerParams(vmem_limit_bytes=48 * MIB),
+        in_specs=[hbm] * 6,
+        out_specs=(hbm,) * 2 + (vmem,) * 4 + (hbm,) * 3 + (vmem,) * 6,
+        scratch_shapes=[pltpu.VMEM(a.shape, a.dtype) for a in (o_in, o_down, o_qkv, o_out, *big, layer_out, grad_tokens)]
+        + [pltpu.SemaphoreType.DMA((12,))],
+        compiler_params=pltpu.CompilerParams(vmem_limit_bytes=62 * MIB),
         name="finish",
     )(o_in, o_down, o_qkv, o_out, layer_out, grad_tokens)
 
@@ -1021,12 +1093,12 @@
     ) = attend_block(
         tokens, cosine, sine, tail, w_query, w_key, w_value, own_out, w_gate, w_up, w_down
     )
-    layer_out, middle_grad, d_gain_in, d_gain_out, g_in, half_down = mlp_block(
+    layer_out, middle_grad, d_gain_in, d_gain_out, half_in, g_down = mlp_block(
         xs, middle, cotangent, gains, gate_full, up_full, down_full
     )
     grad_tokens, o_in, o_down, o_qkv, o_out = retreat_block(
         middle_grad, attended, context, probs, kv, queries, qkv_pre, normed, tokens, w_qkv,
-        w_out_full, g_in, cosine, sine, gains, d_gain_in, d_gain_out, half_down,
+        w_out_full, g_down, cosine, sine, gains, d_gain_in, d_gain_out, half_in,
     )
     like = lambda a, kind: jax.ShapeDtypeStruct(a.shape, kind)
     weights = (w_query, w_key, w_value, w_out, w_gate, w_up, w_down)

time: 303 us -> 286 us (0.944)
  Pallas kernels: 289 us -> 275 us
  local copies, waits for them, and re-layouts: 6.32 us -> 0.56 us
    pallas_call x1, Pallas kernels: 101 us -> 74.7 us  [retreat_block(): pl.pallas_call(retreat_kernel, out_shape=(low(n, width), low(4, 2, 2, *p_...]
    pallas_call x1, Pallas kernels: 104 us -> 116 us  [mlp_block(): pl.pallas_call(mlp_kernel, out_shape=(shape((n, width), BF16), shape((n,...]
    unnamed x12 -> x0, local copies, waits for them, and re-layouts: 5.76 us -> none
where the time goes in v4:
time: 286 us; the launch traced here: 280 us
  Pallas kernels  275 us (96%)
  other arithmetic  3.45 us (1%)
    pallas_call x1, Pallas kernels, mlp_block(): pl.pallas_call(mlp_kernel, out_shape=(shape((n, width), BF16), shape((n,...  116 us
    pallas_call x1, Pallas kernels, attend_block(): pl.pallas_call(attend_kernel, out_shape=held + (shape((8, cols), F32),),...  78.8 us
    pallas_call x1, Pallas kernels, retreat_block(): pl.pallas_call(retreat_kernel, out_shape=(low(n, width), low(4, 2, 2, *p_...  74.7 us

profile of v4, /device:TPU:0, one launch (start us, length us, event | category | flops | bytes accessed | tf_op | source)
XLA Modules:
  0.0 280.5 jit_solution(3434174895481547074)
XLA Ops:
  0.7 0.7 broadcast_select_fusion.1
  1.4 0.1 select_n.89
  1.5 0.1 select_n.91
  1.6 0.8 broadcast_select_fusion.5
  2.4 0.1 select_n.81
  2.5 0.1 select_n.83
  2.6 0.1 select_n.85
  2.7 0.1 select_n.87
  2.9 0.6 pad_maximum_fusion.tail
  3.5 1.2 multiply_sine_fusion
  4.7 78.8 %attend.1 = (bf16[4,512,1152]{2,1,0:T(8,128)(2,1)}, bf16[1152,896]{1,0:T(8,128)(2,1)}, bf16[1152,896]{1,0:T(8,128)(2,1)}, bf16[896,1152]{1,0:T(8,128)(2,1)}, bf1...) custom-call(bf16[256,1152]{1,0:T(8,128)(2,1)} %tokens_h.1, ...), custom_call_target="tpu_custom_call" | custom-call | tf_op jit(solution)/shard_map/attend/pallas_call | solution.py:632
  83.5 116.1 %mlp_block.1 = (bf16[256,1152]{1,0:T(8,128)(2,1)}, f32[256,1152]{1,0:T(8,128)}, f32[1,1152]{1,0:T(1,128)}, f32[1,1152]{1,0:T(1,128)}, bf16[2,72,896]{2,1,0:T(8,1...) custom-call(bf16[4,512,1152]{2,1,0:T(8,128)(2,1)} %get-tuple-element.41.xs_h, f32[256,1152]{1,0:T(8,128)} %get-tuple-element.42.middle_h, ...), custom_call_target="tpu_custom_call" | custom-call | tf_op jit(solution)/shard_map/mlp_block/pallas_call | solution.py:338
  199.6 74.7 %retreat.1 = (bf16[256,1152]{1,0:T(8,128)(2,1)}, bf16[4,2,2,72,896]{4,3,2,1,0:T(8,128)(2,1)}, bf16[4,2,2,32,1152]{4,3,2,1,0:T(8,128)(2,1)}, bf16[2,2,80,384]{3,2,1,0:T(8,128)(2,1)}, bf16[2,2,16,1152]{3,2,1,0:T(8,128)(2,1)}) custom-call(f32[256,1152]{1,0:T(8,128)} %get-tuple-element.47.middle_grad_h, f32[256,1152]{1,0:T(8,128)} %get-tuple-element.48.attended_h, ...), custom_call_target="tpu_custom_call" | custom-call | tf_op jit(solution)/shard_map/retreat/pallas_call | solution.py:954
  274.3 5.7 %finish.1 = (bf16[256,1152]{1,0:T(8,128)(2,1)}, bf16[256,1152]{1,0:T(8,128)(2,1)}, f32[72,1024]{1,0:T(8,128)}, f32[72,256]{1,0:T(8,128)}, f32[72,256]{1,0:T(8,12...) custom-call(bf16[4,2,2,72,896]{4,3,2,1,0:T(8,128)(2,1)} %get-tuple-e, ...), custom_call_target="tpu_custom_call" | custom-call | tf_op jit(solution)/shard_map/finish/pallas_call | solution.py:1036
  (5 shorter events, 0.1 us)

commit v5 on v4

--- a/solution.py
+++ b/solution.py
@@ -128,6 +128,21 @@
         self.b0 = copy(own.at[hi], full.at[1, hi], left)
         self.a1 = copy(own.at[hi], full.at[3, hi], right)
         self.b1 = copy(own.at[lo], full.at[1, lo], left)
+        full[0, :n] = own[...]
+
+    def start_low(self):
+        here, own, full, copy = self.here, self.own, self.full, self.lines.copy
+        lo = pl.ds(0, own.shape[0] // 2)
+        self.a0 = copy(own.at[lo], full.at[3, lo], here.to(dx=1))
+        self.b1 = copy(own.at[lo], full.at[1, lo], here.to(dx=3))
+
+    def start_high(self):
+        here, own, full, copy = self.here, self.own, self.full, self.lines.copy
+        n = own.shape[0]
+        hi = pl.ds(n // 2, n // 2)
+        self.b0 = copy(own.at[hi], full.at[1, hi], here.to(dx=3))
+        self.a1 = copy(own.at[hi], full.at[3, hi], here.to(dx=1))
+        self.core = copy(own, full.at[0, pl.ds(n, n)], here.mate())
         full[0, :n] = own[...]
 
     def ready0(self):
@@ -211,9 +226,10 @@
 
 def mlp_kernel(
     xs_h, middle_h, cot_h, gains, w_gate_h, w_up_h, w_down_h,
-    layer_out, middle_grad, d_gain_in, d_gain_out, half_in, d_down_h,
+    layer_out, middle_grad, d_gain_in, d_gain_out, half_a, half_b, near_a, near_b,
+    down_half_a, down_half_b, down_near_a, down_near_b, d_in_h, d_down_h,
     xs, middle, cot, w_gate, w_up, w_down, d_in, gs, act, slope, hidden, cross_f, cross_b, landed_f, landed_b, stage_core, stage_ring,
-    mine, mixed_grad, d_down, swap, *rest,
+    mine, mixed_grad, d_down, *rest,
 ):
     here = Place()
     moves = Moves(rest[-1])
@@ -229,7 +245,8 @@
     gain_in, gain_out = gains[2:3, :width], gains[3:4, :width]
 
     sums = RingSum(here, lines, mine, landed_f, cross_f, stage_core, stage_ring)
-    in_sum = PlaneSum(here, lines, d_in, *rest[:8])
+    in_sum = PlaneSum(here, lines, d_in, *[None] * 8)
+    down_sum = PlaneSum(here, lines, d_down, *[None] * 8)
 
     def forward(r):
         x = xs[r]
@@ -284,11 +301,6 @@
     backward(2)
 
     flat = lambda ref: ref[...].reshape(ref.shape[0] * ref.shape[1], ref.shape[2])
-    for mat, side in ((0, slope), (1, act)):
-        grad_side = dot(flat(xs), flat(side), TN)
-        for f in range(16):
-            d_in[f // 4, (f // 2) % 2, mat, f % 2] = grad_side[72 * f : 72 * f + 72].astype(BF16)
-    in_sum.first()
     grad_down = dot(flat(hidden), flat(gs), TN)
     for k in range(8):
         for p in range(4):
@@ -296,8 +308,19 @@
             at = PART * k + 32 * p
             d_down[k // 2, k % 2, p // 2, p % 2, :rows] = grad_down[at : at + rows].astype(BF16)
         d_down[k // 2, k % 2, 1, 1, PART - 96 :] = jnp.zeros((128 - PART, width), BF16)
+    down_sum.begin(
+        down_half_a, down_half_b, [down_near_a.at[0], down_near_a.at[1]],
+        [down_near_b.at[0], down_near_b.at[1]],
+    )
     moves.store(d_down, d_down_h)
-    in_sum.middle()
+    for mat, side in ((0, slope), (1, act)):
+        grad_side = dot(flat(xs), flat(side), TN)
+        for f in range(16):
+            d_in[f // 4, (f // 2) % 2, mat, f % 2] = grad_side[72 * f : 72 * f + 72].astype(BF16)
+    in_sum.begin(
+        half_a, half_b, [near_a.at[0], near_a.at[1]], [near_b.at[0], near_b.at[1]]
+    )
+    moves.store(d_in, d_in_h)
 
     update = sums.total()
     base = middle[...]
@@ -305,12 +328,8 @@
     factor, grad = norm_back(base, u, width)
     d_gain_in[...] = jnp.sum(update * base * factor, axis=0, keepdims=True)
     middle_grad[...] = cot[...].astype(F32) + grad
-    in_sum.second()
-    for path in (0, 1):
-        swap[path] = in_sum.result(path).astype(BF16)
-    across = lines.copy(swap.at[1 - here.c], half_in.at[here.c], here.mate())
-    half_in[here.c] = swap[here.c]
-    across.wait_recv()
+    down_sum.begun()
+    in_sum.begun()
     lines.drain()
     moves.drain()
 
@@ -330,10 +349,9 @@
         + [pltpu.VMEM((3, n, width), BF16)] * 2
         + [pltpu.VMEM((4, n, width), BF16), pltpu.VMEM((3, n, width), BF16)]
         + [pltpu.VMEM((n, width), F32), pltpu.VMEM((n, width), BF16)]
-        + [pltpu.VMEM(d_down.shape, BF16), pltpu.VMEM((2, *d_in.shape[4:]), BF16)]
-        + PlaneSum.scratch(d_in.shape[4:])
-        + [pltpu.SemaphoreType.DMA((43,))] * 2
-        + [pltpu.SemaphoreType.DMA((10,))]
+        + [pltpu.VMEM(d_down.shape, BF16)]
+        + [pltpu.SemaphoreType.DMA((40,))] * 2
+        + [pltpu.SemaphoreType.DMA((11,))]
     )
     return pl.pallas_call(
         mlp_kernel,
@@ -342,11 +360,13 @@
             shape((n, width), F32),
             shape((1, width), F32),
             shape((1, width), F32),
-            shape((2, *d_in.shape[4:]), BF16),
+            *[shape((2, 2, *d_in.shape[4:]), BF16)] * 4,
+            *[shape((2, 2, *d_down.shape[4:]), BF16)] * 4,
+            d_in,
             d_down,
         ),
         in_specs=[hbm] * 3 + [vmem] + [hbm] * 3,
-        out_specs=(vmem,) * 5 + (hbm,),
+        out_specs=(vmem,) * 12 + (hbm,) * 2,
         scratch_shapes=scratch,
         compiler_params=pltpu.CompilerParams(
             collective_id=1, has_side_effects=True, vmem_limit_bytes=63 * MIB
@@ -523,7 +543,6 @@
             core_qkv[p // 2].wait_recv()
         if p == 1:
             gather[1].relay()
-            gather[2].second()
         total = jnp.zeros((8, wide), F32)
         cols = slice(p * wide, (p + 1) * wide)
         for f in range(16):
@@ -540,6 +559,7 @@
     kv[yl, :, :head_dim] = key
     kv[yl, :, head_dim:] = qkv_pre[:, at + head_dim :].astype(BF16)
     kv_sent = lines.copy(kv.at[yl], kv.at[yl], here.pair())
+    gather[2].second()
     keep(normed)
     keep(qkv_pre)
     for h in range(heads):
@@ -552,27 +572,34 @@
     keep(kv)
     keys = kv[:, :, :head_dim].reshape(2 * n, head_dim)
     values = kv[:, :, head_dim:].reshape(2 * n, head_dim)
-    row = lax.broadcasted_iota(jnp.int32, (n, 2 * n), 0) + yl * n
-    allowed = lax.broadcasted_iota(jnp.int32, (n, 2 * n), 1) <= row
-    for h in range(heads):
-        if h == 1:
-            gather[3].first()
-        cols = slice(h * head_dim, (h + 1) * head_dim)
-        scores = jnp.where(allowed, dot(queries[:, cols], keys, NT), -1e30)
-        terms = jnp.exp(scores - jnp.max(scores, axis=-1, keepdims=True))
-        low = (terms * (1.0 / jnp.sum(terms, axis=-1, keepdims=True))).astype(BF16)
-        probs[h] = low
-        context[:, cols] = dot(low, values).astype(BF16)
-    core_out.wait_recv()
-    att = dot(context[...], w_out[...].reshape(at, width))
-    attended[...] = att
-    r = lax.rsqrt(jnp.mean(att * att, axis=-1, keepdims=True) + EPS)
-    mid = x + att * r * (1.0 + gains[1:2, :width])
-    middle[...] = mid
-    r = lax.rsqrt(jnp.mean(mid * mid, axis=-1, keepdims=True) + EPS)
-    mlp_in[...] = (mid * r * (1.0 + gains[2:3, :width])).astype(BF16)
     ring = RingGather(here, lines, mlp_in, xs)
-    ring.start()
+    half = n // 2
+    for part in range(2):
+        spot = slice(part * half, (part + 1) * half)
+        row = lax.broadcasted_iota(jnp.int32, (half, 2 * n), 0) + (yl * n + part * half)
+        allowed = lax.broadcasted_iota(jnp.int32, (half, 2 * n), 1) <= row
+        for h in range(heads):
+            if part == 0 and h == 2:
+                gather[3].first()
+            cols = slice(h * head_dim, (h + 1) * head_dim)
+            scores = jnp.where(allowed, dot(queries[spot, cols], keys, NT), -1e30)
+            terms = jnp.exp(scores - jnp.max(scores, axis=-1, keepdims=True))
+            low = (terms * (1.0 / jnp.sum(terms, axis=-1, keepdims=True))).astype(BF16)
+            probs[h, spot] = low
+            context[spot, cols] = dot(low, values).astype(BF16)
+        if part == 0:
+            core_out.wait_recv()
+        att = dot(context[spot, :], w_out[...].reshape(at, width))
+        attended[spot, :] = att
+        r = lax.rsqrt(jnp.mean(att * att, axis=-1, keepdims=True) + EPS)
+        mid = x[spot] + att * r * (1.0 + gains[1:2, :width])
+        middle[spot, :] = mid
+        r = lax.rsqrt(jnp.mean(mid * mid, axis=-1, keepdims=True) + EPS)
+        mlp_in[spot, :] = (mid * r * (1.0 + gains[2:3, :width])).astype(BF16)
+        if part == 0:
+            ring.start_low()
+        else:
+            ring.start_high()
     gather[2].relay()
     gather[3].second()
     for ref in (probs, context, w_out, attended, middle):
@@ -677,36 +704,59 @@
         return ((low, yh, yl, 0), (high, yh, yl, 0)), ((z, 0, slice(None), 1), (z, 1, slice(None), 1))
 
     def first(self):
+        low, high = pl.ds(0, 2), pl.ds(2, 2)
+        self.begin(
+            self.half_a,
+            self.half_b,
+            [self.landed_a.at[0, high], self.landed_a.at[1, low]],
+            [self.landed_b.at[0, 1], self.landed_b.at[1, 0]],
+        )
+
+    def begin(self, half_a, half_b, near_a, near_b):
         here, g, copy = self.here, self.grads, self.lines.copy
         up_y, down_y, up_z, down_z = here.to(dy=1), here.to(dy=3), here.to(dz=1), here.to(dz=3)
-        low, high = pl.ds(0, 2), pl.ds(2, 2)
         a, b = self.spots(2)
         self.half = [
-            copy(g.at[a[0]], self.half_a.at[0], up_y),
-            copy(g.at[a[1]], self.half_a.at[1], down_y),
-            copy(g.at[b[0]], self.half_b.at[0], up_z),
-            copy(g.at[b[1]], self.half_b.at[1], down_z),
+            copy(g.at[a[0]], half_a.at[0], up_y),
+            copy(g.at[a[1]], half_a.at[1], down_y),
+            copy(g.at[b[0]], half_b.at[0], up_z),
+            copy(g.at[b[1]], half_b.at[1], down_z),
         ]
         (a1, b1), (a3, b3) = self.spots(1), self.spots(3)
+        self.a = [copy(g.at[a1[1]], near_a[0], up_y), copy(g.at[a3[0]], near_a[1], down_y)]
+        self.b = [copy(g.at[b1[1]], near_b[0], up_z), copy(g.at[b3[0]], near_b[1], down_z)]
+
+    def begun(self):
+        for made in self.half + self.a + self.b:
+            made.wait_recv()
+
+    def resume(self, moves, half_a, half_b, near_a, near_b):
+        low, high = pl.ds(0, 2), pl.ds(2, 2)
+        self.half = [moves.start(half_a, self.half_a), moves.start(half_b, self.half_b)]
         self.a = [
-            copy(g.at[a1[1]], self.landed_a.at[0, high], up_y),
-            copy(g.at[a3[0]], self.landed_a.at[1, low], down_y),
+            moves.start(near_a.at[0], self.landed_a.at[0, high]),
+            moves.start(near_a.at[1], self.landed_a.at[1, low]),
         ]
         self.b = [
-            copy(g.at[b1[1]], self.landed_b.at[0, 1], up_z),
-            copy(g.at[b3[0]], self.landed_b.at[1, 0], down_z),
+            moves.start(near_b.at[0], self.landed_b.at[0, 1]),
+            moves.start(near_b.at[1], self.landed_b.at[1, 0]),
         ]
+
+    def resumed(self):
+        for made in self.half + self.a + self.b:
+            made.wait()
+        self.half, self.a, self.b = [], [], []
 
     def middle(self):
         here, g, copy = self.here, self.grads, self.lines.copy
         low, high = pl.ds(0, 2), pl.ds(2, 2)
         (a1, b1), (a3, b3) = self.spots(1), self.spots(3)
-        for made, spot, half in zip(
-            self.half,
+        for made in self.half:
+            made.wait_recv()
+        for spot, half in zip(
             (a1[0], a3[1], b1[0], b3[1]),
             (self.half_a.at[0], self.half_a.at[1], self.half_b.at[0], self.half_b.at[1]),
         ):
-            made.wait_recv()
             g[spot] = (g[spot].astype(F32) + half[...].astype(F32)).astype(BF16)
         self.a += [
             copy(g.at[a1[0]], self.landed_a.at[0, low], here.to(dy=1)),
@@ -757,21 +807,32 @@
 
 def retreat_kernel(
     middle_grad_h, attended_h, context_h, probs_h, kv_h, queries_h, qkv_pre_h, normed_h, tokens_h,
-    w_qkv_h, w_out_h, g_down_h, cosine, sine, gains, d_gain_in, d_gain_out, half_in,
+    w_qkv_h, w_out_h, g_down_h, g_in_h, half_a, half_b, near_a, near_b,
+    down_half_a, down_half_b, down_near_a, down_near_b,
+    cosine, sine, gains, d_gain_in, d_gain_out,
     grad_tokens, o_in, o_down, o_qkv, o_out,
     middle_grad, attended, context, probs, kv, queries, qkv_pre, normed, tokens, w_qkv, w_out,
-    g_down,
+    g_down, g_in,
     context_grad, attn_side, kv_part, kv_give, kv_land, g_qkv, g_out, d_gains,
-    chip_qkv, chip_out, cross_qkv, cross_out, half_qkv, half_out, land_qkv, land_out, *rest,
+    chip_qkv, chip_out, cross_qkv, cross_out, swap, half_qkv, half_out, land_qkv, land_out, *rest,
 ):
     here = Place()
     send, recv, moved = rest[-3:]
     x, yl, c = here.x, here.yl, here.c
     moves = Moves(moved)
-    loads = {
+    lines = Lines(send, recv)
+    copy = lines.copy
+    sums = [
+        PlaneSum(here, lines, g, *rest[8 * k : 8 * k + 8])
+        for k, g in enumerate((g_down, chip_qkv, chip_out, g_in))
+    ]
+    loads = {"g_in": moves.start(g_in_h, g_in)}
+    sums[3].resume(moves, half_a, half_b, near_a, near_b)
+    loads["g_down"] = moves.start(g_down_h, g_down)
+    sums[0].resume(moves, down_half_a, down_half_b, down_near_a, down_near_b)
+    loads |= {
         name: moves.start(a, b)
         for name, a, b in (
-            ("g_down", g_down_h, g_down),
             ("attended", attended_h, attended),
             ("middle_grad", middle_grad_h, middle_grad),
             ("w_out", w_out_h, w_out),
@@ -791,21 +852,17 @@
             loads[name].wait()
 
     greet([here.mate()] + plane_peers(here) + [here.to(dx=d) for d in (1, 2, 3)])
-    lines = Lines(send, recv)
-    copy = lines.copy
     n, width = middle_grad.shape
     head_dim = 2 * cosine.shape[1]
     heads = queries.shape[1] // head_dim
     rows = width // 16
     at = heads * head_dim
-    sums = [
-        PlaneSum(here, lines, g, *rest[8 * k : 8 * k + 8])
-        for k, g in enumerate((g_down, chip_qkv, chip_out))
-    ]
-    o_in[x, yl] = half_in[...]
-    in_pair = copy(half_in, o_in.at[x, yl], here.pair())
+    ready("g_in")
+    sums[3].resumed()
+    sums[3].middle()
     ready("g_down")
-    sums[0].first()
+    sums[0].resumed()
+    sums[0].middle()
     ready("attended", "middle_grad", "w_out", "context")
 
     att, dy = attended[...], middle_grad[...]
@@ -820,13 +877,6 @@
     grad_out = dot(context[...], attended_grad, TN)
     g_out[...] = grad_out.astype(BF16).reshape(g_out.shape)
     give_out = copy(g_out.at[:, :, 1 - c], cross_out, here.mate())
-    in_pair.wait_recv()
-    right, left = here.to(dx=1), here.to(dx=3)
-    own = [o_in.at[x, m] for m in (0, 1)]
-    early = [copy(own[0], own[0], right), copy(own[1], own[1], left)]
-    late = [copy(own[1], own[1], right), copy(own[0], own[0], left)]
-    sums[0].middle()
-
     ready("probs", "kv", "queries", "qkv_pre")
     keys = kv[:, :, :head_dim].reshape(2 * n, head_dim)
     values = kv[:, :, head_dim:].reshape(2 * n, head_dim)
@@ -854,14 +904,28 @@
         )
         attn_side[:, cols] = side
         d_query = d_query + d_scale
+        if h == 1:
+            sums[3].second()
+        if h == 2:
+            sums[0].second()
     kv_give[...] = kv_part[1 - yl].astype(BF16)
     kv_sent = copy(kv_give, kv_land, here.pair())
+    ready("w_qkv", "normed", "tokens")
+    normed_grad = dot(attn_side[:, :at], w_qkv[:, :at], NT)
+    grad_query = dot(normed[...], attn_side[:, :at], TN)
+    for path in (0, 1):
+        swap[path] = sums[3].result(path).astype(BF16)
+    across = copy(swap.at[1 - c], o_in.at[x, yl, c], here.mate())
+    o_in[x, yl, c] = swap[c]
+    for path in (0, 1):
+        o_down[x, yl, path] = sums[0].result(path).astype(BF16)
+    down_pair = copy(o_down.at[x, yl], o_down.at[x, yl], here.pair())
     give_out.wait_recv()
+    across.wait_recv()
+    in_pair = copy(o_in.at[x, yl], o_in.at[x, yl], here.pair())
     for z in range(4):
         for yh in range(2):
             chip_out[z, yh] = (g_out[z, yh, c].astype(F32) + cross_out[z, yh].astype(F32)).astype(BF16)
-    sums[2].first()
-    sums[0].second()
     kv_sent.wait_recv()
     kv_grad = (kv_part[yl] + kv_land[...].astype(F32)).astype(BF16)
     side, d_key = head_backward(
@@ -871,48 +935,54 @@
     attn_side[:, at + head_dim :] = kv_grad[:, head_dim:]
     d_gains[0:1, width : width + head_dim] = d_query
     d_gains[1:2, width : width + head_dim] = d_key
-
-    ready("w_qkv", "normed", "tokens")
-    normed_grad = dot(attn_side[...], w_qkv[...], NT)
+    down_pair.wait_recv()
+    down_x = [copy(o_down.at[x], o_down.at[x], here.to(dx=d)) for d in (1, 3, 2)]
+
+    normed_grad = normed_grad + dot(attn_side[:, at:], w_qkv[:, at:], NT)
     tok = tokens[...].astype(F32)
     r, grad = norm_back(tok, normed_grad * (1.0 + gains[0:1, :width]), width)
     grad_tokens[...] = (middle_grad[...] + grad).astype(BF16)
     d_gains[0:1, :width] = jnp.sum(normed_grad * tok * r, axis=0, keepdims=True)
-    grad_qkv = dot(normed[...], attn_side[...], TN)
+    grad_kv = dot(normed[...], attn_side[:, at:], TN)
+    wide = g_qkv.shape[-1]
     for p in range(4):
-        cols = slice(p * g_qkv.shape[-1], (p + 1) * g_qkv.shape[-1])
-        tail = d_gains[:, cols].astype(BF16)
+        cols = slice(p * wide, (p + 1) * wide)
         for f in range(16):
             spot = (f // 4, (f // 2) % 2, f % 2, p // 2, p % 2)
-            block = jnp.concatenate(
-                [grad_qkv[rows * f : rows * f + rows, cols], d_gains[:, cols]], axis=0
-            )
-            g_qkv[spot] = block.astype(BF16)
+            span = slice(rows * f, rows * f + rows)
+            parts = []
+            if p * wide < at:
+                parts.append(grad_query[span, p * wide : min((p + 1) * wide, at)])
+            if (p + 1) * wide > at:
+                parts.append(grad_kv[span, max(p * wide - at, 0) : (p + 1) * wide - at])
+            block = parts[0] if len(parts) == 1 else jnp.concatenate(parts, axis=1)
+            g_qkv[spot] = jnp.concatenate([block, d_gains[:, cols]], axis=0).astype(BF16)
     give_qkv = copy(g_qkv.at[:, :, 1 - c], cross_qkv, here.mate())
-
-    for made, at_x, m, to in ((early[0], left[0], 0, right), (early[1], right[0], 1, left)):
-        made.wait_recv()
-        late.append(copy(o_in.at[at_x, m], o_in.at[at_x, m], to))
+    sums[2].first()
+    in_pair.wait_recv()
+    right, left = here.to(dx=1), here.to(dx=3)
+    own = [o_in.at[x, m] for m in (0, 1)]
+    early = [copy(own[0], own[0], right), copy(own[1], own[1], left)]
+    late = [copy(own[1], own[1], right), copy(own[0], own[0], left)]
     give_qkv.wait_recv()
     for z in range(4):
         for yh in range(2):
             chip_qkv[z, yh] = (g_qkv[z, yh, c].astype(F32) + cross_qkv[z, yh].astype(F32)).astype(BF16)
     sums[1].first()
-    for path in (0, 1):
-        o_down[x, yl, path] = sums[0].result(path).astype(BF16)
-    down_pair = copy(o_down.at[x, yl], o_down.at[x, yl], here.pair())
     sums[2].middle()
     sums[1].middle()
-    down_pair.wait_recv()
-    down_x = [copy(o_down.at[x], o_down.at[x], here.to(dx=d)) for d in (1, 3, 2)]
+    for made, at_x, m, to in ((early[0], left[0], 0, right), (early[1], right[0], 1, left)):
+        made.wait_recv()
+        late.append(copy(o_in.at[at_x, m], o_in.at[at_x, m], to))
     sums[2].second()
+    sums[1].second()
     for path in (0, 1):
         half_out[path] = sums[2].result(path).astype(BF16)
-    by_x = [copy(half_out, land_out.at[d - 1], here.to(dx=d)) for d in (1, 3, 2)]
-    sums[1].second()
-    for path in (0, 1):
         half_qkv[path] = sums[1].result(path).astype(BF16)
-    by_x += [copy(half_qkv, land_qkv.at[d - 1], here.to(dx=d)) for d in (1, 3, 2)]
+    by_x = []
+    for d in (1, 3, 2):
+        by_x.append(copy(half_qkv, land_qkv.at[d - 1], here.to(dx=d)))
+        by_x.append(copy(half_out, land_out.at[d - 1], here.to(dx=d)))
     for made in by_x:
         made.wait_recv()
     for half, land, out in ((half_qkv, land_qkv, o_qkv), (half_out, land_out, o_out)):
@@ -930,26 +1000,26 @@
 def retreat_block(*args):
     (
         middle_grad, attended, context, probs, kv, queries, qkv_pre, normed, tokens, w_qkv, w_out,
-        g_down, cosine, _, _, _, _, half_in,
+        g_down, g_in, *_, cosine, _, _, _, _,
     ) = args
     vmem, hbm = pl.BlockSpec(memory_space=pltpu.VMEM), pl.BlockSpec(memory_space=pl.ANY)
     shape = jax.ShapeDtypeStruct
     n, width = middle_grad.shape
     out_width, head_dim = queries.shape[1], 2 * cosine.shape[1]
     cols = qkv_pre.shape[1]
-    p_in, p_down, p_out = half_in.shape[1:], g_down.shape[4:], w_out.shape[5:]
+    p_in, p_down, p_out = g_in.shape[4:], g_down.shape[4:], w_out.shape[5:]
     p_qkv = (width // 16 + 8, cols // 4)
     vm = lambda *s: pltpu.VMEM(s, BF16)
     scratch = [pltpu.VMEM(a.shape, a.dtype) for a in args[:11]]
-    scratch += [vm(*g_down.shape)]
+    scratch += [vm(*g_down.shape), vm(*g_in.shape)]
     scratch += [vm(n, out_width), vm(n, cols), pltpu.VMEM((2, n, 2 * head_dim), F32)]
     scratch += [vm(n, 2 * head_dim)] * 2
     scratch += [vm(4, 2, 2, 2, 2, *p_qkv), vm(4, 2, 2, 2, 2, *p_out), pltpu.VMEM((8, cols), F32)]
     scratch += [vm(4, 2, 2, 2, *p_qkv), vm(4, 2, 2, 2, *p_out)] * 2
-    scratch += [vm(2, *p_qkv), vm(2, *p_out), vm(3, 2, *p_qkv), vm(3, 2, *p_out)]
-    for piece in (p_down, p_qkv, p_out):
+    scratch += [vm(2, *p_in), vm(2, *p_qkv), vm(2, *p_out), vm(3, 2, *p_qkv), vm(3, 2, *p_out)]
+    for piece in (p_down, p_qkv, p_out, p_in):
         scratch += PlaneSum.scratch(piece)
-    scratch += [pltpu.SemaphoreType.DMA((76,))] * 2 + [pltpu.SemaphoreType.DMA((12,))]
+    scratch += [pltpu.SemaphoreType.DMA((79,))] * 2 + [pltpu.SemaphoreType.DMA((25,))]
     low = lambda *s: shape(s, BF16)
     return pl.pallas_call(
         retreat_kernel,
@@ -960,7 +1030,7 @@
             low(2, 2, *p_qkv),
             low(2, 2, *p_out),
         ),
-        in_specs=[hbm] * 12 + [vmem] * 6,
+        in_specs=[hbm] * 21 + [vmem] * 5,
         out_specs=(vmem,) * 5,
         scratch_shapes=scratch,
         compiler_params=pltpu.CompilerParams(
@@ -1093,12 +1163,12 @@
     ) = attend_block(
         tokens, cosine, sine, tail, w_query, w_key, w_value, own_out, w_gate, w_up, w_down
     )
-    layer_out, middle_grad, d_gain_in, d_gain_out, half_in, g_down = mlp_block(
+    layer_out, middle_grad, d_gain_in, d_gain_out, *begun, g_in, g_down = mlp_block(
         xs, middle, cotangent, gains, gate_full, up_full, down_full
     )
     grad_tokens, o_in, o_down, o_qkv, o_out = retreat_block(
         middle_grad, attended, context, probs, kv, queries, qkv_pre, normed, tokens, w_qkv,
-        w_out_full, g_down, cosine, sine, gains, d_gain_in, d_gain_out, half_in,
+        w_out_full, g_down, g_in, *begun, cosine, sine, gains, d_gain_in, d_gain_out,
     )
     like = lambda a, kind: jax.ShapeDtypeStruct(a.shape, kind)
     weights = (w_query, w_key, w_value, w_out, w_gate, w_up, w_down)

time: 286 us -> 276 us (0.965)
  Pallas kernels: 275 us -> 266 us
    pallas_call x1, Pallas kernels: 116 us -> 108 us  [mlp_block(): pl.pallas_call(mlp_kernel, out_shape=(shape((n, width), BF16), shape((n,...]
    pallas_call x1, Pallas kernels: 78.8 us -> 73.2 us  [attend_block(): pl.pallas_call(attend_kernel, out_shape=held + (shape((8, cols), F32),),...]
    pallas_call x1, Pallas kernels: 74.7 us -> 79 us  [retreat_block(): pl.pallas_call(retreat_kernel, out_shape=(low(n, width), low(4, 2, 2, *p_...]
where the time goes in v5:
time: 276 us; the launch traced here: 271 us
  Pallas kernels  266 us (96%)
  other arithmetic  3.45 us (1%)
    pallas_call x1, Pallas kernels, mlp_block(): pl.pallas_call(mlp_kernel, out_shape=(shape((n, width), BF16), shape((n,...  108 us
    pallas_call x1, Pallas kernels, retreat_block(): pl.pallas_call(retreat_kernel, out_shape=(low(n, width), low(4, 2, 2, *p_...  79 us
    pallas_call x1, Pallas kernels, attend_block(): pl.pallas_call(attend_kernel, out_shape=held + (shape((8, cols), F32),),...  73.2 us
    pallas_call x1, Pallas kernels, finish_block(): pl.pallas_call(finish_kernel, out_shape=out_shape, in_specs=[hbm] * 6, ou...  5.7 us

profile of v5, /device:TPU:0, one launch (start us, length us, event | category | flops | bytes accessed | tf_op | source)
XLA Modules:
  0.0 271.5 jit_solution(16232746146391449573)
XLA Ops:
  0.7 0.7 broadcast_select_fusion.1
  1.4 0.1 select_n.89
  1.5 0.1 select_n.91
  1.6 0.8 broadcast_select_fusion.5
  2.4 0.1 select_n.81
  2.5 0.1 select_n.83
  2.6 0.1 select_n.85
  2.7 0.1 select_n.87
  2.9 0.6 pad_maximum_fusion.tail
  3.5 1.2 multiply_sine_fusion
  4.7 73.2 %attend.1 = (bf16[4,512,1152]{2,1,0:T(8,128)(2,1)}, bf16[1152,896]{1,0:T(8,128)(2,1)}, bf16[1152,896]{1,0:T(8,128)(2,1)}, bf16[896,1152]{1,0:T(8,128)(2,1)}, bf1...) custom-call(bf16[256,1152]{1,0:T(8,128)(2,1)} %tokens_h.1, ...), custom_call_target="tpu_custom_call" | custom-call | tf_op jit(solution)/shard_map/attend/pallas_call | solution.py:659
  78.0 108.3 %mlp_block.1 = (bf16[256,1152]{1,0:T(8,128)(2,1)}, f32[256,1152]{1,0:T(8,128)}, f32[1,1152]{1,0:T(1,128)}, f32[1,1152]{1,0:T(1,128)}, bf16[2,2,72,896]{3,2,1,0:T...) custom-call(bf16[4,512,1152]{2,1,0:T(8,128)(2,1)} %get-tuple-element, ...), custom_call_target="tpu_custom_call" | custom-call | tf_op jit(solution)/shard_map/mlp_block/pallas_call | solution.py:356
  186.3 79.0 %retreat.1 = (bf16[256,1152]{1,0:T(8,128)(2,1)}, bf16[4,2,2,72,896]{4,3,2,1,0:T(8,128)(2,1)}, bf16[4,2,2,32,1152]{4,3,2,1,0:T(8,128)(2,1)}, bf16[2,2,80,384]{3,2,1,0:T(8,128)(2,1)}, bf16[2,2,16,1152]{3,2,1,0:T(8,128)(2,1)}) custom-call(f32[256,1152]{1,0:T(8,128)} %get-tuple-element.55.middle_grad_h, f32[256,1152]{1,0:T(8,128)} %get-tuple-element.56.attended_h, ...), custom_call_target="tpu_custom_call" | custom-call | tf_op jit(solution)/shard_map/retreat/pallas_call | solution.py:1024
  265.3 5.7 %finish.1 = (bf16[256,1152]{1,0:T(8,128)(2,1)}, bf16[256,1152]{1,0:T(8,128)(2,1)}, f32[72,1024]{1,0:T(8,128)}, f32[72,256]{1,0:T(8,128)}, f32[72,256]{1,0:T(8,12...) custom-call(bf16[4,2,2,72,896]{4,3,2,1,0:T(8,128)(2,1)} %get-tuple-e, ...), custom_call_target="tpu_custom_call" | custom-call | tf_op jit(solution)/shard_map/finish/pallas_call | solution.py:1106
  (5 shorter events, 0.1 us)

commit v6 on v5

--- a/solution.py
+++ b/solution.py
@@ -17,6 +17,7 @@
 MIB = 2**20
 PART = 112
 CORE_UNITS = 8 * PART
+UNITS_OF_SHARD = 432
 
 
 def dot(a, b, dims=NN):
@@ -83,6 +84,11 @@
         self.send, self.recv, self.used, self.open = send, recv, 0, []
 
     def copy(self, src, dst, device):
+        made = self.plan(src, dst, device)
+        made.start()
+        return made
+
+    def plan(self, src, dst, device):
         k = self.used
         self.used += 1
         made = pltpu.make_async_remote_copy(
@@ -93,7 +99,6 @@
             device_id=device,
             device_id_type=MESH,
         )
-        made.start()
         self.open.append(made)
         return made
 
@@ -301,6 +306,13 @@
     backward(2)
 
     flat = lambda ref: ref[...].reshape(ref.shape[0] * ref.shape[1], ref.shape[2])
+    send_in = in_sum.begin_by_owner(half_a, half_b, near_a, near_b)
+    for mat, side in ((0, slope), (1, act)):
+        grad_side = dot(flat(xs), flat(side), TN)
+        for f in range(16):
+            d_in[f // 4, (f // 2) % 2, mat, f % 2] = grad_side[72 * f : 72 * f + 72].astype(BF16)
+        send_in(mat)
+    moves.store(d_in, d_in_h)
     grad_down = dot(flat(hidden), flat(gs), TN)
     for k in range(8):
         for p in range(4):
@@ -313,14 +325,6 @@
         [down_near_b.at[0], down_near_b.at[1]],
     )
     moves.store(d_down, d_down_h)
-    for mat, side in ((0, slope), (1, act)):
-        grad_side = dot(flat(xs), flat(side), TN)
-        for f in range(16):
-            d_in[f // 4, (f // 2) % 2, mat, f % 2] = grad_side[72 * f : 72 * f + 72].astype(BF16)
-    in_sum.begin(
-        half_a, half_b, [near_a.at[0], near_a.at[1]], [near_b.at[0], near_b.at[1]]
-    )
-    moves.store(d_in, d_in_h)
 
     update = sums.total()
     base = middle[...]
@@ -350,7 +354,7 @@
         + [pltpu.VMEM((4, n, width), BF16), pltpu.VMEM((3, n, width), BF16)]
         + [pltpu.VMEM((n, width), F32), pltpu.VMEM((n, width), BF16)]
         + [pltpu.VMEM(d_down.shape, BF16)]
-        + [pltpu.SemaphoreType.DMA((40,))] * 2
+        + [pltpu.SemaphoreType.DMA((44,))] * 2
         + [pltpu.SemaphoreType.DMA((11,))]
     )
     return pl.pallas_call(
@@ -726,6 +730,39 @@
         self.a = [copy(g.at[a1[1]], near_a[0], up_y), copy(g.at[a3[0]], near_a[1], down_y)]
         self.b = [copy(g.at[b1[1]], near_b[0], up_z), copy(g.at[b3[0]], near_b[1], down_z)]
 
+    def begin_by_owner(self, half_a, half_b, near_a, near_b):
+        here, g, plan = self.here, self.grads, self.lines.plan
+        up_y, down_y, up_z, down_z = here.to(dy=1), here.to(dy=3), here.to(dz=1), here.to(dz=3)
+        (a, b), (a1, b1), (a3, b3) = self.spots(2), self.spots(1), self.spots(3)
+        same = [plan(g.at[a[0]], half_a.at[0], up_y), plan(g.at[a[1]], half_a.at[1], down_y)]
+        other = [plan(g.at[a1[1]], near_a.at[0], up_y), plan(g.at[a3[0]], near_a.at[1], down_y)]
+        by_z = [
+            [
+                plan(g.at[b[0][0], 0, k, 1], half_b.at[0, k], up_z),
+                plan(g.at[b[0][0], 1, k, 1], half_b.at[1, k], down_z),
+                plan(g.at[b1[0][0], 1, k, 1], near_b.at[0, k], up_z),
+                plan(g.at[b3[0][0], 0, k, 1], near_b.at[1, k], down_z),
+            ]
+            for k in range(2)
+        ]
+        self.half, self.a, self.b = same, other, by_z[0] + by_z[1]
+
+        def send(k):
+            @pl.when(here.yl == k)
+            def _():
+                for made in same:
+                    made.start()
+
+            @pl.when(here.yl != k)
+            def _():
+                for made in other:
+                    made.start()
+
+            for made in by_z[k]:
+                made.start()
+
+        return send
+
     def begun(self):
         for made in self.half + self.a + self.b:
             made.wait_recv()
@@ -810,8 +847,8 @@
     w_qkv_h, w_out_h, g_down_h, g_in_h, half_a, half_b, near_a, near_b,
     down_half_a, down_half_b, down_near_a, down_near_b,
     cosine, sine, gains, d_gain_in, d_gain_out,
-    grad_tokens, o_in, o_down, o_qkv, o_out,
-    middle_grad, attended, context, probs, kv, queries, qkv_pre, normed, tokens, w_qkv, w_out,
+    grad_tokens, laid_h, o_down, o_qkv, o_out,
+    laid, row, o_in, middle_grad, attended, context, probs, kv, queries, qkv_pre, normed, tokens, w_qkv, w_out,
     g_down, g_in,
     context_grad, attn_side, kv_part, kv_give, kv_land, g_qkv, g_out, d_gains,
     chip_qkv, chip_out, cross_qkv, cross_out, swap, half_qkv, half_out, land_qkv, land_out, *rest,
@@ -983,6 +1020,17 @@
     for d in (1, 3, 2):
         by_x.append(copy(half_qkv, land_qkv.at[d - 1], here.to(dx=d)))
         by_x.append(copy(half_out, land_out.at[d - 1], here.to(dx=d)))
+    for made in late:
+        made.wait_recv()
+    block = row.shape[1] // 16
+    for m in range(2):
+        for k in range(4):
+            count = min(PART, block - PART * k)
+            for f in range(16):
+                piece = o_in[k, m, f % 2].astype(F32)[:, PART * (f // 2) : PART * (f // 2) + count]
+                row[:, block * f + PART * k : block * f + PART * k + count] = piece
+        laid[m] = row[...].astype(BF16)
+        moves.store(laid.at[m], laid_h.at[m])
     for made in by_x:
         made.wait_recv()
     for half, land, out in ((half_qkv, land_qkv, o_qkv), (half_out, land_out, o_out)):
@@ -992,9 +1040,10 @@
                 total = total + land[j, path].astype(F32)
             out[yl, path] = total.astype(BF16)
     ends = [copy(o.at[yl], o.at[yl], here.pair()) for o in (o_qkv, o_out)]
-    for made in down_x + late + ends:
+    for made in down_x + ends:
         made.wait_recv()
     lines.drain()
+    moves.drain()
 
 
 def retreat_block(*args):
@@ -1010,7 +1059,9 @@
     p_in, p_down, p_out = g_in.shape[4:], g_down.shape[4:], w_out.shape[5:]
     p_qkv = (width // 16 + 8, cols // 4)
     vm = lambda *s: pltpu.VMEM(s, BF16)
-    scratch = [pltpu.VMEM(a.shape, a.dtype) for a in args[:11]]
+    units = 16 * UNITS_OF_SHARD
+    scratch = [vm(2, width // 16, units), pltpu.VMEM((width // 16, units), F32), vm(4, 2, 2, *p_in)]
+    scratch += [pltpu.VMEM(a.shape, a.dtype) for a in args[:11]]
     scratch += [vm(*g_down.shape), vm(*g_in.shape)]
     scratch += [vm(n, out_width), vm(n, cols), pltpu.VMEM((2, n, 2 * head_dim), F32)]
     scratch += [vm(n, 2 * head_dim)] * 2
@@ -1019,19 +1070,19 @@
     scratch += [vm(2, *p_in), vm(2, *p_qkv), vm(2, *p_out), vm(3, 2, *p_qkv), vm(3, 2, *p_out)]
     for piece in (p_down, p_qkv, p_out, p_in):
         scratch += PlaneSum.scratch(piece)
-    scratch += [pltpu.SemaphoreType.DMA((79,))] * 2 + [pltpu.SemaphoreType.DMA((25,))]
+    scratch += [pltpu.SemaphoreType.DMA((79,))] * 2 + [pltpu.SemaphoreType.DMA((27,))]
     low = lambda *s: shape(s, BF16)
     return pl.pallas_call(
         retreat_kernel,
         out_shape=(
             low(n, width),
-            low(4, 2, 2, *p_in),
+            low(2, width // 16, units),
             low(4, 2, 2, *p_down),
             low(2, 2, *p_qkv),
             low(2, 2, *p_out),
         ),
         in_specs=[hbm] * 21 + [vmem] * 5,
-        out_specs=(vmem,) * 5,
+        out_specs=(vmem, hbm) + (vmem,) * 3,
         scratch_shapes=scratch,
         compiler_params=pltpu.CompilerParams(
             collective_id=2, has_side_effects=True, vmem_limit_bytes=63 * MIB
@@ -1048,7 +1099,7 @@
     out_gains = rest[:6]
     o_in, o_down, o_qkv, o_out, out_gate, out_up, out_down, shown, taken, moved = rest[6:]
     moves = Moves(moved)
-    load_in = [moves.start(o_in_h.at[:, m], o_in.at[:, m]) for m in (0, 1)]
+    load_in = [moves.start(o_in_h.at[m], o_in.at[m]) for m in (0, 1)]
     load_tokens = [moves.start(shown_h, shown), moves.start(taken_h, taken)]
     load_down = moves.start(o_down_h, o_down)
     load_rest = [moves.start(o_qkv_h, o_qkv), moves.start(o_out_h, o_out)]
@@ -1058,11 +1109,7 @@
     at, head_dim = out_query.shape[1], out_key.shape[1]
     for m, out, out_h in ((0, out_gate, out_gate_h), (1, out_up, out_up_h)):
         load_in[m].wait()
-        for k in range(4):
-            count = min(PART, block - PART * k)
-            for f in range(16):
-                piece = o_in[k, m, f % 2].astype(F32)[:, PART * (f // 2) : PART * (f // 2) + count]
-                out[:, block * f + PART * k : block * f + PART * k + count] = piece
+        out[...] = o_in[m].astype(F32)
         moves.store(out, out_h)
     for made, held, out_h in zip(load_tokens, (shown, taken), (layer_out_h, grad_tokens_h)):
         made.wait()

time: 276 us -> 271 us (0.982)
  Pallas kernels: 266 us -> 261 us
    pallas_call x1, Pallas kernels: 108 us -> 104 us  [mlp_block(): pl.pallas_call(mlp_kernel, out_shape=(shape((n, width), BF16), shape((n,...]
where the time goes in v6:
time: 271 us; the launch traced here: 266 us
  Pallas kernels  261 us (96%)
  other arithmetic  3.45 us (1%)
    pallas_call x1, Pallas kernels, mlp_block(): pl.pallas_call(mlp_kernel, out_shape=(shape((n, width), BF16), shape((n,...  104 us
    pallas_call x1, Pallas kernels, retreat_block(): pl.pallas_call(retreat_kernel, out_shape=(low(n, width), low(2, width //...  78.4 us
    pallas_call x1, Pallas kernels, attend_block(): pl.pallas_call(attend_kernel, out_shape=held + (shape((8, cols), F32),),...  73.2 us

profile of v6, /device:TPU:0, one launch (start us, length us, event | category | flops | bytes accessed | tf_op | source)
XLA Modules:
  0.0 266.1 jit_solution(3530736386034006036)
XLA Ops:
  0.7 0.7 broadcast_select_fusion.1
  1.4 0.1 select_n.89
  1.5 0.1 select_n.91
  1.6 0.8 broadcast_select_fusion.5
  2.4 0.1 select_n.81
  2.5 0.1 select_n.83
  2.6 0.1 select_n.85
  2.7 0.1 select_n.87
  2.9 0.6 pad_maximum_fusion.tail
  3.5 1.2 multiply_sine_fusion
  4.7 73.2 %attend.1 = (bf16[4,512,1152]{2,1,0:T(8,128)(2,1)}, bf16[1152,896]{1,0:T(8,128)(2,1)}, bf16[1152,896]{1,0:T(8,128)(2,1)}, bf16[896,1152]{1,0:T(8,128)(2,1)}, bf1...) custom-call(bf16[256,1152]{1,0:T(8,128)(2,1)} %tokens_h.1, ...), custom_call_target="tpu_custom_call" | custom-call | tf_op jit(solution)/shard_map/attend/pallas_call | solution.py:663
  78.0 104.0 %mlp_block.1 = (bf16[256,1152]{1,0:T(8,128)(2,1)}, f32[256,1152]{1,0:T(8,128)}, f32[1,1152]{1,0:T(1,128)}, f32[1,1152]{1,0:T(1,128)}, bf16[2,2,72,896]{3,2,1,0:T...) custom-call(bf16[4,512,1152]{2,1,0:T(8,128)(2,1)} %get-tuple-element, ...), custom_call_target="tpu_custom_call" | custom-call | tf_op jit(solution)/shard_map/mlp_block/pallas_call | solution.py:360
  182.0 78.4 %retreat.1 = (bf16[256,1152]{1,0:T(8,128)(2,1)}, bf16[2,72,6912]{2,1,0:T(8,128)(2,1)}, bf16[4,2,2,32,1152]{4,3,2,1,0:T(8,128)(2,1)}, bf16[2,2,80,384]{3,2,1,0:T(8,128)(2,1)}, bf16[2,2,16,1152]{3,2,1,0:T(8,128)(2,1)}) custom-call(f32[256,1152]{1,0:T(8,128)} %get-tuple-element.55.middle_grad_h, f32[256,1152]{1,0:T(8,128)} %get-tuple-element.56.attended_h, ...), custom_call_target="tpu_custom_call" | custom-call | tf_op jit(solution)/shard_map/retreat/pallas_call | solution.py:1075
  260.4 5.3 %finish.1 = (bf16[256,1152]{1,0:T(8,128)(2,1)}, bf16[256,1152]{1,0:T(8,128)(2,1)}, f32[72,1024]{1,0:T(8,128)}, f32[72,256]{1,0:T(8,128)}, f32[72,256]{1,0:T(8,12...) custom-call(bf16[2,72,6912]{2,1,0:T(8,128)(2,1)} %get-tuple-element., ...), custom_call_target="tpu_custom_call" | custom-call | tf_op jit(solution)/shard_map/finish/pallas_call | solution.py:1153
  (5 shorter events, 0.1 us)

commit v7 on v6

--- a/solution.py
+++ b/solution.py
@@ -275,13 +275,13 @@
     cot_f = cot[...].astype(F32)
     u = cot_f * (1.0 + gain_out)
     factor, grad = norm_back(mixed, u, width)
-    layer_out[...] = (middle[...] + mixed * factor * (1.0 + gain_out)).astype(BF16)
-    d_gain_out[...] = jnp.sum(cot_f * mixed * factor, axis=0, keepdims=True)
     mixed_grad[...] = grad.astype(BF16)
 
     ring = RingGather(here, lines, mixed_grad, gs)
     sums = RingSum(here, lines, mine, landed_b, cross_b, stage_core, stage_ring)
     ring.start()
+    layer_out[...] = (middle[...] + mixed * factor * (1.0 + gain_out)).astype(BF16)
+    d_gain_out[...] = jnp.sum(cot_f * mixed * factor, axis=0, keepdims=True)
 
     def backward(r):
         hidden_grad = dot(gs[r], w_down[...], NT)
@@ -463,7 +463,7 @@
 
 
 def attend_kernel(
-    tokens, cosine, sine, tail, w_query, w_key, w_value, own_out, w_gate, w_up, w_down,
+    tokens, cosine, sine, tail, w_query, w_key, w_value, own_out, w_gate_h, w_up_h, w_down_h,
     *refs,
 ):
     kept = refs[:14]
@@ -474,8 +474,11 @@
         attended, qkv_pre, middle,
     ) = held
     mlp_in, own_qkv, own_in, own_down, full_qkv, full_in, full_down, chip_in = refs[29:37]
-    send, recv, local, moved = refs[37:]
+    w_gate, w_up, w_down, send, recv, local, moved = refs[37:]
     moves = Moves(moved)
+    load_gate, load_up, load_down = [
+        moves.start(a, b) for a, b in ((w_gate_h, w_gate), (w_up_h, w_up), (w_down_h, w_down))
+    ]
     place = {id(a): b for a, b in zip(held, kept)}
     keep = lambda ref: moves.store(ref, place[id(ref)])
     here = Place()
@@ -514,7 +517,8 @@
     gather[1].first()
     lane = lax.broadcasted_iota(jnp.int32, (rows, PART), 1)
     inside = lane < block - x_at * PART
-    for mat, weight in ((0, w_gate), (1, w_up)):
+    for mat, weight, load in ((0, w_gate, load_gate), (1, w_up, load_up)):
+        load.wait()
         turned = pltpu.roll(weight[...].astype(F32), lax.rem(units - PART * x_at, units), 1)
         for core in range(2):
             parts = [
@@ -525,6 +529,7 @@
     across = lines.copy(own_in.at[1 - c], chip_in.at[:, c], here.mate())
     chip_in[:, c] = own_in[c]
     gather[0].second()
+    load_down.wait()
     for p in range(3):
         start = pl.multiple_of(PART * x_at + 32 * p, 16)
         own_down[p // 2, p % 2] = w_down[pl.ds(start, 32)]
@@ -663,7 +668,7 @@
     return pl.pallas_call(
         attend_kernel,
         out_shape=held + (shape((8, cols), F32),),
-        in_specs=[vmem] * 11,
+        in_specs=[vmem] * 8 + [pl.BlockSpec(memory_space=pl.ANY)] * 3,
         out_specs=(pl.BlockSpec(memory_space=pl.ANY),) * 14 + (vmem,),
         scratch_shapes=[pltpu.VMEM(a.shape, a.dtype) for a in held]
         + [
@@ -675,10 +680,13 @@
             vm(4, 2, 2, 2, *p_in),
             vm(4, 2, 2, 2, *p_down),
             vm(2, 2, *p_in),
+            vm(*w_gate.shape),
+            vm(*w_up.shape),
+            vm(*w_down.shape),
             pltpu.SemaphoreType.DMA((87,)),
             pltpu.SemaphoreType.DMA((87,)),
             pltpu.SemaphoreType.DMA((4,)),
-            pltpu.SemaphoreType.DMA((14,)),
+            pltpu.SemaphoreType.DMA((17,)),
         ],
         compiler_params=pltpu.CompilerParams(
             collective_id=0, has_side_effects=True, vmem_limit_bytes=62 * MIB

time: 271 us -> 270 us (level)
  no operation moved by 1% of the time
where the time goes in v7:
time: 270 us; the launch traced here: 265 us
  Pallas kernels  260 us (96%)
  other arithmetic  3.45 us (1%)
    pallas_call x1, Pallas kernels, mlp_block(): pl.pallas_call(mlp_kernel, out_shape=(shape((n, width), BF16), shape((n,...  104 us
    pallas_call x1, Pallas kernels, retreat_block(): pl.pallas_call(retreat_kernel, out_shape=(low(n, width), low(2, width //...  78.4 us
    pallas_call x1, Pallas kernels, attend_block(): pl.pallas_call(attend_kernel, out_shape=held + (shape((8, cols), F32),),...  72.3 us

profile of v7, /device:TPU:0, one launch (start us, length us, event | category | flops | bytes accessed | tf_op | source)
XLA Modules:
  0.0 265.1 jit_solution(12527884285155418495)
XLA Ops:
  0.7 0.7 broadcast_select_fusion.1
  1.4 0.1 select_n.89
  1.5 0.1 select_n.91
  1.6 0.8 broadcast_select_fusion.5
  2.4 0.1 select_n.81
  2.5 0.1 select_n.83
  2.6 0.1 select_n.85
  2.7 0.1 select_n.87
  2.9 0.6 pad_maximum_fusion.tail
  3.5 1.2 multiply_sine_fusion
  4.7 72.3 %attend.1 = (bf16[4,512,1152]{2,1,0:T(8,128)(2,1)}, bf16[1152,896]{1,0:T(8,128)(2,1)}, bf16[1152,896]{1,0:T(8,128)(2,1)}, bf16[896,1152]{1,0:T(8,128)(2,1)}, bf1...) custom-call(bf16[256,1152]{1,0:T(8,128)(2,1)} %tokens_h.1, ...), custom_call_target="tpu_custom_call" | custom-call | tf_op jit(solution)/shard_map/attend/pallas_call | solution.py:668
  77.0 103.9 %mlp_block.1 = (bf16[256,1152]{1,0:T(8,128)(2,1)}, f32[256,1152]{1,0:T(8,128)}, f32[1,1152]{1,0:T(1,128)}, f32[1,1152]{1,0:T(1,128)}, bf16[2,2,72,896]{3,2,1,0:T...) custom-call(bf16[4,512,1152]{2,1,0:T(8,128)(2,1)} %get-tuple-element, ...), custom_call_target="tpu_custom_call" | custom-call | tf_op jit(solution)/shard_map/mlp_block/pallas_call | solution.py:360
  180.9 78.4 %retreat.1 = (bf16[256,1152]{1,0:T(8,128)(2,1)}, bf16[2,72,6912]{2,1,0:T(8,128)(2,1)}, bf16[4,2,2,32,1152]{4,3,2,1,0:T(8,128)(2,1)}, bf16[2,2,80,384]{3,2,1,0:T(8,128)(2,1)}, bf16[2,2,16,1152]{3,2,1,0:T(8,128)(2,1)}) custom-call(f32[256,1152]{1,0:T(8,128)} %get-tuple-element.55.middle_grad_h, f32[256,1152]{1,0:T(8,128)} %get-tuple-element.56.attended_h, ...), custom_call_target="tpu_custom_call" | custom-call | tf_op jit(solution)/shard_map/retreat/pallas_call | solution.py:1083
  259.3 5.3 %finish.1 = (bf16[256,1152]{1,0:T(8,128)(2,1)}, bf16[256,1152]{1,0:T(8,128)(2,1)}, f32[72,1024]{1,0:T(8,128)}, f32[72,256]{1,0:T(8,128)}, f32[72,256]{1,0:T(8,12...) custom-call(bf16[2,72,6912]{2,1,0:T(8,128)(2,1)} %get-tuple-element., ...), custom_call_target="tpu_custom_call" | custom-call | tf_op jit(solution)/shard_map/finish/pallas_call | solution.py:1161
  (5 shorter events, 0.1 us)
